TPU v7x, 128 devices: a whole 4x4x4 slice. The times are simulated.
128 devices in a mesh: gx: 16 (over z, x_hi, core), gy: 4 (over y), gz: 2 (over x_lo).
Axes of the slice: x: 4 (x_hi: 2, x_lo: 2; x = x_hi * 2 + x_lo), y: 4, z: 4, core: 2. Of those that a mesh axis runs over, the one named last changes fastest.
Arguments:
- electric: float32 [3, 160, 128, 512], P(None, 'gz', 'gx', 'gy'), may hold values from -6 to 6
- magnetic: float32 [3, 160, 128, 512], P(None, 'gz', 'gx', 'gy'), may hold values from -6 to 6
- material: int32 [160, 128, 512], P('gz', 'gx', 'gy'), may hold values from 0 to 4, as said below
- decay: float32 [5], replicated, may hold values from 0.5 to 1
- gain: float32 [5], replicated, may hold values from 0.15 to 0.45
- kernels: float32 [2, 24, 15, 15], replicated, may hold values from -0.0390625 to 0.0390625
Outputs:
- electric_out: float32 [3, 160, 128, 512], P(None, 'gz', 'gx', 'gy')
- image: float32 [128, 512], P(('gx', 'gz'), 'gy')
Inputs may be any that keep to these rules, and one draw needn't show every extreme that they name: `material`: 0 vacuum, 1 molybdenum, 2 silicon, 3 absorber, 4 capping.
All inputs are finite; a program needn't handle non-finite values.
Results may differ from a plain program's by a relative error of at most 0.00028.
Values sent between devices are 32-bit elements; how exact they have to be, the bound alone decides.
No kernel may reach another device: no remote copies, remote signals or barrier semaphores. Data moves between devices by JAX's collectives and lax.ppermute only.
A program may use at most 128 MiB of HBM per device.

v0:
```python
import functools

import jax
import jax.numpy as jnp
from jax import lax
from jax.experimental import pallas as pl
from jax.experimental.pallas import tpu as pltpu
from jax.sharding import PartitionSpec as P

STEPS = 6
W = STEPS
Y, Z, X = range(3)
NC = 7
SOURCE = ((0, 1), (0, 2), (0, 0), (1, 1), (1, 2), (1, 0))
ROWS = 8 + 2 * W
BASE = 4
HELD = BASE + ROWS + 2
CUT = 4
TILES = 7
ON = 5
LAG = 4
VMEM = 56 * 1024 * 1024
F32 = jnp.float32
HBM = pl.BlockSpec(memory_space=pl.ANY)
LOCAL = pl.BlockSpec(memory_space=pltpu.VMEM)


def around(value, axis, steps):
    count = lax.axis_size(axis)
    return lax.ppermute(value, axis, [(i, (i + steps) % count) for i in range(count)])


def copy_all(pairs, sems):
    copies = [pltpu.make_async_copy(a, b, sems.at[i]) for i, (a, b) in enumerate(pairs)]
    for copy in copies:
        copy.start()
    for copy in copies:
        copy.wait()


def params():
    return pltpu.CompilerParams(vmem_limit_bytes=VMEM)


def cost(us):
    return pl.CostEstimate(flops=0, bytes_accessed=int(us * 3e6), transcendentals=0)


def pack_kernel(ta, tb, el, mg, mat, *refs):
    if ta:
        own, up, down, strip, ext, matv, planes, strips, sems = refs
    else:
        strip_above, own, up, down, strip, ext, matv, planes, strips, sems = refs
    tiles = tb - ta
    rows = pl.ds(64 * ta, 64 * tiles)
    loads = [(mat.at[rows], matv)]
    for c, (which, comp) in enumerate(SOURCE):
        loads.append(((el, mg)[which].at[comp, rows], ext.at[c]))
    copy_all(loads, sems)

    lane = lax.broadcasted_iota(jnp.int32, (8, 128), 1)
    masks = [((lane - 16 * c + W + 128) % 128) < 2 * W for c in range(NC)]

    def row(r, _):
        for t in range(tiles):
            z = 8 * t
            total = None
            for c in range(NC):
                if c == 6:
                    v = matv[pl.ds(64 * t + r, 8, stride=8), :].astype(F32)
                    planes[48 + r, z : z + 8, :] = v
                else:
                    v = ext[c, pl.ds(64 * t + r, 8, stride=8), :]
                    if c >= 3:
                        v = v * 2.0
                    planes[24 * (c // 3) + 3 * r + c % 3, z : z + 8, :] = v
                turned = pltpu.roll(v, 16 * c, 1) if c else v
                total = jnp.where(masks[c], turned, total) if c else v
            strips[r, z : z + 8, :] = total
        return 0

    lax.fori_loop(0, 8, row, 0)
    pairs = [(planes, own)]
    pairs += [
        (planes.at[pl.ds(a, n)], up.at[pl.ds(b, n)])
        for a, b, n in ((6, 0, 18), (30, 18, 2), (33, 20, 15), (51, 35, 5))
    ]
    pairs += [
        (planes.at[pl.ds(a, n)], down.at[pl.ds(b, n)])
        for a, b, n in ((0, 0, 17), (24, 17, 15), (48, 32, 5))
    ]
    if ta:
        pairs.append((strips, strip))
    else:
        pairs.append((strips, strip.at[:, pl.ds(0, 8 * tiles)]))
        pairs.append((strip_above, strip.at[:, pl.ds(8 * tiles, 80 - 8 * tiles)]))
    copy_all(pairs, sems)


def pack(ta, tb, el, mg, mat, *strip_above):
    layers = 8 * (tb - ta)
    return pl.pallas_call(
        functools.partial(pack_kernel, ta, tb),
        out_shape=[
            jax.ShapeDtypeStruct((8 * NC, layers, 128), F32),
            jax.ShapeDtypeStruct((40, layers, 128), F32),
            jax.ShapeDtypeStruct((37, layers, 128), F32),
            jax.ShapeDtypeStruct((8, layers if ta else 80, 128), F32),
        ],
        in_specs=[HBM] * (3 + len(strip_above)),
        out_specs=[HBM] * 4,
        scratch_shapes=[
            pltpu.VMEM((6, 8 * layers, 128), F32),
            pltpu.VMEM((8 * layers, 128), jnp.int32),
            pltpu.VMEM((8 * NC, layers, 128), F32),
            pltpu.VMEM((8, layers, 128), F32),
            pltpu.SemaphoreType.DMA((10,)),
        ],
        compiler_params=params(),
        cost_estimate=cost(3),
        name="pack_upper" if ta else "pack_lower",
    )(el, mg, mat, *strip_above)


def edge_kernel(from_low, from_high, own_u, own_l, strips, edge, sems):
    gz = lax.axis_index("gz")
    lane = lax.broadcasted_iota(jnp.int32, (8, 80, 128), 2)
    strips[...] = jnp.where(lane % 16 < 8, from_high[...], from_low[...])

    @pl.when(gz == 0)
    def _():
        copy_all([(own_u.at[:, pl.ds(8 * (9 - CUT), 8)], edge.at[pl.ds(0, 56)])], sems)
        edge[56:64] = strips[:, 72:80, :]

    @pl.when(gz == 1)
    def _():
        copy_all([(own_l.at[:, pl.ds(0, 8)], edge.at[pl.ds(0, 56)])], sems)
        edge[56:64] = strips[:, 0:8, :]


def edges(from_low, from_high, own_u, own_l):
    return pl.pallas_call(
        edge_kernel,
        out_shape=[
            jax.ShapeDtypeStruct((8, 80, 128), F32),
            jax.ShapeDtypeStruct((64, 8, 128), F32),
        ],
        in_specs=[LOCAL, LOCAL, HBM, HBM],
        out_specs=[LOCAL, LOCAL],
        scratch_shapes=[pltpu.SemaphoreType.DMA((1,))],
        compiler_params=params(),
        cost_estimate=cost(1),
        name="edges",
    )(from_low, from_high, own_u, own_l)


def corner_kernel(strips, edge, up, down, sems):
    pairs = [
        (edge.at[pl.ds(a, n)], up.at[pl.ds(b, n)])
        for a, b, n in ((6, 0, 18), (30, 18, 2), (33, 20, 15), (51, 35, 5), (58, 100, 6))
    ]
    pairs += [
        (edge.at[pl.ds(a, n)], down.at[pl.ds(b, n)])
        for a, b, n in ((0, 0, 17), (24, 17, 15), (48, 32, 5), (56, 97, 6))
    ]
    pairs.append((strips.at[pl.ds(20, 60)], up.at[pl.ds(40, 60)]))
    pairs.append((strips.at[pl.ds(0, 60)], down.at[pl.ds(37, 60)]))
    copy_all(pairs, sems)


def corners(strips, edge):
    return pl.pallas_call(
        corner_kernel,
        out_shape=[
            jax.ShapeDtypeStruct((106, 8, 128), F32),
            jax.ShapeDtypeStruct((103, 8, 128), F32),
        ],
        in_specs=[HBM, HBM],
        out_specs=[HBM, HBM],
        scratch_shapes=[pltpu.SemaphoreType.DMA((11,))],
        compiler_params=params(),
        cost_estimate=cost(1),
        name="corners",
    )(strips, edge)


def steps_kernel(upper, decay, gain, strips, edge, low_c, high_c, *refs):
    gz = lax.axis_index("gz")
    if upper:
        own_u, low_u, high_u, out, plane, *scratch = refs
        sets = [((own_u, low_u, high_u), 8 * (10 - CUT), 0)]
        halo, counts = TILES - 1, gz == 0
        held = [(t, t + CUT) for t in range(TILES - 1)]
    else:
        own_u, low_u, high_u, own_l, low_l, high_l, _, out, *scratch = refs
        sets = [
            ((own_l, low_l, high_l), 8 * CUT, 8),
            ((own_u, low_u, high_u), 8 * (TILES - 1 - CUT), 8 + 8 * CUT),
        ]
        halo, counts = 0, gz == 1
        held = [(t, t - 1) for t in range(1, TILES)]
    ea0, ea1, eb0, eb1, ma0, ma1, mb0, mb1, d0, d1, g0, g1, ya, yb, ym, stage, sems = scratch
    es, ms, yes = ((ea0, ea1), (eb0, eb1)), ((ma0, ma1), (mb0, mb1)), (ya, yb)
    ds_, gs = (d0, d1), (g0, g1)

    moves = []
    for (own, low, high), layers, to in sets:
        src, zf, zd = pl.ds(0, layers), pl.ds(8 + to, layers), pl.ds(to, layers)
        first, mid, last_ = BASE, BASE + W, BASE + W + 8
        for ref, a, n, dst, b, z in (
            (own, 0, 24, ea0, 3 * mid, zf),
            (own, 24, 24, ma0, 3 * mid, zf),
            (own, 48, 8, d0, mid, zd),
            (low, 0, 18, ea0, 3 * first, zf),
            (low, 18, 2, ma0, 3 * first, zf),
            (low, 20, 15, ma0, 3 * first + 3, zf),
            (low, 35, 5, d0, first + 1, zd),
            (high, 0, 17, ea0, 3 * last_, zf),
            (high, 17, 15, ma0, 3 * last_, zf),
            (high, 32, 5, d0, last_, zd),
        ):
            moves.append((ref.at[pl.ds(a, n), src], dst.at[pl.ds(b, n), z]))
    copies = [pltpu.make_async_copy(a, b, sems.at[i]) for i, (a, b) in enumerate(moves)]
    for copy in copies:
        copy.start()

    zero = jnp.zeros((8, 128), F32)
    top = 8 + 8 * TILES

    def unpack(ref, first, ref_z, first_z, count, row):
        def body(r, _):
            at = BASE + row + r
            for t, tile in held + [(halo, None)]:
                v = ref_z[first_z + r] if tile is None else ref[first + 10 * r + tile]
                z = 8 * t
                for c in range(NC):
                    turned = pltpu.roll(v, 128 - 16 * c, 1) if c else v
                    if c < 3:
                        ea1[3 * at + c, 8 + z : 16 + z, :] = turned
                    elif c < 6:
                        ma1[3 * at + c - 3, 8 + z : 16 + z, :] = turned
                    else:
                        d1[at, z : z + 8, :] = turned
            return 0

        lax.fori_loop(0, count, body, 0)

    unpack(low_c, 40, low_c, 100, W, 0)
    unpack(strips, 0, edge, 56, 8, W)
    unpack(high_c, 37, high_c, 97, W, W + 8)

    def ends(r, _):
        for pair in ms:
            for m in pair:
                m[3 * r + X, 0:8, :] = zero
                m[3 * r + Y, 0:8, :] = zero
        for pair in es:
            for e in pair:
                e[3 * r + X, top : top + 8, :] = zero
                e[3 * r + Y, top : top + 8, :] = zero
        return 0

    lax.fori_loop(0, HELD, ends, 0)
    hz = 8 * halo

    @pl.when(counts)
    def _():
        for ref, a, n, dst, b, to in (
            (edge, 0, 24, ea0, 3 * (BASE + W), 8),
            (edge, 24, 24, ma0, 3 * (BASE + W), 8),
            (edge, 48, 8, d0, BASE + W, 0),
            (low_c, 0, 18, ea0, 3 * BASE, 8),
            (low_c, 18, 2, ma0, 3 * BASE, 8),
            (low_c, 20, 15, ma0, 3 * BASE + 3, 8),
            (low_c, 35, 5, d0, BASE + 1, 0),
            (high_c, 0, 17, ea0, 3 * (BASE + W + 8), 8),
            (high_c, 17, 15, ma0, 3 * (BASE + W + 8), 8),
            (high_c, 32, 5, d0, BASE + W + 8, 0),
        ):
            for i in range(n):
                dst[b + i, hz + to : hz + to + 8, :] = ref[a + i]

    @pl.when(jnp.logical_not(counts))
    def _():
        def clear(i, _):
            for ref in (ea0, ea1, ma0, ma1):
                ref[3 * BASE + i, hz + 8 : hz + 16, :] = zero
            return 0

        lax.fori_loop(0, 3 * ROWS, clear, 0)

    for copy in copies:
        copy.wait()

    live = jnp.where(counts, 1.0, 0.0).astype(F32)

    def tables(r, _):
        for t in range(TILES):
            z = 8 * t
            for d, g in zip(ds_, gs):
                ids = d[r, z : z + 8, :]
                d_cells, g_cells = zero, zero
                for i in range(5):
                    hit = ids == float(i)
                    d_cells = jnp.where(hit, decay[i], d_cells)
                    g_cells = jnp.where(hit, gain[i] * 0.5, g_cells)
                if t == halo:
                    d_cells, g_cells = d_cells * live, g_cells * live
                d[r, z : z + 8, :] = d_cells
                g[r, z : z + 8, :] = g_cells
        return 0

    lax.fori_loop(BASE + 1, BASE + ROWS - 1, tables, 0)

    lane = lax.broadcasted_iota(jnp.int32, (8, 128), 1)
    last, first_lane = lane == 127, lane == 0
    units = [(row, t) for row in range(2) for t in range(TILES)]

    def first_turn(i, _):
        kept = []
        for row, t in units:
            r = BASE + 2 * i + row
            for j, c in enumerate((X, Z)):
                pair = [pltpu.roll(e[3 * r + c, 8 + 8 * t : 16 + 8 * t, :], 127, 1) for e in es[0]]
                kept.append((4 * r + 2 * j, 8 * t, pair))
        for i, z, (a, b) in kept:
            ya[i, z : z + 8, :] = jnp.where(last, b, a)
            ya[i + 1, z : z + 8, :] = jnp.where(last, a, b)
        return 0

    lax.fori_loop(0, ROWS // 2, first_turn, 0)

    def block(old, m, start):
        new = 1 - old
        base = start + 2 * m
        b3, b4 = 3 * base, 4 * base
        waiting = []

        def keep():
            for y, b, i, z, (a, c), edge_lane in waiting.pop(0):
                y[b + i, z : z + 8, :] = jnp.where(edge_lane, c, a)
                y[b + (i + 1), z : z + 8, :] = jnp.where(edge_lane, a, c)

        for row, t in units:
            e, z = row - 2, 8 * t
            turned = [[], []]
            for k in range(2):

                def magnetic(c, r=e, shift=0):
                    return ms[new][k][b3 + (3 * r + c), 8 + z + shift : 16 + z + shift, :]

                def electric(c):
                    return es[old][k][b3 + (3 * e + c), 8 + z : 16 + z, :]

                mx_y = ym[4 * row + k, z : z + 8, :]
                mz_y = ym[4 * row + 2 + k, z : z + 8, :]
                mx, my, mz = magnetic(X), magnetic(Y), magnetic(Z)
                d = ds_[k][base + e, z : z + 8, :]
                g = gs[k][base + e, z : z + 8, :]
                ex = d * electric(X) + g * ((mz - mz_y) - (my - magnetic(Y, e, -1)))
                ey = d * electric(Y) + g * ((mx - magnetic(X, e, -1)) - (mz - magnetic(Z, e - 1)))
                ez = d * electric(Z) + g * ((my - magnetic(Y, e - 1)) - (mx - mx_y))
                for c, v in ((X, ex), (Y, ey), (Z, ez)):
                    es[new][k][b3 + (3 * e + c), 8 + z : 16 + z, :] = v
                turned[0].append(pltpu.roll(ex, 127, 1))
                turned[1].append(pltpu.roll(ez, 127, 1))
            waiting.append(
                [(yes[new], b4, 4 * e + 2 * j, z, turned[j], last) for j in range(2)]
            )
            if len(waiting) > LAG:
                keep()
        for row, t in units:
            z = 8 * t
            turned = [[], []]
            for k in range(2):

                def electric(c, r=row, shift=0):
                    return es[old][k][b3 + (3 * r + c), 8 + z + shift : 16 + z + shift, :]

                def magnetic(c):
                    return ms[old][k][b3 + (3 * row + c), 8 + z : 16 + z, :]

                ex_y = yes[old][b4 + (4 * row + k), z : z + 8, :]
                ez_y = yes[old][b4 + (4 * row + 2 + k), z : z + 8, :]
                ex, ey, ez = electric(X), electric(Y), electric(Z)
                cx = (ez_y - ez) - (electric(Y, row, 1) - ey)
                cy = (electric(X, row, 1) - ex) - (electric(Z, row + 1) - ez)
                cz = (electric(Y, row + 1) - ey) - (ex_y - ex)
                if t == halo and not upper:
                    cx, cy, cz = cx * live, cy * live, cz * live
                mx, my, mz = magnetic(X) - cx, magnetic(Y) - cy, magnetic(Z) - cz
                for c, v in ((X, mx), (Y, my), (Z, mz)):
                    ms[new][k][b3 + (3 * row + c), 8 + z : 16 + z, :] = v
                turned[0].append(pltpu.roll(mx, 1, 1))
                turned[1].append(pltpu.roll(mz, 1, 1))
            waiting.append([(ym, 0, 4 * row + 2 * j, z, turned[j], first_lane) for j in range(2)])
            if len(waiting) > LAG:
                keep()
        while waiting:
            keep()
        return start

    def two_steps(s, _):
        for old in range(2):
            left = STEPS - 1 - old - 2 * s
            lax.fori_loop(0, W + left, functools.partial(block, old), BASE + W - left - 2)
        return 0

    lax.fori_loop(0, STEPS // 2, two_steps, 0)

    def emit(r, _):
        for c, source in enumerate((X, Y, Z)):
            for t in range(ON):
                stage[c, pl.ds(64 * t + r, 8, stride=8), :] = ea0[
                    3 * (r + BASE + W) + source, 16 + 8 * t : 24 + 8 * t, :
                ]
        return 0

    lax.fori_loop(0, 8, emit, 0)
    if upper:
        plane[0] = stage[0, 64 * ON - 8 : 64 * ON, :]
        plane[1] = stage[1, 64 * ON - 8 : 64 * ON, :]
    copy_all([(stage, out.at[:, pl.ds(64 * ON if upper else 0, 64 * ON)])], sems)


def run_steps(upper, decay, gain, sides, arrays):
    smem = pl.BlockSpec(memory_space=pltpu.SMEM)
    out_shape = [jax.ShapeDtypeStruct((3, 640, 128), F32)]
    out_specs = [HBM]
    aliases = {}
    if upper:
        out_shape.append(jax.ShapeDtypeStruct((2, 8, 128), F32))
        out_specs.append(LOCAL)
    else:
        aliases = {6 + len(arrays) - 1: 0}
    z = 16 + 8 * TILES
    field = pltpu.VMEM((3 * HELD, z, 128), F32)
    table = pltpu.VMEM((HELD, 8 * TILES, 128), F32)
    turned = pltpu.VMEM((4 * HELD, 8 * TILES, 128), F32)
    return pl.pallas_call(
        functools.partial(steps_kernel, upper),
        out_shape=out_shape,
        in_specs=[smem, smem] + [LOCAL] * 4 + [HBM] * len(arrays),
        out_specs=out_specs,
        scratch_shapes=[field] * 8
        + [table] * 4
        + [turned] * 2
        + [
            pltpu.VMEM((8, 8 * TILES, 128), F32),
            pltpu.VMEM((3, 64 * ON, 128), F32),
            pltpu.SemaphoreType.DMA((20,)),
        ],
        input_output_aliases=aliases,
        compiler_params=params(),
        cost_estimate=cost(15),
        name="steps_upper" if upper else "steps_lower",
    )(decay, gain, *sides, *arrays)


def image_kernel(weights, centre, before, after, out, sh, rhs):
    gz = lax.axis_index("gz")
    lane = lax.broadcasted_iota(jnp.int32, (24, 128), 1)
    for q in range(15):
        shift = q - 7
        for c in range(2):
            v = centre[c]
            if shift > 0:
                v = jnp.where(
                    lane >= 128 - shift,
                    pltpu.roll(after[c], 128 - shift, 1),
                    pltpu.roll(v, 128 - shift, 1),
                )
            elif shift < 0:
                v = jnp.where(
                    lane < -shift, pltpu.roll(before[c], -shift, 1), pltpu.roll(v, -shift, 1)
                )
            sh[q, c] = v

    def fill(side):
        for q in range(15):
            for c in range(2):
                for i in range(4):
                    start = 4 * side + 1 + i
                    rhs[16 * q : 16 * q + 16, (4 * c + i) * 128 : (4 * c + i + 1) * 128] = sh[
                        q, c, start : start + 16, :
                    ]

    @pl.when(gz == 0)
    def _():
        fill(0)

    @pl.when(gz == 1)
    def _():
        fill(1)

    amplitude = jnp.dot(
        weights[...],
        rhs[...],
        precision=lax.Precision.HIGHEST,
        preferred_element_type=jnp.float32,
    )
    power = jnp.sum(amplitude * amplitude, axis=0, keepdims=True)
    for i in range(4):
        out[i : i + 1, :] = (
            power[:, i * 128 : (i + 1) * 128] + power[:, (4 + i) * 128 : (5 + i) * 128]
        )


def image_of(weights, centre, before, after):
    return pl.pallas_call(
        image_kernel,
        out_shape=jax.ShapeDtypeStruct((4, 128), jnp.float32),
        in_specs=[pl.BlockSpec(memory_space=pltpu.VMEM)] * 4,
        out_specs=pl.BlockSpec(memory_space=pltpu.VMEM),
        scratch_shapes=[
            pltpu.VMEM((15, 2, 24, 128), jnp.float32),
            pltpu.VMEM((240, 1024), jnp.float32),
        ],
        compiler_params=pltpu.CompilerParams(vmem_limit_bytes=VMEM),
        name="image",
    )(weights, centre, before, after)


def behind(value, *others):
    return lax.optimization_barrier((value, *others))[0]


def on_device(electric, magnetic, material, decay, gain, kernels):
    el = electric.reshape(3, 640, 128)
    mg = magnetic.reshape(3, 640, 128)
    mat = material.reshape(640, 128)
    weights = jnp.pad(
        kernels.transpose(0, 1, 3, 2).reshape(48, 15, 15), ((0, 0), (0, 0), (0, 1))
    ).reshape(48, 240)

    own_u, up_u, down_u, strip_u = pack(CUT, 10, el, mg, mat)
    low_u, high_u = around(up_u, "gx", 1), around(down_u, "gx", -1)
    own_l, up_l, down_l, strip = pack(0, CUT, el, mg, mat, strip_u)
    strips, edge = edges(around(strip, "gy", 1), around(strip, "gy", -1), own_u, own_l)
    strips = strips.reshape(80, 8, 128)
    edge = around(edge, "gz", 1)
    up_c, down_c = corners(strips, edge)
    low_c, high_c = around(up_c, "gx", 1), around(down_c, "gx", -1)
    up_l, down_l = behind((up_l, down_l), up_c)
    low_l, high_l = around(up_l, "gx", 1), around(down_l, "gx", -1)

    sides = [strips, edge, low_c, high_c]
    field, plane = run_steps(True, decay, gain, sides, [own_u, low_u, high_u])
    top = lax.ppermute(plane, "gz", [(1, 0)])
    top = jnp.where(lax.axis_index("gz") == 1, plane, top)
    top = jnp.stack([top, around(top, "gy", 1), around(top, "gy", -1)])
    top = jnp.concatenate([around(top, "gx", 1), top, around(top, "gx", -1)], 2)
    image = image_of(weights, top[0], top[1], top[2])
    (field,) = run_steps(
        False, decay, gain, sides, [own_u, low_u, high_u, own_l, low_l, high_l, field]
    )
    return (field.reshape(3, 80, 8, 128), image)


def solution(mesh):
    in_specs = (
        P(None, "gz", "gx", "gy"),
        P(None, "gz", "gx", "gy"),
        P("gz", "gx", "gy"),
        P(),
        P(),
        P(),
    )
    out_specs = (P(None, "gz", "gx", "gy"), P(("gx", "gz"), "gy"))
    return jax.shard_map(
        on_device, mesh=mesh, in_specs=in_specs, out_specs=out_specs, check_vma=False
    )
```

profile of v0, /device:TPU:2, one launch (start us, length us, event | category | flops | bytes accessed | tf_op | source)
XLA Modules:
  0.0 159.4 jit_solution(8731395843017659181)
XLA Ops:
  0.6 4.1 %pack_upper.1 = (f32[56,48,128]{2,1,0:T(8,128)}, f32[40,48,128]{2,1,0:T(8,128)}, f32[37,48,128]{2,1,0:T(8,128)}, f32[8,48,128]{2,1,0:T(8,128)}) custom-call(f32[3,640,128]{2,1,0:T(8,128)} %bitcast.18, f32[3,640,128]{2,1,0:T(8,128)} %bitcast.20, s32[640,128]{1,0:T(8,128)} %bitcast.25), custom_call_target="tpu_custom_call" | custom-call | bytes 9000000 | tf_op jit(solution)/shard_map/pack_upper/pallas_call | solution.py:102
  4.7 0.0 copy-start.10
  4.7 0.0 copy-start.11
  4.8 9.3 %pack_lower.1 = (f32[56,32,128]{2,1,0:T(8,128)}, f32[40,32,128]{2,1,0:T(8,128)}, f32[37,32,128]{2,1,0:T(8,128)}, f32[8,80,128]{2,1,0:T(8,128)}) custom-call(f32[3,640,128]{2,1,0:T(8,128)} %bitcast.19, f32[3,640,128]{2,1,0:T(8,128)} %bitcast.21, s32[640,128]{1,0:T(8,128)} %bitcast.26, f32[8,48,128]{2,1,0:T(8,128)} %get-tuple-element.18.refs_0_), custom_call_target="tpu_custom_call" | custom-call | bytes 9000000 | tf_op jit(solution)/shard_map/pack_lower/pallas_call | solution.py:102
  14.1 1.6 %collective-permute-start = (f32[8,80,128]{2,1,0:T(8,128)}, f32[8,80,128]{2,1,0:T(8,128)S(1)}, u32[]{:S(2)}, u32[]{:S(2)}) collective-permute-start(f32[8,80,128]{2,1,0:T(8,128)} %get-tuple-element.19), channel_id=1, source_target_pairs={{0,2},{2,4},{4,6},{6,0},{1,3},{3,5},{5,7},{7,1},{8,10},{10,12},{12... | collective-permute-start | bytes 983048 | tf_op jit(solution)/shard_map/ppermute | solution.py:30
  15.7 1.7 %collective-permute-start.1 = (f32[8,80,128]{2,1,0:T(8,128)}, f32[8,80,128]{2,1,0:T(8,128)S(1)}, u32[]{:S(2)}, u32[]{:S(2)}) collective-permute-start(f32[8,80,128]{2,1,0:T(8,128)} %get-tuple-element.19), channel_id=1, source_target_pairs={{0,6},{2,0},{4,2},{6,4},{1,7},{3,1},{5,3},{7,5},{8,14},{10,8},{12,... | collective-permute-start | bytes 983048 | tf_op jit(solution)/shard_map/ppermute | solution.py:30
  17.4 0.0 copy-done.10
  17.4 0.0 collective-permute-start.5
  17.4 0.0 copy-done.11
  17.4 5.4 %collective-permute-start.6 = (f32[37,48,128]{2,1,0:T(8,128)S(1)}, f32[37,48,128]{2,1,0:T(8,128)S(1)}, u32[]{:S(2)}, u32[]{:S(2)}) collective-permute-start(f32[37,48,128]{2,1,0:T(8,128)S(1)} %copy-done.11), channel_id=1, source_target_pairs={{0,120},{8,0},{16,8},{24,16},{32,24},{40,32},{48,40},{56,48},{64,5... | collective-permute-start | bytes 2727944 | tf_op jit(solution)/shard_map/ppermute | solution.py:30
  22.7 2.3 %collective-permute-done.from_low = f32[8,80,128]{2,1,0:T(8,128)S(1)} collective-permute-done((f32[8,80,128]{2,1,0:T(8,128)}, f32[8,80,128]{2,1,0:T(8,128)S(1)}, u32[]{:S(2)}, u32[]{:S(2)}) %collective-permute-start) | collective-permute-done | bytes 327712 | tf_op jit(solution)/shard_map/ppermute | solution.py:30
  25.1 0.0 copy-start.7
  25.1 0.0 collective-permute-done.1.from_high
  25.1 0.0 copy-start.8
  25.1 0.7 copy-done.7
  25.8 0.1 copy-done.8
  25.9 2.9 %edges.1 = (f32[8,80,128]{2,1,0:T(8,128)}, f32[64,8,128]{2,1,0:T(8,128)}) custom-call(f32[8,80,128]{2,1,0:T(8,128)} %copy-done.7, f32[8,80,128]{2,1,0:T(8,128)} %copy-done.8, f32[56,48,128]{2,1,0:T(8,128)} %get-tuple-element.20.own_u.refs_0_, f32[56,32,128]{2,1,0:T(8,128)} %get-tuple-element.21.own_l.refs_3_), custom_call_target="tpu_custom_call" | custom-call | bytes 3000000 | tf_op jit(solution)/shard_map/edges/pallas_call | solution.py:142
  28.8 0.6 collective-permute-start.2
  29.4 18.4 %collective-permute-done.2.edge = f32[64,8,128]{2,1,0:T(8,128)S(1)} collective-permute-done((f32[64,8,128]{2,1,0:T(8,128)}, f32[64,8,128]{2,1,0:T(8,128)S(1)}, u32[]{:S(2)}, u32[]{:S(2)}) %collective-permute-start.2) | collective-permute-done | bytes 262176 | tf_op jit(solution)/shard_map/ppermute | solution.py:30
  47.8 0.0 copy-start.2
  47.8 0.7 copy-done.2
  48.5 27.1 %corners.1 = (f32[106,8,128]{2,1,0:T(8,128)}, f32[103,8,128]{2,1,0:T(8,128)}) custom-call(f32[80,8,128]{2,1,0:T(8,128)} %bitcast.22, f32[64,8,128]{2,1,0:T(8,128)} %copy-done.2), custom_call_target="tpu_custom_call" | custom-call | bytes 3000000 | tf_op jit(solution)/shard_map/corners/pallas_call | solution.py:172
  75.6 0.1 collective-permute-start.3
  75.7 0.0 copy-start.12
  75.7 0.0 copy-start.13
  75.7 0.0 copy-start.9
  75.8 5.3 %collective-permute-start.4 = (f32[103,8,128]{2,1,0:T(8,128)}, f32[103,8,128]{2,1,0:T(8,128)S(1)}, u32[]{:S(2)}, u32[]{:S(2)}) collective-permute-start(f32[103,8,128]{2,1,0:T(8,128)} %get-tuple-element.25), channel_id=1, source_target_pairs={{0,120},{8,0},{16,8},{24,16},{32,24},{40,32},{48,40},{56,48},{64,5... | collective-permute-start | bytes 1265672 | tf_op jit(solution)/shard_map/ppermute | solution.py:30
  81.1 0.0 collective-permute-done.6.refs_2_
  81.1 0.0 collective-permute-done.5.refs_1_
  81.1 0.0 copy-start
  81.1 5.9 %collective-permute-done.4.high_c = f32[103,8,128]{2,1,0:T(8,128)S(1)} collective-permute-done((f32[103,8,128]{2,1,0:T(8,128)}, f32[103,8,128]{2,1,0:T(8,128)S(1)}, u32[]{:S(2)}, u32[]{:S(2)}) %collective-permute-start.4) | collective-permute-done | bytes 421920 | tf_op jit(solution)/shard_map/ppermute | solution.py:30
  87.0 4.1 %collective-permute-done.3.low_c = f32[106,8,128]{2,1,0:T(8,128)S(1)} collective-permute-done((f32[106,8,128]{2,1,0:T(8,128)}, f32[106,8,128]{2,1,0:T(8,128)S(1)}, u32[]{:S(2)}, u32[]{:S(2)}) %collective-permute-start.3) | collective-permute-done | bytes 434208 | tf_op jit(solution)/shard_map/ppermute | solution.py:30
  91.1 0.0 copy-done.1
  91.1 0.0 copy-done
  91.1 0.0 copy-done.4
  91.1 0.0 copy-start.3
  91.1 0.7 copy-done.3
  91.8 21.2 %steps_upper.1 = (f32[3,640,128]{2,1,0:T(8,128)}, f32[2,8,128]{2,1,0:T(8,128)}) custom-call(f32[5]{0:T(128)} %decay.3, f32[5]{0:T(128)} %gain.3, f32[80,8,128]{2,1,0:T(8,128)} %bitcast.23, f32[64,8,128]{2,1,0:T(8,128)} %copy-done.2, f32[106,8,128]{2,1,0:T(8,128)} %copy-done.3, f32[103,8,128]{2,1,0:T(8,128)} %copy-done.4, ...), custom_call_target="tpu_custom_call" | custom-call | bytes 45000000 | tf_op jit(solution)/shard_map/steps_upper/pallas_call | solution.py:440
  113.0 1.3 collective-permute-start.9
  114.3 0.0 copy-done.12
  114.3 1.1 collective-permute-start.7
  115.5 0.0 copy-done.13
  115.5 4.3 %collective-permute-start.8 = (f32[37,32,128]{2,1,0:T(8,128)S(1)}, f32[37,32,128]{2,1,0:T(8,128)S(1)}, u32[]{:S(2)}, u32[]{:S(2)}) collective-permute-start(f32[37,32,128]{2,1,0:T(8,128)S(1)} %copy-done.13), channel_id=1, source_target_pairs={{0,120},{8,0},{16,8},{24,16},{32,24},{40,32},{48,40},{56,48},{64,5... | collective-permute-start | bytes 1818632 | tf_op jit(solution)/shard_map/ppermute | solution.py:30
  119.7 0.0 collective-permute-done.9
  119.8 0.7 broadcast_select_fusion
  120.5 0.4 collective-permute-start.10
  120.8 2.9 %collective-permute-start.11 = (f32[2,8,128]{2,1,0:T(8,128)S(1)}, f32[2,8,128]{2,1,0:T(8,128)S(1)}, u32[]{:S(2)}, u32[]{:S(2)}) collective-permute-start(f32[2,8,128]{2,1,0:T(8,128)S(1)} %broadcast_select_fusion), channel_id=1, source_target_pairs={{0,6},{2,0},{4,2},{6,4},{1,7},{3,1},{5,3},{7,5},{8,14},{10,8},{12,... | collective-permute-start | bytes 24584 | tf_op jit(solution)/shard_map/ppermute | solution.py:30
  123.7 1.6 %collective-permute-done.10 = f32[2,8,128]{2,1,0:T(8,128)S(1)} collective-permute-done((f32[2,8,128]{2,1,0:T(8,128)S(1)}, f32[2,8,128]{2,1,0:T(8,128)S(1)}, u32[]{:S(2)}, u32[]{:S(2)}) %collective-permute-start.10) | collective-permute-done | bytes 8224 | tf_op jit(solution)/shard_map/ppermute | solution.py:30
  125.3 0.0 collective-permute-done.11
  125.3 0.0 collective-permute-start.12
  125.3 5.4 %collective-permute-start.13 = (f32[3,2,8,128]{3,2,1,0:T(8,128)S(1)}, f32[3,2,8,128]{3,2,1,0:T(8,128)S(1)}, u32[]{:S(2)}, u32[]{:S(2)}) collective-permute-start(f32[3,2,8,128]{3,2,1,0:T(8,128)S(1)} %pad_maximum_fusion.1), channel_id=1, source_target_pairs={{0,120},{8,0},{16,8},{24,16},{32,24},{40,32},{48,40},{56,48},{64,5... | collective-permute-start | bytes 73736 | tf_op jit(solution)/shard_map/ppermute | solution.py:30
  130.7 0.0 copy-done.9
  130.7 0.2 reshape.30
  130.9 0.7 copy.11.weights
  131.6 3.4 %collective-permute-done.12 = f32[3,2,8,128]{3,2,1,0:T(8,128)S(1)} collective-permute-done((f32[3,2,8,128]{3,2,1,0:T(8,128)S(1)}, f32[3,2,8,128]{3,2,1,0:T(8,128)S(1)}, u32[]{:S(2)}, u32[]{:S(2)}) %collective-permute-start.12) | collective-permute-done | bytes 24608 | tf_op jit(solution)/shard_map/ppermute | solution.py:30
  135.0 0.0 collective-permute-done.13
  135.0 0.6 slice_bitcast_fusion
  135.7 2.4 %image.1 = f32[4,128]{1,0:T(4,128)} custom-call(f32[48,240]{1,0:T(8,128)} %copy.11.weights, f32[2,24,128]{2,1,0:T(8,128)} %get-tuple-element.36.centre, f32[2,24,128]{2,1,0:T(8,128)} %get-tuple-element.35.before, f32[2,24,128]{2,1,0:T(8,128)} %get-tuple-element.34.after), custom_call_target="tpu_custom_call" | custom-call | tf_op jit(solution)/shard_map/image/pallas_call | solution.py:510
  138.1 0.0 collective-permute-done.8.refs_5_
  138.1 0.0 collective-permute-done.7.refs_4_
  138.1 0.0 copy-start.5
  138.1 0.8 copy-done.6
  138.9 0.2 copy-done.5
  139.2 20.2 %steps_lower.1 = f32[3,640,128]{2,1,0:T(8,128)} custom-call(f32[5]{0:T(128)} %decay.3, f32[5]{0:T(128)} %gain.3, f32[80,8,128]{2,1,0:T(8,128)} %bitcast.24, f32[64,8,128]{2,1,0:T(8,128)} %copy-done.2, f32[106,8,128]{2,1,0:T(8,128)} %copy-done.3, f32[103,8,128]{2,1,0:T(8,128)} %copy-done.4, ...), custom_call_target="tpu_custom_call", output_to_operand_aliasing={{}: (12, {})} | custom-call | bytes 45000000 | tf_op jit(solution)/shard_map/steps_lower/pallas_call | solution.py:440
  (7 shorter events, 0.1 us)
Async XLA Ops:
  4.7 12.6 %copy-start.10 = (f32[40,48,128]{2,1,0:T(8,128)S(1)}, f32[40,48,128]{2,1,0:T(8,128)}, u32[]{:S(2)}) copy-start(f32[40,48,128]{2,1,0:T(8,128)} %get-tuple-element.26) | copy-start | bytes 2949124
  4.7 12.6 %copy-start.11 = (f32[37,48,128]{2,1,0:T(8,128)S(1)}, f32[37,48,128]{2,1,0:T(8,128)}, u32[]{:S(2)}) copy-start(f32[37,48,128]{2,1,0:T(8,128)} %get-tuple-element.27) | copy-start | bytes 2727940
  14.1 11.0 %collective-permute-start = (f32[8,80,128]{2,1,0:T(8,128)}, f32[8,80,128]{2,1,0:T(8,128)S(1)}, u32[]{:S(2)}, u32[]{:S(2)}) collective-permute-start(f32[8,80,128]{2,1,0:T(8,128)} %get-tuple-element.19), channel_id=1, source_target_pairs={{0,2},{2,4},{4,6},{6,0},{1,3},{3,5},{5,7},{7,1},{8,10},{10,12},{12... | collective-permute-start | bytes 983048 | tf_op jit(solution)/shard_map/ppermute | solution.py:30
  15.7 9.4 %collective-permute-start.1 = (f32[8,80,128]{2,1,0:T(8,128)}, f32[8,80,128]{2,1,0:T(8,128)S(1)}, u32[]{:S(2)}, u32[]{:S(2)}) collective-permute-start(f32[8,80,128]{2,1,0:T(8,128)} %get-tuple-element.19), channel_id=1, source_target_pairs={{0,6},{2,0},{4,2},{6,4},{1,7},{3,1},{5,3},{7,5},{8,14},{10,8},{12,... | collective-permute-start | bytes 983048 | tf_op jit(solution)/shard_map/ppermute | solution.py:30
  17.4 63.7 %collective-permute-start.5 = (f32[40,48,128]{2,1,0:T(8,128)S(1)}, f32[40,48,128]{2,1,0:T(8,128)S(1)}, u32[]{:S(2)}, u32[]{:S(2)}) collective-permute-start(f32[40,48,128]{2,1,0:T(8,128)S(1)} %copy-done.10), channel_id=1, source_target_pairs={{0,8},{8,16},{16,24},{24,32},{32,40},{40,48},{48,56},{56,64},{64,7... | collective-permute-start | bytes 2949128 | tf_op jit(solution)/shard_map/ppermute | solution.py:30
  17.4 63.7 %collective-permute-start.6 = (f32[37,48,128]{2,1,0:T(8,128)S(1)}, f32[37,48,128]{2,1,0:T(8,128)S(1)}, u32[]{:S(2)}, u32[]{:S(2)}) collective-permute-start(f32[37,48,128]{2,1,0:T(8,128)S(1)} %copy-done.11), channel_id=1, source_target_pairs={{0,120},{8,0},{16,8},{24,16},{32,24},{40,32},{48,40},{56,48},{64,5... | collective-permute-start | bytes 2727944 | tf_op jit(solution)/shard_map/ppermute | solution.py:30
  25.1 0.7 copy-start.7
  25.1 0.8 copy-start.8
  28.8 19.0 %collective-permute-start.2 = (f32[64,8,128]{2,1,0:T(8,128)}, f32[64,8,128]{2,1,0:T(8,128)S(1)}, u32[]{:S(2)}, u32[]{:S(2)}) collective-permute-start(f32[64,8,128]{2,1,0:T(8,128)} %get-tuple-element.23), channel_id=1, source_target_pairs={{0,1},{1,0},{2,3},{3,2},{4,5},{5,4},{6,7},{7,6},{8,9},{9,8},{10,11... | collective-permute-start | bytes 786440 | tf_op jit(solution)/shard_map/ppermute | solution.py:30
  47.8 0.7 copy-start.2
  75.6 15.4 %collective-permute-start.3 = (f32[106,8,128]{2,1,0:T(8,128)}, f32[106,8,128]{2,1,0:T(8,128)S(1)}, u32[]{:S(2)}, u32[]{:S(2)}) collective-permute-start(f32[106,8,128]{2,1,0:T(8,128)} %get-tuple-element.24), channel_id=1, source_target_pairs={{0,8},{8,16},{16,24},{24,32},{32,40},{40,48},{48,56},{56,64},{64,7... | collective-permute-start | bytes 1302536 | tf_op jit(solution)/shard_map/ppermute | solution.py:30
  75.7 38.6 %copy-start.12 = (f32[40,32,128]{2,1,0:T(8,128)S(1)}, f32[40,32,128]{2,1,0:T(8,128)}, u32[]{:S(2)}) copy-start(f32[40,32,128]{2,1,0:T(8,128)} %get-tuple-element.30) | copy-start | bytes 1966084
  75.7 39.7 %copy-start.13 = (f32[37,32,128]{2,1,0:T(8,128)S(1)}, f32[37,32,128]{2,1,0:T(8,128)}, u32[]{:S(2)}) copy-start(f32[37,32,128]{2,1,0:T(8,128)} %get-tuple-element.31) | copy-start | bytes 1818628
  75.7 54.9 %copy-start.9 = (f32[2,24,15,15]{1,0,3,2:T(2,128)S(1)}, f32[2,24,15,15]{1,0,3,2:T(2,128)}, u32[]{:S(2)}) copy-start(f32[2,24,15,15]{1,0,3,2:T(2,128)} %param.11) | copy-start | bytes 129604
  75.8 11.2 %collective-permute-start.4 = (f32[103,8,128]{2,1,0:T(8,128)}, f32[103,8,128]{2,1,0:T(8,128)S(1)}, u32[]{:S(2)}, u32[]{:S(2)}) collective-permute-start(f32[103,8,128]{2,1,0:T(8,128)} %get-tuple-element.25), channel_id=1, source_target_pairs={{0,120},{8,0},{16,8},{24,16},{32,24},{40,32},{48,40},{56,48},{64,5... | collective-permute-start | bytes 1265672 | tf_op jit(solution)/shard_map/ppermute | solution.py:30
  81.1 10.0 %copy-start.1 = (f32[37,48,128]{2,1,0:T(8,128)}, f32[37,48,128]{2,1,0:T(8,128)S(1)}, u32[]{:S(2)}) copy-start(f32[37,48,128]{2,1,0:T(8,128)S(1)} %collective-permute-done.6.refs_2_) | copy-start | bytes 2727940
  81.1 10.0 %copy-start = (f32[40,48,128]{2,1,0:T(8,128)}, f32[40,48,128]{2,1,0:T(8,128)S(1)}, u32[]{:S(2)}) copy-start(f32[40,48,128]{2,1,0:T(8,128)S(1)} %collective-permute-done.5.refs_1_) | copy-start | bytes 2949124
  87.0 4.1 %copy-start.4 = (f32[103,8,128]{2,1,0:T(8,128)}, f32[103,8,128]{2,1,0:T(8,128)S(1)}, u32[]{:S(2)}) copy-start(f32[103,8,128]{2,1,0:T(8,128)S(1)} %collective-permute-done.4.high_c) | copy-start | bytes 1265668
  91.1 0.8 copy-start.3
  113.0 6.7 %collective-permute-start.9 = (f32[2,8,128]{2,1,0:T(8,128)}, f32[2,8,128]{2,1,0:T(8,128)S(1)}, u32[]{:S(2)}, u32[]{:S(2)}) collective-permute-start(f32[2,8,128]{2,1,0:T(8,128)} %get-tuple-element.33), channel_id=1, source_target_pairs={{1,0},{3,2},{5,4},{7,6},{9,8},{11,10},{13,12},{15,14},{17,16},{19,... | collective-permute-start | bytes 24584 | tf_op jit(solution)/shard_map/ppermute | solution.py:549
  114.3 23.8 %collective-permute-start.7 = (f32[40,32,128]{2,1,0:T(8,128)S(1)}, f32[40,32,128]{2,1,0:T(8,128)S(1)}, u32[]{:S(2)}, u32[]{:S(2)}) collective-permute-start(f32[40,32,128]{2,1,0:T(8,128)S(1)} %copy-done.12), channel_id=1, source_target_pairs={{0,8},{8,16},{16,24},{24,32},{32,40},{40,48},{48,56},{56,64},{64,7... | collective-permute-start | bytes 1966088 | tf_op jit(solution)/shard_map/ppermute | solution.py:30
  115.5 22.6 %collective-permute-start.8 = (f32[37,32,128]{2,1,0:T(8,128)S(1)}, f32[37,32,128]{2,1,0:T(8,128)S(1)}, u32[]{:S(2)}, u32[]{:S(2)}) collective-permute-start(f32[37,32,128]{2,1,0:T(8,128)S(1)} %copy-done.13), channel_id=1, source_target_pairs={{0,120},{8,0},{16,8},{24,16},{32,24},{40,32},{48,40},{56,48},{64,5... | collective-permute-start | bytes 1818632 | tf_op jit(solution)/shard_map/ppermute | solution.py:30
  120.5 4.9 %collective-permute-start.10 = (f32[2,8,128]{2,1,0:T(8,128)S(1)}, f32[2,8,128]{2,1,0:T(8,128)S(1)}, u32[]{:S(2)}, u32[]{:S(2)}) collective-permute-start(f32[2,8,128]{2,1,0:T(8,128)S(1)} %broadcast_select_fusion), channel_id=1, source_target_pairs={{0,2},{2,4},{4,6},{6,0},{1,3},{3,5},{5,7},{7,1},{8,10},{10,12},{12... | collective-permute-start | bytes 24584 | tf_op jit(solution)/shard_map/ppermute | solution.py:30
  120.8 4.5 %collective-permute-start.11 = (f32[2,8,128]{2,1,0:T(8,128)S(1)}, f32[2,8,128]{2,1,0:T(8,128)S(1)}, u32[]{:S(2)}, u32[]{:S(2)}) collective-permute-start(f32[2,8,128]{2,1,0:T(8,128)S(1)} %broadcast_select_fusion), channel_id=1, source_target_pairs={{0,6},{2,0},{4,2},{6,4},{1,7},{3,1},{5,3},{7,5},{8,14},{10,8},{12,... | collective-permute-start | bytes 24584 | tf_op jit(solution)/shard_map/ppermute | solution.py:30
  125.3 9.7 %collective-permute-start.12 = (f32[3,2,8,128]{3,2,1,0:T(8,128)S(1)}, f32[3,2,8,128]{3,2,1,0:T(8,128)S(1)}, u32[]{:S(2)}, u32[]{:S(2)}) collective-permute-start(f32[3,2,8,128]{3,2,1,0:T(8,128)S(1)} %pad_maximum_fusion.1), channel_id=1, source_target_pairs={{0,8},{8,16},{16,24},{24,32},{32,40},{40,48},{48,56},{56,64},{64,7... | collective-permute-start | bytes 73736 | tf_op jit(solution)/shard_map/ppermute | solution.py:30
  125.3 9.7 %collective-permute-start.13 = (f32[3,2,8,128]{3,2,1,0:T(8,128)S(1)}, f32[3,2,8,128]{3,2,1,0:T(8,128)S(1)}, u32[]{:S(2)}, u32[]{:S(2)}) collective-permute-start(f32[3,2,8,128]{3,2,1,0:T(8,128)S(1)} %pad_maximum_fusion.1), channel_id=1, source_target_pairs={{0,120},{8,0},{16,8},{24,16},{32,24},{40,32},{48,40},{56,48},{64,5... | collective-permute-start | bytes 73736 | tf_op jit(solution)/shard_map/ppermute | solution.py:30
  138.1 0.9 copy-start.6
  138.1 1.1 copy-start.5
where the time goes:
time: 160 us; the launch traced here: 159 us
  Pallas kernels  87.2 us (54%)
  waiting for transfers between devices  35.7 us (22%)
  starting transfers between devices  30 us (19%)
  local copies, waits for them, and re-layouts  4.95 us (3%)
    pallas_call x2, Pallas kernels, run_steps(): pl.pallas_call(functools.partial(steps_kernel, upper), out_shape=out_shap...  41.4 us
    ppermute x13, waiting for transfers between devices, around(): lax.ppermute(value, axis, [(i, (i + steps) % count) for i in range(count)])  35.7 us
    ppermute x13, starting transfers between devices, around(): lax.ppermute(value, axis, [(i, (i + steps) % count) for i in range(count)])  28.7 us
    pallas_call x1, Pallas kernels, corners(): pl.pallas_call(corner_kernel, out_shape=[jax.ShapeDtypeStruct((106, 8, 12...  27.1 us
    pallas_call x2, Pallas kernels, pack(): pl.pallas_call(functools.partial(pack_kernel, ta, tb), out_shape=[jax.Sha...  13.4 us
    unnamed x28, local copies, waits for them, and re-layouts  3.39 us
  transfers between devices with their start and end apart: 14, of which 6 were waited for; matrix products, arithmetic and copies ran while one was open for 1% of the time, Pallas kernels for 20%

commit v1 on v0

--- a/solution.py
+++ b/solution.py
@@ -47,10 +47,7 @@
 
 
 def pack_kernel(ta, tb, el, mg, mat, *refs):
-    if ta:
-        own, up, down, strip, ext, matv, planes, strips, sems = refs
-    else:
-        strip_above, own, up, down, strip, ext, matv, planes, strips, sems = refs
+    own, up, down, strip, ext, matv, planes, strips, sems = refs
     tiles = tb - ta
     rows = pl.ds(64 * ta, 64 * tiles)
     loads = [(mat.at[rows], matv)]
@@ -58,8 +55,7 @@
         loads.append(((el, mg)[which].at[comp, rows], ext.at[c]))
     copy_all(loads, sems)
 
-    lane = lax.broadcasted_iota(jnp.int32, (8, 128), 1)
-    masks = [((lane - 16 * c + W + 128) % 128) < 2 * W for c in range(NC)]
+    masks = strip_masks()
 
     def row(r, _):
         for t in range(tiles):
@@ -89,15 +85,11 @@
         (planes.at[pl.ds(a, n)], down.at[pl.ds(b, n)])
         for a, b, n in ((0, 0, 17), (24, 17, 15), (48, 32, 5))
     ]
-    if ta:
-        pairs.append((strips, strip))
-    else:
-        pairs.append((strips, strip.at[:, pl.ds(0, 8 * tiles)]))
-        pairs.append((strip_above, strip.at[:, pl.ds(8 * tiles, 80 - 8 * tiles)]))
+    pairs.append((strips, strip))
     copy_all(pairs, sems)
 
 
-def pack(ta, tb, el, mg, mat, *strip_above):
+def pack(ta, tb, el, mg, mat):
     layers = 8 * (tb - ta)
     return pl.pallas_call(
         functools.partial(pack_kernel, ta, tb),
@@ -105,9 +97,9 @@
             jax.ShapeDtypeStruct((8 * NC, layers, 128), F32),
             jax.ShapeDtypeStruct((40, layers, 128), F32),
             jax.ShapeDtypeStruct((37, layers, 128), F32),
-            jax.ShapeDtypeStruct((8, layers if ta else 80, 128), F32),
+            jax.ShapeDtypeStruct((8, layers, 128), F32),
         ],
-        in_specs=[HBM] * (3 + len(strip_above)),
+        in_specs=[HBM] * 3,
         out_specs=[HBM] * 4,
         scratch_shapes=[
             pltpu.VMEM((6, 8 * layers, 128), F32),
@@ -119,69 +111,110 @@
         compiler_params=params(),
         cost_estimate=cost(3),
         name="pack_upper" if ta else "pack_lower",
-    )(el, mg, mat, *strip_above)
-
-
-def edge_kernel(from_low, from_high, own_u, own_l, strips, edge, sems):
+    )(el, mg, mat)
+
+
+def edge_kernel(el, mg, mat, edge, ext, matv, sems):
     gz = lax.axis_index("gz")
-    lane = lax.broadcasted_iota(jnp.int32, (8, 80, 128), 2)
-    strips[...] = jnp.where(lane % 16 < 8, from_high[...], from_low[...])
+
+    def load(first):
+        rows = pl.ds(64 * first, 64)
+        loads = [(mat.at[rows], matv)]
+        for c, (which, comp) in enumerate(SOURCE):
+            loads.append(((el, mg)[which].at[comp, rows], ext.at[c]))
+        copy_all(loads, sems)
 
     @pl.when(gz == 0)
     def _():
-        copy_all([(own_u.at[:, pl.ds(8 * (9 - CUT), 8)], edge.at[pl.ds(0, 56)])], sems)
-        edge[56:64] = strips[:, 72:80, :]
+        load(9)
 
     @pl.when(gz == 1)
     def _():
-        copy_all([(own_l.at[:, pl.ds(0, 8)], edge.at[pl.ds(0, 56)])], sems)
-        edge[56:64] = strips[:, 0:8, :]
-
-
-def edges(from_low, from_high, own_u, own_l):
+        load(0)
+
+    for r in range(8):
+        for c in range(6):
+            v = ext[c, pl.ds(r, 8, stride=8), :]
+            edge[24 * (c // 3) + 3 * r + c % 3] = v * 2.0 if c >= 3 else v
+        edge[48 + r] = matv[pl.ds(r, 8, stride=8), :].astype(F32)
+
+
+def edge_layers(el, mg, mat):
     return pl.pallas_call(
         edge_kernel,
-        out_shape=[
-            jax.ShapeDtypeStruct((8, 80, 128), F32),
-            jax.ShapeDtypeStruct((64, 8, 128), F32),
+        out_shape=jax.ShapeDtypeStruct((56, 8, 128), F32),
+        in_specs=[HBM] * 3,
+        out_specs=LOCAL,
+        scratch_shapes=[
+            pltpu.VMEM((6, 64, 128), F32),
+            pltpu.VMEM((64, 128), jnp.int32),
+            pltpu.SemaphoreType.DMA((7,)),
         ],
-        in_specs=[LOCAL, LOCAL, HBM, HBM],
-        out_specs=[LOCAL, LOCAL],
-        scratch_shapes=[pltpu.SemaphoreType.DMA((1,))],
         compiler_params=params(),
         cost_estimate=cost(1),
-        name="edges",
-    )(from_low, from_high, own_u, own_l)
-
-
-def corner_kernel(strips, edge, up, down, sems):
-    pairs = [
-        (edge.at[pl.ds(a, n)], up.at[pl.ds(b, n)])
-        for a, b, n in ((6, 0, 18), (30, 18, 2), (33, 20, 15), (51, 35, 5), (58, 100, 6))
-    ]
-    pairs += [
-        (edge.at[pl.ds(a, n)], down.at[pl.ds(b, n)])
-        for a, b, n in ((0, 0, 17), (24, 17, 15), (48, 32, 5), (56, 97, 6))
-    ]
-    pairs.append((strips.at[pl.ds(20, 60)], up.at[pl.ds(40, 60)]))
-    pairs.append((strips.at[pl.ds(0, 60)], down.at[pl.ds(37, 60)]))
-    copy_all(pairs, sems)
-
-
-def corners(strips, edge):
+        name="edge_layers",
+    )(el, mg, mat)
+
+
+def strip_masks():
+    lane = lax.broadcasted_iota(jnp.int32, (8, 128), 1)
+    return [((lane - 16 * c + W + 128) % 128) < 2 * W for c in range(NC)]
+
+
+def strip_kernel(strip_l, strip_u, edge, out):
+    masks = strip_masks()
+    for r in range(8):
+        for t in range(10):
+            at = 8 * t
+            out[11 * r + t] = (
+                strip_l[r, at : at + 8, :]
+                if t < CUT
+                else strip_u[r, at - 8 * CUT : at - 8 * CUT + 8, :]
+            )
+        total = edge[3 * r]
+        for c in range(1, NC):
+            v = edge[48 + r] if c == 6 else edge[24 * (c // 3) + 3 * r + c % 3]
+            total = jnp.where(masks[c], pltpu.roll(v, 16 * c, 1), total)
+        out[11 * r + 10] = total
+
+
+def own_strips(strip_l, strip_u, edge):
+    return pl.pallas_call(
+        strip_kernel,
+        out_shape=jax.ShapeDtypeStruct((88, 8, 128), F32),
+        in_specs=[LOCAL] * 3,
+        out_specs=LOCAL,
+        compiler_params=params(),
+        cost_estimate=cost(1),
+        name="own_strips",
+    )(strip_l, strip_u, edge)
+
+
+def corner_kernel(from_low, from_high, edge, strips, up, down):
+    lane = lax.broadcasted_iota(jnp.int32, (88, 8, 128), 2)
+    strips[...] = jnp.where(lane % 16 < 8, from_high[...], from_low[...])
+    for a, b, n in ((6, 0, 18), (30, 18, 2), (33, 20, 15), (51, 35, 5)):
+        up[b : b + n] = edge[a : a + n]
+    for a, b, n in ((0, 0, 17), (24, 17, 15), (48, 32, 5)):
+        down[b : b + n] = edge[a : a + n]
+    up[40:106] = strips[22:88]
+    down[37:103] = strips[0:66]
+
+
+def corners(from_low, from_high, edge):
     return pl.pallas_call(
         corner_kernel,
         out_shape=[
+            jax.ShapeDtypeStruct((88, 8, 128), F32),
             jax.ShapeDtypeStruct((106, 8, 128), F32),
             jax.ShapeDtypeStruct((103, 8, 128), F32),
         ],
-        in_specs=[HBM, HBM],
-        out_specs=[HBM, HBM],
-        scratch_shapes=[pltpu.SemaphoreType.DMA((11,))],
+        in_specs=[LOCAL] * 3,
+        out_specs=[LOCAL] * 3,
         compiler_params=params(),
         cost_estimate=cost(1),
         name="corners",
-    )(strips, edge)
+    )(from_low, from_high, edge)
 
 
 def steps_kernel(upper, decay, gain, strips, edge, low_c, high_c, *refs):
@@ -227,11 +260,11 @@
     zero = jnp.zeros((8, 128), F32)
     top = 8 + 8 * TILES
 
-    def unpack(ref, first, ref_z, first_z, count, row):
+    def unpack(ref, first, count, row):
         def body(r, _):
             at = BASE + row + r
-            for t, tile in held + [(halo, None)]:
-                v = ref_z[first_z + r] if tile is None else ref[first + 10 * r + tile]
+            for t, tile in held + [(halo, 10)]:
+                v = ref[first + 11 * r + tile]
                 z = 8 * t
                 for c in range(NC):
                     turned = pltpu.roll(v, 128 - 16 * c, 1) if c else v
@@ -245,9 +278,9 @@
 
         lax.fori_loop(0, count, body, 0)
 
-    unpack(low_c, 40, low_c, 100, W, 0)
-    unpack(strips, 0, edge, 56, 8, W)
-    unpack(high_c, 37, high_c, 97, W, W + 8)
+    unpack(low_c, 40, W, 0)
+    unpack(strips, 0, 8, W)
+    unpack(high_c, 37, W, W + 8)
 
     def ends(r, _):
         for pair in ms:
@@ -521,10 +554,6 @@
     )(weights, centre, before, after)
 
 
-def behind(value, *others):
-    return lax.optimization_barrier((value, *others))[0]
-
-
 def on_device(electric, magnetic, material, decay, gain, kernels):
     el = electric.reshape(3, 640, 128)
     mg = magnetic.reshape(3, 640, 128)
@@ -533,19 +562,23 @@
         kernels.transpose(0, 1, 3, 2).reshape(48, 15, 15), ((0, 0), (0, 0), (0, 1))
     ).reshape(48, 240)
 
+    edge = around(edge_layers(el, mg, mat), "gz", 1)
     own_u, up_u, down_u, strip_u = pack(CUT, 10, el, mg, mat)
     low_u, high_u = around(up_u, "gx", 1), around(down_u, "gx", -1)
-    own_l, up_l, down_l, strip = pack(0, CUT, el, mg, mat, strip_u)
-    strips, edge = edges(around(strip, "gy", 1), around(strip, "gy", -1), own_u, own_l)
-    strips = strips.reshape(80, 8, 128)
-    edge = around(edge, "gz", 1)
-    up_c, down_c = corners(strips, edge)
+    own_l, up_l, down_l, strip_l = pack(0, CUT, el, mg, mat)
+    strips = own_strips(strip_l, strip_u, edge)
+    from_low, from_high = around(strips, "gy", 1), around(strips, "gy", -1)
+    from_low, from_high, low_u, high_u = lax.optimization_barrier(
+        (from_low, from_high, low_u, high_u)
+    )
+    strips, up_c, down_c = corners(from_low, from_high, edge)
     low_c, high_c = around(up_c, "gx", 1), around(down_c, "gx", -1)
-    up_l, down_l = behind((up_l, down_l), up_c)
+    up_l, down_l, low_c, high_c = lax.optimization_barrier((up_l, down_l, low_c, high_c))
     low_l, high_l = around(up_l, "gx", 1), around(down_l, "gx", -1)
 
     sides = [strips, edge, low_c, high_c]
     field, plane = run_steps(True, decay, gain, sides, [own_u, low_u, high_u])
+    plane, low_l, high_l = lax.optimization_barrier((plane, low_l, high_l))
     top = lax.ppermute(plane, "gz", [(1, 0)])
     top = jnp.where(lax.axis_index("gz") == 1, plane, top)
     top = jnp.stack([top, around(top, "gy", 1), around(top, "gy", -1)])

time: 160 us -> 134 us (0.84)
  Pallas kernels: 87.2 us -> 57.7 us
  starting transfers between devices: 30 us -> 33.1 us
  local copies, waits for them, and re-layouts: 4.95 us -> 3.03 us
    pallas_call x2 -> x3, Pallas kernels: 30 us -> 6.2 us  [the longest x1 2.59 us: corners(): pl.pallas_call(corner_kernel, out_shape=[jax.ShapeDtypeStruct((88, 8, 128...]
    pallas_call x2, Pallas kernels: 13.4 us -> 7.62 us  [pack(): pl.pallas_call(functools.partial(pack_kernel, ta, tb), out_shape=[jax.Sha...]
    ppermute x1, starting transfers between devices: 1.29 us -> 3.82 us  [on_device(): top = lax.ppermute(plane, 'gz', [(1, 0)])]
    unnamed x28 -> x20, local copies, waits for them, and re-layouts: 3.39 us -> 1.45 us
  transfers between devices with their start and end apart: 14 -> 14, of which waited for: 6 -> 8; matrix products, arithmetic and copies ran while one was open for 1% -> 1% of each run, Pallas kernels for 20% -> 37%
where the time goes in v1:
time: 134 us; the launch traced here: 132 us
  Pallas kernels  57.7 us (43%)
  waiting for transfers between devices  36.7 us (27%)
  starting transfers between devices  33.1 us (25%)
  local copies, waits for them, and re-layouts  3.03 us (2%)
    pallas_call x2, Pallas kernels, run_steps(): pl.pallas_call(functools.partial(steps_kernel, upper), out_shape=out_shap...  41.5 us
    ppermute x13, waiting for transfers between devices, around(): lax.ppermute(value, axis, [(i, (i + steps) % count) for i in range(count)])  35.1 us
    ppermute x13, starting transfers between devices, around(): lax.ppermute(value, axis, [(i, (i + steps) % count) for i in range(count)])  29.2 us
    pallas_call x2, Pallas kernels, pack(): pl.pallas_call(functools.partial(pack_kernel, ta, tb), out_shape=[jax.Sha...  7.62 us
    ppermute x1, starting transfers between devices, on_device(): top = lax.ppermute(plane, 'gz', [(1, 0)])  3.82 us
  transfers between devices with their start and end apart: 14, of which 8 were waited for; matrix products, arithmetic and copies ran while one was open for 1% of the time, Pallas kernels for 37%

profile of v1, /device:TPU:2, one launch (start us, length us, event | category | flops | bytes accessed | tf_op | source)
XLA Modules:
  0.0 132.0 jit_solution(14333899824635956896)
XLA Ops:
  0.6 4.1 %pack_upper.1 = (f32[56,48,128]{2,1,0:T(8,128)}, f32[40,48,128]{2,1,0:T(8,128)}, f32[37,48,128]{2,1,0:T(8,128)}, f32[8,48,128]{2,1,0:T(8,128)}) custom-call(f32[3,640,128]{2,1,0:T(8,128)} %bitcast.17, f32[3,640,128]{2,1,0:T(8,128)} %bitcast.20, s32[640,128]{1,0:T(8,128)} %bitcast.23), custom_call_target="tpu_custom_call" | custom-call | bytes 9000000 | tf_op jit(solution)/shard_map/pack_upper/pallas_call | solution.py:94
  4.8 0.1 collective-permute-start.3
  4.8 5.3 %collective-permute-start.4 = (f32[37,48,128]{2,1,0:T(8,128)}, f32[37,48,128]{2,1,0:T(8,128)S(1)}, u32[]{:S(2)}, u32[]{:S(2)}) collective-permute-start(f32[37,48,128]{2,1,0:T(8,128)} %get-tuple-element.29), channel_id=1, source_target_pairs={{0,120},{8,0},{16,8},{24,16},{32,24},{40,32},{48,40},{56,48},{64,5... | collective-permute-start | bytes 2727944 | tf_op jit(solution)/shard_map/ppermute | solution.py:30
  10.2 1.7 %edge_layers.1 = f32[56,8,128]{2,1,0:T(8,128)} custom-call(f32[3,640,128]{2,1,0:T(8,128)} %bitcast.18, f32[3,640,128]{2,1,0:T(8,128)} %bitcast.21, s32[640,128]{1,0:T(8,128)} %bitcast.24), custom_call_target="tpu_custom_call" | custom-call | bytes 3000000 | tf_op jit(solution)/shard_map/edge_layers/pallas_call | solution.py:143
  11.9 1.3 collective-permute-start
  13.1 3.5 %pack_lower.1 = (f32[56,32,128]{2,1,0:T(8,128)}, f32[40,32,128]{2,1,0:T(8,128)}, f32[37,32,128]{2,1,0:T(8,128)}, f32[8,32,128]{2,1,0:T(8,128)}) custom-call(f32[3,640,128]{2,1,0:T(8,128)} %bitcast.19, f32[3,640,128]{2,1,0:T(8,128)} %bitcast.22, s32[640,128]{1,0:T(8,128)} %bitcast.25), custom_call_target="tpu_custom_call" | custom-call | bytes 9000000 | tf_op jit(solution)/shard_map/pack_lower/pallas_call | solution.py:94
  16.6 0.0 copy-start.8
  16.6 0.0 copy-start.9
  16.6 18.1 %collective-permute-done.edge = f32[56,8,128]{2,1,0:T(8,128)S(1)} collective-permute-done((f32[56,8,128]{2,1,0:T(8,128)}, f32[56,8,128]{2,1,0:T(8,128)S(1)}, u32[]{:S(2)}, u32[]{:S(2)}) %collective-permute-start) | collective-permute-done | bytes 229408 | tf_op jit(solution)/shard_map/ppermute | solution.py:30
  34.8 0.0 copy-start.1
  34.8 0.7 copy-done.1
  35.4 2.0 %own_strips.1 = f32[88,8,128]{2,1,0:T(8,128)} custom-call(f32[8,32,128]{2,1,0:T(8,128)} %get-tuple-element.26.strip_l, f32[8,48,128]{2,1,0:T(8,128)} %get-tuple-element.27.strip_u, f32[56,8,128]{2,1,0:T(8,128)} %copy-done.1), custom_call_target="tpu_custom_call" | custom-call | bytes 3000000 | tf_op jit(solution)/shard_map/own_strips/pallas_call | solution.py:182
  37.4 1.6 %collective-permute-start.1 = (f32[88,8,128]{2,1,0:T(8,128)}, f32[88,8,128]{2,1,0:T(8,128)S(1)}, u32[]{:S(2)}, u32[]{:S(2)}) collective-permute-start(f32[88,8,128]{2,1,0:T(8,128)} %own_strips.1), channel_id=1, source_target_pairs={{0,2},{2,4},{4,6},{6,0},{1,3},{3,5},{5,7},{7,1},{8,10},{10,12},{12... | collective-permute-start | bytes 1081352 | tf_op jit(solution)/shard_map/ppermute | solution.py:30
  39.0 1.7 %collective-permute-start.2 = (f32[88,8,128]{2,1,0:T(8,128)}, f32[88,8,128]{2,1,0:T(8,128)S(1)}, u32[]{:S(2)}, u32[]{:S(2)}) collective-permute-start(f32[88,8,128]{2,1,0:T(8,128)} %own_strips.1), channel_id=1, source_target_pairs={{0,6},{2,0},{4,2},{6,4},{1,7},{3,1},{5,3},{7,5},{8,14},{10,8},{12,... | collective-permute-start | bytes 1081352 | tf_op jit(solution)/shard_map/ppermute | solution.py:30
  40.6 5.6 %collective-permute-done.1.from_low = f32[88,8,128]{2,1,0:T(8,128)S(1)} collective-permute-done((f32[88,8,128]{2,1,0:T(8,128)}, f32[88,8,128]{2,1,0:T(8,128)S(1)}, u32[]{:S(2)}, u32[]{:S(2)}) %collective-permute-start.1) | collective-permute-done | bytes 360480 | tf_op jit(solution)/shard_map/ppermute | solution.py:30
  46.3 0.0 copy-start.5
  46.3 0.4 collective-permute-done.2.from_high
  46.6 0.0 copy-start.6
  46.6 0.0 collective-permute-done.4.refs_2_
  46.6 0.0 copy-start.2
  46.6 0.0 collective-permute-done.3.refs_1_
  46.6 0.4 copy-done.5
  47.0 0.4 copy-done.6
  47.4 0.0 copy-start
  47.4 2.6 %corners.1 = (f32[88,8,128]{2,1,0:T(8,128)}, f32[106,8,128]{2,1,0:T(8,128)}, f32[103,8,128]{2,1,0:T(8,128)}) custom-call(f32[88,8,128]{2,1,0:T(8,128)} %copy-done.5, f32[88,8,128]{2,1,0:T(8,128)} %copy-done.6, f32[56,8,128]{2,1,0:T(8,128)} %copy-done.1), custom_call_target="tpu_custom_call" | custom-call | bytes 3000000 | tf_op jit(solution)/shard_map/corners/pallas_call | solution.py:205
  50.0 0.0 collective-permute-start.5
  50.0 5.4 %collective-permute-start.6 = (f32[103,8,128]{2,1,0:T(8,128)}, f32[103,8,128]{2,1,0:T(8,128)S(1)}, u32[]{:S(2)}, u32[]{:S(2)}) collective-permute-start(f32[103,8,128]{2,1,0:T(8,128)} %get-tuple-element.36), channel_id=1, source_target_pairs={{0,120},{8,0},{16,8},{24,16},{32,24},{40,32},{48,40},{56,48},{64,5... | collective-permute-start | bytes 1265672 | tf_op jit(solution)/shard_map/ppermute | solution.py:30
  55.3 8.2 %collective-permute-done.6.high_c = f32[103,8,128]{2,1,0:T(8,128)S(1)} collective-permute-done((f32[103,8,128]{2,1,0:T(8,128)}, f32[103,8,128]{2,1,0:T(8,128)S(1)}, u32[]{:S(2)}, u32[]{:S(2)}) %collective-permute-start.6) | collective-permute-done | bytes 421920 | tf_op jit(solution)/shard_map/ppermute | solution.py:30
  63.5 0.0 copy-start.4
  63.5 0.9 collective-permute-done.5.low_c
  64.3 0.0 copy-start.3
  64.3 0.0 copy-done.8
  64.3 2.6 %collective-permute-start.7 = (f32[40,32,128]{2,1,0:T(8,128)S(1)}, f32[40,32,128]{2,1,0:T(8,128)}, u32[]{:S(2)}, u32[]{:S(2)}) collective-permute-start(f32[40,32,128]{2,1,0:T(8,128)S(1)} %copy-done.8), channel_id=1, source_target_pairs={{0,8},{8,16},{16,24},{24,32},{32,40},{40,48},{48,56},{56,64},{64,7... | collective-permute-start | bytes 1966088 | tf_op jit(solution)/shard_map/ppermute | solution.py:30
  66.9 0.0 copy-done.9
  66.9 2.8 %collective-permute-start.8 = (f32[37,32,128]{2,1,0:T(8,128)S(1)}, f32[37,32,128]{2,1,0:T(8,128)}, u32[]{:S(2)}, u32[]{:S(2)}) collective-permute-start(f32[37,32,128]{2,1,0:T(8,128)S(1)} %copy-done.9), channel_id=1, source_target_pairs={{0,120},{8,0},{16,8},{24,16},{32,24},{40,32},{48,40},{56,48},{64,5... | collective-permute-start | bytes 1818632 | tf_op jit(solution)/shard_map/ppermute | solution.py:30
  69.7 0.0 copy-done.2
  69.7 0.0 copy-done
  69.7 0.0 copy-done.4
  69.7 0.0 copy-done.3
  69.7 0.0 copy-start.7
  69.7 21.2 %steps_upper.1 = (f32[3,640,128]{2,1,0:T(8,128)}, f32[2,8,128]{2,1,0:T(8,128)}) custom-call(f32[5]{0:T(128)} %decay.3, f32[5]{0:T(128)} %gain.3, f32[88,8,128]{2,1,0:T(8,128)} %get-tuple-element.32.strips, f32[56,8,128]{2,1,0:T(8,128)} %copy-done.1, f32[106,8,128]{2,1,0:T(8,128)} %copy-done.3, f32[103,8,128]{2,1,0:T(8,128)} %copy-done.4, ...), custom_call_target="tpu_custom_call" | custom-call | bytes 45000000 | tf_op jit(solution)/shard_map/steps_upper/pallas_call | solution.py:473
  91.0 0.0 collective-permute-done.8.refs_5_
  91.0 0.0 collective-permute-done.7.refs_4_
  91.0 3.8 %collective-permute-start.9 = (f32[2,8,128]{2,1,0:T(8,128)}, f32[2,8,128]{2,1,0:T(8,128)S(1)}, u32[]{:S(2)}, u32[]{:S(2)}) collective-permute-start(f32[2,8,128]{2,1,0:T(8,128)} %get-tuple-element.49), channel_id=1, source_target_pairs={{1,0},{3,2},{5,4},{7,6},{9,8},{11,10},{13,12},{15,14},{17,16},{19,... | collective-permute-start | bytes 24584 | tf_op jit(solution)/shard_map/ppermute | solution.py:582
  94.8 1.6 %collective-permute-done.9 = f32[2,8,128]{2,1,0:T(8,128)S(1)} collective-permute-done((f32[2,8,128]{2,1,0:T(8,128)}, f32[2,8,128]{2,1,0:T(8,128)S(1)}, u32[]{:S(2)}, u32[]{:S(2)}) %collective-permute-start.9) | collective-permute-done | bytes 8224 | tf_op jit(solution)/shard_map/ppermute | solution.py:582
  96.4 0.7 broadcast_select_fusion
  97.1 1.6 %collective-permute-start.10 = (f32[2,8,128]{2,1,0:T(8,128)S(1)}, f32[2,8,128]{2,1,0:T(8,128)S(1)}, u32[]{:S(2)}, u32[]{:S(2)}) collective-permute-start(f32[2,8,128]{2,1,0:T(8,128)S(1)} %broadcast_select_fusion), channel_id=1, source_target_pairs={{0,2},{2,4},{4,6},{6,0},{1,3},{3,5},{5,7},{7,1},{8,10},{10,12},{12... | collective-permute-start | bytes 24584 | tf_op jit(solution)/shard_map/ppermute | solution.py:30
  98.7 1.7 %collective-permute-start.11 = (f32[2,8,128]{2,1,0:T(8,128)S(1)}, f32[2,8,128]{2,1,0:T(8,128)S(1)}, u32[]{:S(2)}, u32[]{:S(2)}) collective-permute-start(f32[2,8,128]{2,1,0:T(8,128)S(1)} %broadcast_select_fusion), channel_id=1, source_target_pairs={{0,6},{2,0},{4,2},{6,4},{1,7},{3,1},{5,3},{7,5},{8,14},{10,8},{12,... | collective-permute-start | bytes 24584 | tf_op jit(solution)/shard_map/ppermute | solution.py:30
  100.3 1.6 %collective-permute-done.10 = f32[2,8,128]{2,1,0:T(8,128)S(1)} collective-permute-done((f32[2,8,128]{2,1,0:T(8,128)S(1)}, f32[2,8,128]{2,1,0:T(8,128)S(1)}, u32[]{:S(2)}, u32[]{:S(2)}) %collective-permute-start.10) | collective-permute-done | bytes 8224 | tf_op jit(solution)/shard_map/ppermute | solution.py:30
  102.0 0.4 collective-permute-done.11
  102.3 0.0 collective-permute-start.12
  102.3 5.4 %collective-permute-start.13 = (f32[3,2,8,128]{3,2,1,0:T(8,128)S(1)}, f32[3,2,8,128]{3,2,1,0:T(8,128)S(1)}, u32[]{:S(2)}, u32[]{:S(2)}) collective-permute-start(f32[3,2,8,128]{3,2,1,0:T(8,128)S(1)} %pad_maximum_fusion.1), channel_id=1, source_target_pairs={{0,120},{8,0},{16,8},{24,16},{32,24},{40,32},{48,40},{56,48},{64,5... | collective-permute-start | bytes 73736 | tf_op jit(solution)/shard_map/ppermute | solution.py:30
  107.7 0.0 copy-done.7
  107.7 0.2 reshape.26
  107.9 0.7 copy.11.weights
  108.6 20.3 %steps_lower.1 = f32[3,640,128]{2,1,0:T(8,128)} custom-call(f32[5]{0:T(128)} %decay.3, f32[5]{0:T(128)} %gain.3, f32[88,8,128]{2,1,0:T(8,128)} %get-tuple-element.32.strips, f32[56,8,128]{2,1,0:T(8,128)} %copy-done.1, f32[106,8,128]{2,1,0:T(8,128)} %copy-done.3, f32[103,8,128]{2,1,0:T(8,128)} %copy-done.4, ...), custom_call_target="tpu_custom_call", output_to_operand_aliasing={{}: (12, {})} | custom-call | bytes 45000000 | tf_op jit(solution)/shard_map/steps_lower/pallas_call | solution.py:473
  128.9 0.0 collective-permute-done.12
  129.0 0.0 collective-permute-done.13
  129.0 0.6 slice_bitcast_fusion
  129.6 2.4 %image.1 = f32[4,128]{1,0:T(4,128)} custom-call(f32[48,240]{1,0:T(8,128)} %copy.11.weights, f32[2,24,128]{2,1,0:T(8,128)} %get-tuple-element.52.centre, f32[2,24,128]{2,1,0:T(8,128)} %get-tuple-element.51.before, f32[2,24,128]{2,1,0:T(8,128)} %get-tuple-element.50.after), custom_call_target="tpu_custom_call" | custom-call | tf_op jit(solution)/shard_map/image/pallas_call | solution.py:543
  (4 shorter events, 0.1 us)
Async XLA Ops:
  4.8 41.9 %collective-permute-start.3 = (f32[40,48,128]{2,1,0:T(8,128)}, f32[40,48,128]{2,1,0:T(8,128)S(1)}, u32[]{:S(2)}, u32[]{:S(2)}) collective-permute-start(f32[40,48,128]{2,1,0:T(8,128)} %get-tuple-element.28), channel_id=1, source_target_pairs={{0,8},{8,16},{16,24},{24,32},{32,40},{40,48},{48,56},{56,64},{64,7... | collective-permute-start | bytes 2949128 | tf_op jit(solution)/shard_map/ppermute | solution.py:30
  4.8 41.8 %collective-permute-start.4 = (f32[37,48,128]{2,1,0:T(8,128)}, f32[37,48,128]{2,1,0:T(8,128)S(1)}, u32[]{:S(2)}, u32[]{:S(2)}) collective-permute-start(f32[37,48,128]{2,1,0:T(8,128)} %get-tuple-element.29), channel_id=1, source_target_pairs={{0,120},{8,0},{16,8},{24,16},{32,24},{40,32},{48,40},{56,48},{64,5... | collective-permute-start | bytes 2727944 | tf_op jit(solution)/shard_map/ppermute | solution.py:30
  11.9 22.9 %collective-permute-start = (f32[56,8,128]{2,1,0:T(8,128)}, f32[56,8,128]{2,1,0:T(8,128)S(1)}, u32[]{:S(2)}, u32[]{:S(2)}) collective-permute-start(f32[56,8,128]{2,1,0:T(8,128)} %edge_layers.1), channel_id=1, source_target_pairs={{0,1},{1,0},{2,3},{3,2},{4,5},{5,4},{6,7},{7,6},{8,9},{9,8},{10,11... | collective-permute-start | bytes 688136 | tf_op jit(solution)/shard_map/ppermute | solution.py:30
  16.6 47.7 %copy-start.8 = (f32[40,32,128]{2,1,0:T(8,128)S(1)}, f32[40,32,128]{2,1,0:T(8,128)}, u32[]{:S(2)}) copy-start(f32[40,32,128]{2,1,0:T(8,128)} %get-tuple-element.44) | copy-start | bytes 1966084
  16.6 50.3 %copy-start.9 = (f32[37,32,128]{2,1,0:T(8,128)S(1)}, f32[37,32,128]{2,1,0:T(8,128)}, u32[]{:S(2)}) copy-start(f32[37,32,128]{2,1,0:T(8,128)} %get-tuple-element.45) | copy-start | bytes 1818628
  34.8 0.7 copy-start.1
  37.4 8.8 %collective-permute-start.1 = (f32[88,8,128]{2,1,0:T(8,128)}, f32[88,8,128]{2,1,0:T(8,128)S(1)}, u32[]{:S(2)}, u32[]{:S(2)}) collective-permute-start(f32[88,8,128]{2,1,0:T(8,128)} %own_strips.1), channel_id=1, source_target_pairs={{0,2},{2,4},{4,6},{6,0},{1,3},{3,5},{5,7},{7,1},{8,10},{10,12},{12... | collective-permute-start | bytes 1081352 | tf_op jit(solution)/shard_map/ppermute | solution.py:30
  39.0 7.6 %collective-permute-start.2 = (f32[88,8,128]{2,1,0:T(8,128)}, f32[88,8,128]{2,1,0:T(8,128)S(1)}, u32[]{:S(2)}, u32[]{:S(2)}) collective-permute-start(f32[88,8,128]{2,1,0:T(8,128)} %own_strips.1), channel_id=1, source_target_pairs={{0,6},{2,0},{4,2},{6,4},{1,7},{3,1},{5,3},{7,5},{8,14},{10,8},{12,... | collective-permute-start | bytes 1081352 | tf_op jit(solution)/shard_map/ppermute | solution.py:30
  46.3 0.7 copy-start.5
  46.6 0.7 copy-start.6
  46.6 23.1 %copy-start.2 = (f32[37,48,128]{2,1,0:T(8,128)}, f32[37,48,128]{2,1,0:T(8,128)S(1)}, u32[]{:S(2)}) copy-start(f32[37,48,128]{2,1,0:T(8,128)S(1)} %collective-permute-done.4.refs_2_) | copy-start | bytes 2727940
  47.4 22.3 %copy-start = (f32[40,48,128]{2,1,0:T(8,128)}, f32[40,48,128]{2,1,0:T(8,128)S(1)}, u32[]{:S(2)}) copy-start(f32[40,48,128]{2,1,0:T(8,128)S(1)} %collective-permute-done.3.refs_1_) | copy-start | bytes 2949124
  50.0 14.4 %collective-permute-start.5 = (f32[106,8,128]{2,1,0:T(8,128)}, f32[106,8,128]{2,1,0:T(8,128)S(1)}, u32[]{:S(2)}, u32[]{:S(2)}) collective-permute-start(f32[106,8,128]{2,1,0:T(8,128)} %get-tuple-element.35), channel_id=1, source_target_pairs={{0,8},{8,16},{16,24},{24,32},{32,40},{40,48},{48,56},{56,64},{64,7... | collective-permute-start | bytes 1302536 | tf_op jit(solution)/shard_map/ppermute | solution.py:30
  50.0 13.5 %collective-permute-start.6 = (f32[103,8,128]{2,1,0:T(8,128)}, f32[103,8,128]{2,1,0:T(8,128)S(1)}, u32[]{:S(2)}, u32[]{:S(2)}) collective-permute-start(f32[103,8,128]{2,1,0:T(8,128)} %get-tuple-element.36), channel_id=1, source_target_pairs={{0,120},{8,0},{16,8},{24,16},{32,24},{40,32},{48,40},{56,48},{64,5... | collective-permute-start | bytes 1265672 | tf_op jit(solution)/shard_map/ppermute | solution.py:30
  63.5 6.2 %copy-start.4 = (f32[103,8,128]{2,1,0:T(8,128)}, f32[103,8,128]{2,1,0:T(8,128)S(1)}, u32[]{:S(2)}) copy-start(f32[103,8,128]{2,1,0:T(8,128)S(1)} %collective-permute-done.6.high_c) | copy-start | bytes 1265668
  64.3 5.4 %copy-start.3 = (f32[106,8,128]{2,1,0:T(8,128)}, f32[106,8,128]{2,1,0:T(8,128)S(1)}, u32[]{:S(2)}) copy-start(f32[106,8,128]{2,1,0:T(8,128)S(1)} %collective-permute-done.5.low_c) | copy-start | bytes 1302532
  64.3 26.7 %collective-permute-start.7 = (f32[40,32,128]{2,1,0:T(8,128)S(1)}, f32[40,32,128]{2,1,0:T(8,128)}, u32[]{:S(2)}, u32[]{:S(2)}) collective-permute-start(f32[40,32,128]{2,1,0:T(8,128)S(1)} %copy-done.8), channel_id=1, source_target_pairs={{0,8},{8,16},{16,24},{24,32},{32,40},{40,48},{48,56},{56,64},{64,7... | collective-permute-start | bytes 1966088 | tf_op jit(solution)/shard_map/ppermute | solution.py:30
  66.9 24.0 %collective-permute-start.8 = (f32[37,32,128]{2,1,0:T(8,128)S(1)}, f32[37,32,128]{2,1,0:T(8,128)}, u32[]{:S(2)}, u32[]{:S(2)}) collective-permute-start(f32[37,32,128]{2,1,0:T(8,128)S(1)} %copy-done.9), channel_id=1, source_target_pairs={{0,120},{8,0},{16,8},{24,16},{32,24},{40,32},{48,40},{56,48},{64,5... | collective-permute-start | bytes 1818632 | tf_op jit(solution)/shard_map/ppermute | solution.py:30
  69.7 38.0 %copy-start.7 = (f32[2,24,15,15]{1,0,3,2:T(2,128)S(1)}, f32[2,24,15,15]{1,0,3,2:T(2,128)}, u32[]{:S(2)}) copy-start(f32[2,24,15,15]{1,0,3,2:T(2,128)} %param.11) | copy-start | bytes 129604
  91.0 5.4 %collective-permute-start.9 = (f32[2,8,128]{2,1,0:T(8,128)}, f32[2,8,128]{2,1,0:T(8,128)S(1)}, u32[]{:S(2)}, u32[]{:S(2)}) collective-permute-start(f32[2,8,128]{2,1,0:T(8,128)} %get-tuple-element.49), channel_id=1, source_target_pairs={{1,0},{3,2},{5,4},{7,6},{9,8},{11,10},{13,12},{15,14},{17,16},{19,... | collective-permute-start | bytes 24584 | tf_op jit(solution)/shard_map/ppermute | solution.py:582
  97.1 4.9 %collective-permute-start.10 = (f32[2,8,128]{2,1,0:T(8,128)S(1)}, f32[2,8,128]{2,1,0:T(8,128)S(1)}, u32[]{:S(2)}, u32[]{:S(2)}) collective-permute-start(f32[2,8,128]{2,1,0:T(8,128)S(1)} %broadcast_select_fusion), channel_id=1, source_target_pairs={{0,2},{2,4},{4,6},{6,0},{1,3},{3,5},{5,7},{7,1},{8,10},{10,12},{12... | collective-permute-start | bytes 24584 | tf_op jit(solution)/shard_map/ppermute | solution.py:30
  98.7 3.7 %collective-permute-start.11 = (f32[2,8,128]{2,1,0:T(8,128)S(1)}, f32[2,8,128]{2,1,0:T(8,128)S(1)}, u32[]{:S(2)}, u32[]{:S(2)}) collective-permute-start(f32[2,8,128]{2,1,0:T(8,128)S(1)} %broadcast_select_fusion), channel_id=1, source_target_pairs={{0,6},{2,0},{4,2},{6,4},{1,7},{3,1},{5,3},{7,5},{8,14},{10,8},{12,... | collective-permute-start | bytes 24584 | tf_op jit(solution)/shard_map/ppermute | solution.py:30
  102.3 26.6 %collective-permute-start.12 = (f32[3,2,8,128]{3,2,1,0:T(8,128)S(1)}, f32[3,2,8,128]{3,2,1,0:T(8,128)S(1)}, u32[]{:S(2)}, u32[]{:S(2)}) collective-permute-start(f32[3,2,8,128]{3,2,1,0:T(8,128)S(1)} %pad_maximum_fusion.1), channel_id=1, source_target_pairs={{0,8},{8,16},{16,24},{24,32},{32,40},{40,48},{48,56},{56,64},{64,7... | collective-permute-start | bytes 73736 | tf_op jit(solution)/shard_map/ppermute | solution.py:30
  102.3 26.6 %collective-permute-start.13 = (f32[3,2,8,128]{3,2,1,0:T(8,128)S(1)}, f32[3,2,8,128]{3,2,1,0:T(8,128)S(1)}, u32[]{:S(2)}, u32[]{:S(2)}) collective-permute-start(f32[3,2,8,128]{3,2,1,0:T(8,128)S(1)} %pad_maximum_fusion.1), channel_id=1, source_target_pairs={{0,120},{8,0},{16,8},{24,16},{32,24},{40,32},{48,40},{56,48},{64,5... | collective-permute-start | bytes 73736 | tf_op jit(solution)/shard_map/ppermute | solution.py:30

commit v2 on v0

v2 whole, which is shorter than its diff:
```python
import functools

import jax
import jax.numpy as jnp
from jax import lax
from jax.experimental import pallas as pl
from jax.experimental.pallas import tpu as pltpu
from jax.sharding import PartitionSpec as P

STEPS = 6
W = STEPS
Y, Z, X = range(3)
NC = 7
SOURCE = ((0, 1), (0, 2), (0, 0), (1, 1), (1, 2), (1, 0))
ROWS = 8 + 2 * W
BASE = 4
HELD = BASE + ROWS + 2
CUT = 6
LAG = 4
VMEM = 56 * 1024 * 1024
F32 = jnp.float32
HBM = pl.BlockSpec(memory_space=pl.ANY)
LOCAL = pl.BlockSpec(memory_space=pltpu.VMEM)


def around(value, axis, steps):
    count = lax.axis_size(axis)
    return lax.ppermute(value, axis, [(i, (i + steps) % count) for i in range(count)])


def beyond(value, steps):
    ny, nz = lax.axis_size("gy"), lax.axis_size("gz")
    pairs = [
        (y * nz + z, (y + steps) % ny * nz + (z + 1) % nz) for y in range(ny) for z in range(nz)
    ]
    return lax.ppermute(value, ("gy", "gz"), pairs)


def copy_all(pairs, sems):
    copies = [pltpu.make_async_copy(a, b, sems.at[i]) for i, (a, b) in enumerate(pairs)]
    for copy in copies:
        copy.start()
    for copy in copies:
        copy.wait()


def params():
    return pltpu.CompilerParams(vmem_limit_bytes=VMEM)


def cost(us):
    return pl.CostEstimate(flops=0, bytes_accessed=int(us * 3e6), transcendentals=0)


def plane_of(r, c):
    return 48 + r if c == 6 else 24 * (c // 3) + 3 * r + c % 3


def strip_masks():
    lane = lax.broadcasted_iota(jnp.int32, (8, 128), 1)
    return [((lane - 16 * c + W + 128) % 128) < 2 * W for c in range(NC)]


def strip_kernel(el, mg, mat, strips, edge, edge_strips, ext, matv, sems):
    gz = lax.axis_index("gz")
    loads = [(mat, matv)]
    for c, (which, comp) in enumerate(SOURCE):
        loads.append(((el, mg)[which].at[comp], ext.at[c]))
    copy_all(loads, sems)
    masks = strip_masks()

    def layers(c, t, r):
        rows = pl.ds(64 * t + r, 8, stride=8)
        if c == 6:
            return matv[rows, :].astype(F32)
        v = ext[c, rows, :]
        return v * 2.0 if c >= 3 else v

    def row(r, _):
        for t in range(10):
            total = layers(0, t, r)
            for c in range(1, NC):
                total = jnp.where(masks[c], pltpu.roll(layers(c, t, r), 16 * c, 1), total)
            strips[r, 8 * t : 8 * t + 8, :] = total
        return 0

    lax.fori_loop(0, 8, row, 0)

    def edges(t):
        for r in range(8):
            for c in range(NC):
                edge[plane_of(r, c)] = layers(c, t, r)
        edge_strips[...] = strips[:, 8 * t : 8 * t + 8, :]

    @pl.when(gz == 0)
    def _():
        edges(9)

    @pl.when(gz == 1)
    def _():
        edges(0)


def own_strips(el, mg, mat):
    return pl.pallas_call(
        strip_kernel,
        out_shape=[
            jax.ShapeDtypeStruct((8, 80, 128), F32),
            jax.ShapeDtypeStruct((8 * NC, 8, 128), F32),
            jax.ShapeDtypeStruct((8, 8, 128), F32),
        ],
        in_specs=[HBM] * 3,
        out_specs=[LOCAL] * 3,
        scratch_shapes=[
            pltpu.VMEM((6, 640, 128), F32),
            pltpu.VMEM((640, 128), jnp.int32),
            pltpu.SemaphoreType.DMA((7,)),
        ],
        compiler_params=params(),
        cost_estimate=cost(3),
        name="own_strips",
    )(el, mg, mat)


def pack_kernel(el, mg, mat, own_u, up_u, down_u, own_l, up_l, down_l, ext, matv, planes, sems):
    loads = [(mat, matv)]
    for c, (which, comp) in enumerate(SOURCE):
        loads.append(((el, mg)[which].at[comp], ext.at[c]))
    copy_all(loads, sems)

    def rows_of(first, last):
        def row(r, _):
            for t in range(first, last):
                rows = pl.ds(64 * t + r, 8, stride=8)
                for c in range(NC):
                    if c == 6:
                        v = matv[rows, :].astype(F32)
                    else:
                        v = ext[c, rows, :]
                        if c >= 3:
                            v = v * 2.0
                    planes[plane_of(r, c), 8 * t : 8 * t + 8, :] = v
            return 0

        lax.fori_loop(0, 8, row, 0)

    def sends(first, last, own, up, down):
        z, to = pl.ds(8 * first, 8 * (last - first)), pl.ds(0, 8 * (last - first))
        pairs = [(planes.at[:, z], own)]
        for a, b, n in ((6, 0, 18), (30, 18, 2), (33, 20, 15), (51, 35, 5)):
            pairs.append((planes.at[pl.ds(a, n), z], up.at[pl.ds(b, n), to]))
        for a, b, n in ((0, 0, 17), (24, 17, 15), (48, 32, 5)):
            pairs.append((planes.at[pl.ds(a, n), z], down.at[pl.ds(b, n), to]))
        return pairs

    rows_of(CUT, 10)
    pairs = sends(CUT, 10, own_u, up_u, down_u)
    upper = [pltpu.make_async_copy(a, b, sems.at[i]) for i, (a, b) in enumerate(pairs)]
    for copy in upper:
        copy.start()
    rows_of(0, CUT)
    pairs = sends(0, CUT, own_l, up_l, down_l)
    lower = [pltpu.make_async_copy(a, b, sems.at[8 + i]) for i, (a, b) in enumerate(pairs)]
    for copy in lower:
        copy.start()
    for copy in upper + lower:
        copy.wait()


def pack(el, mg, mat):
    shapes = []
    for layers, more in ((8 * (10 - CUT), 8), (8 * CUT, 0)):
        shapes += [
            jax.ShapeDtypeStruct((8 * NC, layers, 128), F32),
            jax.ShapeDtypeStruct((40 + W, layers + more, 128), F32),
            jax.ShapeDtypeStruct((37 + W, layers + more, 128), F32),
        ]
    return pl.pallas_call(
        pack_kernel,
        out_shape=shapes,
        in_specs=[HBM] * 3,
        out_specs=[HBM] * 6,
        scratch_shapes=[
            pltpu.VMEM((6, 640, 128), F32),
            pltpu.VMEM((640, 128), jnp.int32),
            pltpu.VMEM((8 * NC, 80, 128), F32),
            pltpu.SemaphoreType.DMA((16,)),
        ],
        compiler_params=params(),
        cost_estimate=cost(5),
        name="pack",
    )(el, mg, mat)


def fill_kernel(from_low, from_high, edge_low, edge_high, edge, *refs):
    strips, up_u, down_u, up_l, down_l, halo, sems = refs[4:]
    lane = lax.broadcasted_iota(jnp.int32, (8, 80, 128), 2)
    halo[:, 0:80, :] = jnp.where(lane % 16 < 8, from_high[...], from_low[...])
    lane = lax.broadcasted_iota(jnp.int32, (8, 8, 128), 2)
    halo[:, 80:88, :] = jnp.where(lane % 16 < 8, edge_high[...], edge_low[...])
    nu, nl = 8 * (10 - CUT), 8 * CUT
    pairs = [(halo, strips)]
    for message, first, count, parts in (
        (up_u, 8 - W, 40, ((6, 0, 18), (30, 18, 2), (33, 20, 15), (51, 35, 5))),
        (down_u, 0, 37, ((0, 0, 17), (24, 17, 15), (48, 32, 5))),
    ):
        rows = pl.ds(first, W)
        pairs.append(
            (halo.at[rows, pl.ds(nl, nu + 8)], message.at[pl.ds(count, W), pl.ds(0, nu + 8)])
        )
        for a, b, n in parts:
            pairs.append((edge.at[pl.ds(a, n)], message.at[pl.ds(b, n), pl.ds(nu, 8)]))
    for message, first, count in ((up_l, 8 - W, 40), (down_l, 0, 37)):
        pairs.append((halo.at[pl.ds(first, W), pl.ds(0, nl)], message.at[pl.ds(count, W)]))
    copy_all(pairs, sems)


def fill(from_low, from_high, edge_low, edge_high, edge, messages):
    shapes = [jax.ShapeDtypeStruct((8, 88, 128), F32)]
    shapes += [jax.ShapeDtypeStruct(m.shape, F32) for m in messages]
    return pl.pallas_call(
        fill_kernel,
        out_shape=shapes,
        in_specs=[LOCAL] * 5 + [HBM] * 4,
        out_specs=[HBM] * 5,
        scratch_shapes=[pltpu.VMEM((8, 88, 128), F32), pltpu.SemaphoreType.DMA((12,))],
        input_output_aliases={5 + i: 1 + i for i in range(4)},
        compiler_params=params(),
        cost_estimate=cost(1),
        name="fill",
    )(from_low, from_high, edge_low, edge_high, edge, *messages)


def steps_kernel(upper, decay, gain, strips, edge, *refs):
    gz = lax.axis_index("gz")
    nu, nl = 8 * (10 - CUT), 8 * CUT
    own_u, low_u, high_u = refs[:3]
    if upper:
        out, plane, *scratch = refs[3:]
        tiles, halo, counts = 11 - CUT, 10 - CUT, gz == 0
        sets = [((own_u, low_u, high_u), 0, nu, 0, nl)]
    else:
        own_l, low_l, high_l, _, out, *scratch = refs[3:]
        tiles, halo, counts = CUT + 3, 0, gz == 1
        sets = [
            ((own_l, low_l, high_l), 0, nl, 8, 0),
            ((own_u, low_u, high_u), 0, 16, 8 + nl, nl),
        ]
    on = 9 - CUT if upper else CUT + 1
    sets.append(((edge, low_u, high_u), nu, 8, 8 * halo, 80))
    ea0, ea1, eb0, eb1, ma0, ma1, mb0, mb1, d0, d1, g0, g1, ya, yb, ym, sv, stage, sems = scratch
    es, ms, yes = ((ea0, ea1), (eb0, eb1)), ((ma0, ma1), (mb0, mb1)), (ya, yb)
    ds_, gs = (d0, d1), (g0, g1)

    first, mid, last_ = BASE, BASE + W, BASE + W + 8
    groups = []
    for (own, low, high), start, layers, to, strip in sets:
        src, zf, zd = pl.ds(start, layers), pl.ds(8 + to, layers), pl.ds(to, layers)
        mine = pl.ds(0, 8) if own is edge else src
        moves = [
            (strips.at[:, pl.ds(strip, layers)], sv.at[pl.ds(W, 8), zd]),
            (low.at[pl.ds(40, W), src], sv.at[pl.ds(0, W), zd]),
            (high.at[pl.ds(37, W), src], sv.at[pl.ds(W + 8, W), zd]),
        ]
        for ref, a, n, dst, b, z in (
            (own, 0, 24, ea0, 3 * mid, zf),
            (own, 24, 24, ma0, 3 * mid, zf),
            (own, 48, 8, d0, mid, zd),
            (low, 0, 18, ea0, 3 * first, zf),
            (low, 18, 2, ma0, 3 * first, zf),
            (low, 20, 15, ma0, 3 * first + 3, zf),
            (low, 35, 5, d0, first + 1, zd),
            (high, 0, 17, ea0, 3 * last_, zf),
            (high, 17, 15, ma0, 3 * last_, zf),
            (high, 32, 5, d0, last_, zd),
        ):
            moves.append((ref.at[pl.ds(a, n), mine if ref is own else src], dst.at[pl.ds(b, n), z]))
        groups.append(moves)
    copies = []
    for moves in groups:
        for a, b in moves:
            copies.append(pltpu.make_async_copy(a, b, sems.at[len(copies)]))
    for copy in copies:
        copy.start()

    zero = jnp.zeros((8, 128), F32)
    top = 8 + 8 * tiles

    def ends(r, _):
        for pair in ms:
            for m in pair:
                m[3 * r + X, 0:8, :] = zero
                m[3 * r + Y, 0:8, :] = zero
        for pair in es:
            for e in pair:
                e[3 * r + X, top : top + 8, :] = zero
                e[3 * r + Y, top : top + 8, :] = zero
        return 0

    lax.fori_loop(0, HELD, ends, 0)
    for copy in copies:
        copy.wait()

    def unpack(r, _):
        at = BASE + r
        for t in range(tiles):
            z = 8 * t
            v = sv[r, z : z + 8, :]
            for c in range(NC):
                turned = pltpu.roll(v, 128 - 16 * c, 1) if c else v
                if c < 3:
                    ea1[3 * at + c, 8 + z : 16 + z, :] = turned
                elif c < 6:
                    ma1[3 * at + c - 3, 8 + z : 16 + z, :] = turned
                else:
                    d1[at, z : z + 8, :] = turned
        return 0

    lax.fori_loop(0, ROWS, unpack, 0)
    hz = 8 * halo

    @pl.when(jnp.logical_not(counts))
    def _():
        def clear(i, _):
            for ref in (ea0, ea1, ma0, ma1):
                ref[3 * BASE + i, hz + 8 : hz + 16, :] = zero
            return 0

        lax.fori_loop(0, 3 * ROWS, clear, 0)

    live = jnp.where(counts, 1.0, 0.0).astype(F32)

    def tables(r, _):
        for t in range(tiles):
            z = 8 * t
            for d, g in zip(ds_, gs):
                ids = d[r, z : z + 8, :]
                d_cells, g_cells = zero, zero
                for i in range(5):
                    hit = ids == float(i)
                    d_cells = jnp.where(hit, decay[i], d_cells)
                    g_cells = jnp.where(hit, gain[i] * 0.5, g_cells)
                if t == halo:
                    d_cells, g_cells = d_cells * live, g_cells * live
                d[r, z : z + 8, :] = d_cells
                g[r, z : z + 8, :] = g_cells
        return 0

    lax.fori_loop(BASE + 1, BASE + ROWS - 1, tables, 0)

    lane = lax.broadcasted_iota(jnp.int32, (8, 128), 1)
    last, first_lane = lane == 127, lane == 0
    units = [(row, t) for row in range(2) for t in range(tiles)]

    def first_turn(i, _):
        kept = []
        for row, t in units:
            r = BASE + 2 * i + row
            for j, c in enumerate((X, Z)):
                pair = [pltpu.roll(e[3 * r + c, 8 + 8 * t : 16 + 8 * t, :], 127, 1) for e in es[0]]
                kept.append((4 * r + 2 * j, 8 * t, pair))
        for i, z, (a, b) in kept:
            ya[i, z : z + 8, :] = jnp.where(last, b, a)
            ya[i + 1, z : z + 8, :] = jnp.where(last, a, b)
        return 0

    lax.fori_loop(0, ROWS // 2, first_turn, 0)

    def block(old, with_e, with_m, m, start):
        new = 1 - old
        base = start + 2 * m
        b3, b4 = 3 * base, 4 * base
        waiting = []

        def keep():
            for y, b, i, z, (a, c), edge_lane in waiting.pop(0):
                y[b + i, z : z + 8, :] = jnp.where(edge_lane, c, a)
                y[b + (i + 1), z : z + 8, :] = jnp.where(edge_lane, a, c)

        for row, t in units if with_e else ():
            e, z = row - 2, 8 * t
            turned = [[], []]
            for k in range(2):

                def magnetic(c, r=e, shift=0):
                    return ms[new][k][b3 + (3 * r + c), 8 + z + shift : 16 + z + shift, :]

                def electric(c):
                    return es[old][k][b3 + (3 * e + c), 8 + z : 16 + z, :]

                mx_y = ym[4 * row + k, z : z + 8, :]
                mz_y = ym[4 * row + 2 + k, z : z + 8, :]
                mx, my, mz = magnetic(X), magnetic(Y), magnetic(Z)
                d = ds_[k][base + e, z : z + 8, :]
                g = gs[k][base + e, z : z + 8, :]
                ex = d * electric(X) + g * ((mz - mz_y) - (my - magnetic(Y, e, -1)))
                ey = d * electric(Y) + g * ((mx - magnetic(X, e, -1)) - (mz - magnetic(Z, e - 1)))
                ez = d * electric(Z) + g * ((my - magnetic(Y, e - 1)) - (mx - mx_y))
                for c, v in ((X, ex), (Y, ey), (Z, ez)):
                    es[new][k][b3 + (3 * e + c), 8 + z : 16 + z, :] = v
                turned[0].append(pltpu.roll(ex, 127, 1))
                turned[1].append(pltpu.roll(ez, 127, 1))
            waiting.append(
                [(yes[new], b4, 4 * e + 2 * j, z, turned[j], last) for j in range(2)]
            )
            if len(waiting) > LAG:
                keep()
        for row, t in units if with_m else ():
            z = 8 * t
            turned = [[], []]
            for k in range(2):

                def electric(c, r=row, shift=0):
                    return es[old][k][b3 + (3 * r + c), 8 + z + shift : 16 + z + shift, :]

                def magnetic(c):
                    return ms[old][k][b3 + (3 * row + c), 8 + z : 16 + z, :]

                ex_y = yes[old][b4 + (4 * row + k), z : z + 8, :]
                ez_y = yes[old][b4 + (4 * row + 2 + k), z : z + 8, :]
                ex, ey, ez = electric(X), electric(Y), electric(Z)
                cx = (ez_y - ez) - (electric(Y, row, 1) - ey)
                cy = (electric(X, row, 1) - ex) - (electric(Z, row + 1) - ez)
                cz = (electric(Y, row + 1) - ey) - (ex_y - ex)
                if t == halo and not upper:
                    cx, cy, cz = cx * live, cy * live, cz * live
                mx, my, mz = magnetic(X) - cx, magnetic(Y) - cy, magnetic(Z) - cz
                for c, v in ((X, mx), (Y, my), (Z, mz)):
                    ms[new][k][b3 + (3 * row + c), 8 + z : 16 + z, :] = v
                turned[0].append(pltpu.roll(mx, 1, 1))
                turned[1].append(pltpu.roll(mz, 1, 1))
            waiting.append([(ym, 0, 4 * row + 2 * j, z, turned[j], first_lane) for j in range(2)])
            if len(waiting) > LAG:
                keep()
        while waiting:
            keep()
        return start

    def two_steps(s, _):
        for old in range(2):
            left = STEPS - 1 - old - 2 * s
            start = BASE + W - left - 2
            block(old, False, True, 0, start)
            lax.fori_loop(1, W - 1 + left, functools.partial(block, old, True, True), start)
            block(old, True, False, W - 1 + left, start)
        return 0

    lax.fori_loop(0, STEPS // 2, two_steps, 0)

    def emit(r, _):
        for c, source in enumerate((X, Y, Z)):
            for t in range(on):
                stage[c, pl.ds(64 * t + r, 8, stride=8), :] = ea0[
                    3 * (r + BASE + W) + source, 16 + 8 * t : 24 + 8 * t, :
                ]
        return 0

    lax.fori_loop(0, 8, emit, 0)
    if upper:
        plane[0] = stage[0, 64 * on - 8 : 64 * on, :]
        plane[1] = stage[1, 64 * on - 8 : 64 * on, :]
    copy_all([(stage, out.at[:, pl.ds(64 * (CUT + 1) if upper else 0, 64 * on)])], sems)


def run_steps(upper, decay, gain, sides, arrays):
    smem = pl.BlockSpec(memory_space=pltpu.SMEM)
    out_shape = [jax.ShapeDtypeStruct((3, 640, 128), F32)]
    out_specs = [HBM]
    aliases = {}
    if upper:
        out_shape.append(jax.ShapeDtypeStruct((2, 8, 128), F32))
        out_specs.append(LOCAL)
    else:
        aliases = {4 + len(arrays) - 1: 0}
    tiles, on = (11 - CUT, 9 - CUT) if upper else (CUT + 3, CUT + 1)
    z = 16 + 8 * tiles
    field = pltpu.VMEM((3 * HELD, z, 128), F32)
    table = pltpu.VMEM((HELD, 8 * tiles, 128), F32)
    turned = pltpu.VMEM((4 * HELD, 8 * tiles, 128), F32)
    return pl.pallas_call(
        functools.partial(steps_kernel, upper),
        out_shape=out_shape,
        in_specs=[smem, smem] + [HBM] * (2 + len(arrays)),
        out_specs=out_specs,
        scratch_shapes=[field] * 8
        + [table] * 4
        + [turned] * 2
        + [
            pltpu.VMEM((8, 8 * tiles, 128), F32),
            pltpu.VMEM((ROWS, 8 * tiles, 128), F32),
            pltpu.VMEM((3, 64 * on, 128), F32),
            pltpu.SemaphoreType.DMA((39,)),
        ],
        input_output_aliases=aliases,
        compiler_params=params(),
        cost_estimate=cost(15),
        name="steps_upper" if upper else "steps_lower",
    )(decay, gain, *sides, *arrays)


def image_kernel(weights, centre, before, after, out, sh, rhs):
    gz = lax.axis_index("gz")
    lane = lax.broadcasted_iota(jnp.int32, (24, 128), 1)
    for q in range(15):
        shift = q - 7
        for c in range(2):
            v = centre[c]
            if shift > 0:
                v = jnp.where(
                    lane >= 128 - shift,
                    pltpu.roll(after[c], 128 - shift, 1),
                    pltpu.roll(v, 128 - shift, 1),
                )
            elif shift < 0:
                v = jnp.where(
                    lane < -shift, pltpu.roll(before[c], -shift, 1), pltpu.roll(v, -shift, 1)
                )
            sh[q, c] = v

    def fill(side):
        for q in range(15):
            for c in range(2):
                for i in range(4):
                    start = 4 * side + 1 + i
                    rhs[16 * q : 16 * q + 16, (4 * c + i) * 128 : (4 * c + i + 1) * 128] = sh[
                        q, c, start : start + 16, :
                    ]

    @pl.when(gz == 0)
    def _():
        fill(0)

    @pl.when(gz == 1)
    def _():
        fill(1)

    amplitude = jnp.dot(
        weights[...],
        rhs[...],
        precision=lax.Precision.HIGHEST,
        preferred_element_type=jnp.float32,
    )
    power = jnp.sum(amplitude * amplitude, axis=0, keepdims=True)
    for i in range(4):
        out[i : i + 1, :] = (
            power[:, i * 128 : (i + 1) * 128] + power[:, (4 + i) * 128 : (5 + i) * 128]
        )


def image_of(weights, centre, before, after):
    return pl.pallas_call(
        image_kernel,
        out_shape=jax.ShapeDtypeStruct((4, 128), jnp.float32),
        in_specs=[pl.BlockSpec(memory_space=pltpu.VMEM)] * 4,
        out_specs=pl.BlockSpec(memory_space=pltpu.VMEM),
        scratch_shapes=[
            pltpu.VMEM((15, 2, 24, 128), jnp.float32),
            pltpu.VMEM((240, 1024), jnp.float32),
        ],
        compiler_params=pltpu.CompilerParams(vmem_limit_bytes=VMEM),
        name="image",
    )(weights, centre, before, after)


def on_device(electric, magnetic, material, decay, gain, kernels):
    el = electric.reshape(3, 640, 128)
    mg = magnetic.reshape(3, 640, 128)
    mat = material.reshape(640, 128)
    weights = jnp.pad(
        kernels.transpose(0, 1, 3, 2).reshape(48, 15, 15), ((0, 0), (0, 0), (0, 1))
    ).reshape(48, 240)

    strips, edge, edge_strips = own_strips(el, mg, mat)
    edge = around(edge, "gz", 1)
    from_low, from_high = around(strips, "gy", 1), around(strips, "gy", -1)
    edge_low, edge_high = beyond(edge_strips, 1), beyond(edge_strips, -1)
    own_u, up_u, down_u, own_l, up_l, down_l = pack(el, mg, mat)
    strips, up_u, down_u, up_l, down_l = fill(
        from_low, from_high, edge_low, edge_high, edge, [up_u, down_u, up_l, down_l]
    )
    low_u, high_u = around(up_u, "gx", 1), around(down_u, "gx", -1)
    low_l, high_l = around(up_l, "gx", 1), around(down_l, "gx", -1)

    sides = [strips, edge]
    field, plane = run_steps(True, decay, gain, sides, [own_u, low_u, high_u])
    top = lax.ppermute(plane, "gz", [(1, 0)])
    top = jnp.where(lax.axis_index("gz") == 1, plane, top)
    top = jnp.stack([top, around(top, "gy", 1), around(top, "gy", -1)])
    top = jnp.concatenate([around(top, "gx", 1), top, around(top, "gx", -1)], 2)
    image = image_of(weights, top[0], top[1], top[2])
    (field,) = run_steps(
        False, decay, gain, sides, [own_u, low_u, high_u, own_l, low_l, high_l, field]
    )
    return (field.reshape(3, 80, 8, 128), image)


def solution(mesh):
    in_specs = (
        P(None, "gz", "gx", "gy"),
        P(None, "gz", "gx", "gy"),
        P("gz", "gx", "gy"),
        P(),
        P(),
        P(),
    )
    out_specs = (P(None, "gz", "gx", "gy"), P(("gx", "gz"), "gy"))
    return jax.shard_map(
        on_device, mesh=mesh, in_specs=in_specs, out_specs=out_specs, check_vma=False
    )
```

time: 160 us -> 114 us (0.71); the launches traced: 159 us -> 112 us
  Pallas kernels: 87.2 us -> 56.4 us
  waiting for transfers between devices: 35.7 us -> 19.1 us
    pallas_call x4 -> x3, Pallas kernels: 43.4 us -> 10.3 us  [the longest x1 4.34 us: pack(): pl.pallas_call(pack_kernel, out_shape=shapes, in_specs=[HBM] * 3, out_spe...]
    ppermute x13 -> x11, waiting for transfers between devices: 35.7 us -> 17.2 us  [around(): lax.ppermute(value, axis, [(i, (i + steps) % count) for i in range(count)])]
    ppermute x13 -> x11, starting transfers between devices: 28.7 us -> 23.1 us  [around(): lax.ppermute(value, axis, [(i, (i + steps) % count) for i in range(count)])]
    ppermute x0 -> x2, starting transfers between devices: none -> 4.14 us  [beyond(): return lax.ppermute(value, ('gy', 'gz'), pairs)]
    pallas_call x2, Pallas kernels: 41.4 us -> 43.7 us  [run_steps(): pl.pallas_call(functools.partial(steps_kernel, upper), out_shape=out_shap...]
    unnamed x28 -> x18, local copies, waits for them, and re-layouts: 3.39 us -> 3.18 us
  transfers between devices with their start and end apart: 14 -> 14, of which waited for: 6 -> 5; matrix products, arithmetic and copies ran while one was open for 1% -> 2% of each run, Pallas kernels for 20% -> 22%
where the time goes in v2:
time: 114 us; the launch traced here: 112 us
  Pallas kernels  56.4 us (49%)
  starting transfers between devices  30.1 us (26%)
  waiting for transfers between devices  19.1 us (17%)
  local copies, waits for them, and re-layouts  4.74 us (4%)
    pallas_call x2, Pallas kernels, run_steps(): pl.pallas_call(functools.partial(steps_kernel, upper), out_shape=out_shap...  43.7 us
    ppermute x11, starting transfers between devices, around(): lax.ppermute(value, axis, [(i, (i + steps) % count) for i in range(count)])  23.1 us
    ppermute x11, waiting for transfers between devices, around(): lax.ppermute(value, axis, [(i, (i + steps) % count) for i in range(count)])  17.2 us
    pallas_call x1, Pallas kernels, pack(): pl.pallas_call(pack_kernel, out_shape=shapes, in_specs=[HBM] * 3, out_spe...  4.34 us
    ppermute x2, starting transfers between devices, beyond(): return lax.ppermute(value, ('gy', 'gz'), pairs)  4.14 us
    pallas_call x1, Pallas kernels, own_strips(): pl.pallas_call(strip_kernel, out_shape=[jax.ShapeDtypeStruct((8, 80, 128)...  3.6 us
    unnamed x18, local copies, waits for them, and re-layouts  3.18 us
    ppermute x1, starting transfers between devices, on_device(): top = lax.ppermute(plane, 'gz', [(1, 0)])  2.81 us
  transfers between devices with their start and end apart: 14, of which 5 were waited for; matrix products, arithmetic and copies ran while one was open for 2% of the time, Pallas kernels for 22%

profile of v2, /device:TPU:2, one launch (start us, length us, event | category | flops | bytes accessed | tf_op | source)
XLA Modules:
  0.0 111.8 jit_solution(15787068106682879656)
XLA Ops:
  0.6 3.6 %own_strips.1 = (f32[8,80,128]{2,1,0:T(8,128)}, f32[56,8,128]{2,1,0:T(8,128)}, f32[8,8,128]{2,1,0:T(8,128)}) custom-call(f32[3,640,128]{2,1,0:T(8,128)} %bitcast.17, f32[3,640,128]{2,1,0:T(8,128)} %bitcast.19, s32[640,128]{1,0:T(8,128)} %bitcast.21), custom_call_target="tpu_custom_call" | custom-call | bytes 9000000 | tf_op jit(solution)/shard_map/own_strips/pallas_call | solution.py:105
  4.2 1.6 %collective-permute-start = (f32[8,80,128]{2,1,0:T(8,128)}, f32[8,80,128]{2,1,0:T(8,128)S(1)}, u32[]{:S(2)}, u32[]{:S(2)}) collective-permute-start(f32[8,80,128]{2,1,0:T(8,128)} %get-tuple-element.18), channel_id=1, source_target_pairs={{0,2},{2,4},{4,6},{6,0},{1,3},{3,5},{5,7},{7,1},{8,10},{10,12},{12... | collective-permute-start | bytes 983048 | tf_op jit(solution)/shard_map/ppermute | solution.py:28
  5.9 1.7 %collective-permute-start.1 = (f32[8,80,128]{2,1,0:T(8,128)}, f32[8,80,128]{2,1,0:T(8,128)S(1)}, u32[]{:S(2)}, u32[]{:S(2)}) collective-permute-start(f32[8,80,128]{2,1,0:T(8,128)} %get-tuple-element.18), channel_id=1, source_target_pairs={{0,6},{2,0},{4,2},{6,4},{1,7},{3,1},{5,3},{7,5},{8,14},{10,8},{12,... | collective-permute-start | bytes 983048 | tf_op jit(solution)/shard_map/ppermute | solution.py:28
  7.5 0.5 collective-permute-start.4
  8.0 1.4 %collective-permute-start.2 = (f32[8,8,128]{2,1,0:T(8,128)}, f32[8,8,128]{2,1,0:T(8,128)S(1)}, u32[]{:S(2)}, u32[]{:S(2)}) collective-permute-start(f32[8,8,128]{2,1,0:T(8,128)} %get-tuple-element.19), channel_id=1, source_target_pairs={{0,3},{1,2},{2,5},{3,4},{4,7},{5,6},{6,1},{7,0},{8,11},{9,10},{10,... | collective-permute-start | bytes 98312 | tf_op jit(solution)/shard_map/ppermute | solution.py:36
  9.4 2.8 %collective-permute-start.3 = (f32[8,8,128]{2,1,0:T(8,128)}, f32[8,8,128]{2,1,0:T(8,128)S(1)}, u32[]{:S(2)}, u32[]{:S(2)}) collective-permute-start(f32[8,8,128]{2,1,0:T(8,128)} %get-tuple-element.19), channel_id=1, source_target_pairs={{0,7},{1,6},{2,1},{3,0},{4,3},{5,2},{6,5},{7,4},{8,15},{9,14},{10,... | collective-permute-start | bytes 98312 | tf_op jit(solution)/shard_map/ppermute | solution.py:36
  12.1 4.3 %pack.1 = (f32[56,32,128]{2,1,0:T(8,128)}, f32[46,40,128]{2,1,0:T(8,128)}, f32[43,40,128]{2,1,0:T(8,128)}, f32[56,48,128]{2,1,0:T(8,128)}, f32[46,48,128]{2,1,0:T(8,128)}, /*index=5*/f32[43,48,128]{2,1,0:T(8,128)}) custom-call(f32[3,640,128]{2,1,0:T(8,128)} %bitcast.18, f32[3,640,128]{2,1,0:T(8,128)} %bitcast.20, s32[640,128]{1,0:T(8,128)} %bitcast.22), custom_call_target="tpu_custom_call" | custom-call | bytes 15000000 | tf_op jit(solution)/shard_map/pack/pallas_call | solution.py:178
  16.5 0.3 collective-permute-done.2.edge_low
  16.8 0.0 copy-start.7
  16.8 0.0 collective-permute-done.3.edge_high
  16.8 0.0 copy-start.8
  16.8 0.0 collective-permute-done.4.edge
  16.8 0.0 copy-start.2
  16.9 0.0 collective-permute-done.from_low
  16.9 0.0 copy-start.4
  16.9 0.0 collective-permute-done.1.from_high
  16.9 0.0 copy-start.5
  16.9 0.6 copy-done.7
  17.4 0.0 copy-done.8
  17.5 0.1 copy-done.2
  17.6 0.1 copy-done.4
  17.7 0.1 copy-done.5
  17.8 2.3 %fill.1 = (f32[8,88,128]{2,1,0:T(8,128)}, f32[46,40,128]{2,1,0:T(8,128)}, f32[43,40,128]{2,1,0:T(8,128)}, f32[46,48,128]{2,1,0:T(8,128)}, f32[43,48,128]{2,1,0:T(8,128)}) custom-call(f32[8,80,128]{2,1,0:T(8,128)} %copy-done.4, f32[8,80,128]{2,1,0:T(8,128)} %copy-done.5, ...), custom_call_target="tpu_custom_call", output_to_operand_aliasing={{1}: (5, {}), {2}: (6, {}), {3}: (7, {}), {4}: (8, {})} | custom-call | bytes 3000000 | tf_op jit(solution)/shard_map/fill/pallas_call | solution.py:221
  20.2 0.1 collective-permute-start.5
  20.2 5.3 %collective-permute-start.6 = (f32[43,40,128]{2,1,0:T(8,128)}, f32[43,40,128]{2,1,0:T(8,128)S(1)}, u32[]{:S(2)}, u32[]{:S(2)}) collective-permute-start(f32[43,40,128]{2,1,0:T(8,128)} %get-tuple-element.28), channel_id=1, source_target_pairs={{0,120},{8,0},{16,8},{24,16},{32,24},{40,32},{48,40},{56,48},{64,5... | collective-permute-start | bytes 2641928 | tf_op jit(solution)/shard_map/ppermute | solution.py:28
  25.6 0.0 collective-permute-start.7
  25.6 5.4 %collective-permute-start.8 = (f32[43,48,128]{2,1,0:T(8,128)}, f32[43,48,128]{2,1,0:T(8,128)}, u32[]{:S(2)}, u32[]{:S(2)}) collective-permute-start(f32[43,48,128]{2,1,0:T(8,128)} %get-tuple-element.31), channel_id=1, source_target_pairs={{0,120},{8,0},{16,8},{24,16},{32,24},{40,32},{48,40},{56,48},{64,5... | collective-permute-start | bytes 3170312 | tf_op jit(solution)/shard_map/ppermute | solution.py:28
  31.0 15.0 %collective-permute-done.6.refs_2_ = f32[43,40,128]{2,1,0:T(8,128)S(1)} collective-permute-done((f32[43,40,128]{2,1,0:T(8,128)}, f32[43,40,128]{2,1,0:T(8,128)S(1)}, u32[]{:S(2)}, u32[]{:S(2)}) %collective-permute-start.6) | collective-permute-done | bytes 880672 | tf_op jit(solution)/shard_map/ppermute | solution.py:28
  45.9 0.0 copy-start.1
  45.9 0.0 collective-permute-done.5.refs_1_
  45.9 0.0 copy-start
  45.9 0.9 copy-done.1
  46.8 0.3 copy-done
  47.2 0.0 copy-start.6
  47.2 18.4 %steps_upper.1 = (f32[3,640,128]{2,1,0:T(8,128)}, f32[2,8,128]{2,1,0:T(8,128)}) custom-call(f32[5]{0:T(128)} %decay.3, f32[5]{0:T(128)} %gain.3, f32[8,88,128]{2,1,0:T(8,128)} %get-tuple-element.25.strips, f32[56,8,128]{2,1,0:T(8,128)} %copy-done.2, f32[56,32,128]{2,1,0:T(8,128)} %get-tuple-element.26.refs_0_, f32[46,40,128]{2,1,0:T(8,128)} %copy-done, ...), custom_call_target="tpu_custom_call" | custom-call | bytes 45000000 | tf_op jit(solution)/shard_map/steps_upper/pallas_call | solution.py:480
  65.6 2.8 %collective-permute-start.9 = (f32[2,8,128]{2,1,0:T(8,128)}, f32[2,8,128]{2,1,0:T(8,128)S(1)}, u32[]{:S(2)}, u32[]{:S(2)}) collective-permute-start(f32[2,8,128]{2,1,0:T(8,128)} %get-tuple-element.33), channel_id=1, source_target_pairs={{1,0},{3,2},{5,4},{7,6},{9,8},{11,10},{13,12},{15,14},{17,16},{19,... | collective-permute-start | bytes 24584 | tf_op jit(solution)/shard_map/ppermute | solution.py:586
  68.4 1.6 %collective-permute-done.9 = f32[2,8,128]{2,1,0:T(8,128)S(1)} collective-permute-done((f32[2,8,128]{2,1,0:T(8,128)}, f32[2,8,128]{2,1,0:T(8,128)S(1)}, u32[]{:S(2)}, u32[]{:S(2)}) %collective-permute-start.9) | collective-permute-done | bytes 8224 | tf_op jit(solution)/shard_map/ppermute | solution.py:586
  69.9 0.7 broadcast_select_fusion
  70.6 0.0 collective-permute-start.10
  70.6 3.2 %collective-permute-start.11 = (f32[2,8,128]{2,1,0:T(8,128)S(1)}, f32[2,8,128]{2,1,0:T(8,128)S(1)}, u32[]{:S(2)}, u32[]{:S(2)}) collective-permute-start(f32[2,8,128]{2,1,0:T(8,128)S(1)} %broadcast_select_fusion), channel_id=1, source_target_pairs={{0,6},{2,0},{4,2},{6,4},{1,7},{3,1},{5,3},{7,5},{8,14},{10,8},{12,... | collective-permute-start | bytes 24584 | tf_op jit(solution)/shard_map/ppermute | solution.py:28
  73.9 1.6 %collective-permute-done.10 = f32[2,8,128]{2,1,0:T(8,128)S(1)} collective-permute-done((f32[2,8,128]{2,1,0:T(8,128)S(1)}, f32[2,8,128]{2,1,0:T(8,128)S(1)}, u32[]{:S(2)}, u32[]{:S(2)}) %collective-permute-start.10) | collective-permute-done | bytes 8224 | tf_op jit(solution)/shard_map/ppermute | solution.py:28
  75.5 0.0 collective-permute-done.11
  75.5 0.0 collective-permute-start.12
  75.5 5.4 %collective-permute-start.13 = (f32[3,2,8,128]{3,2,1,0:T(8,128)S(1)}, f32[3,2,8,128]{3,2,1,0:T(8,128)S(1)}, u32[]{:S(2)}, u32[]{:S(2)}) collective-permute-start(f32[3,2,8,128]{3,2,1,0:T(8,128)S(1)} %pad_maximum_fusion.1), channel_id=1, source_target_pairs={{0,120},{8,0},{16,8},{24,16},{32,24},{40,32},{48,40},{56,48},{64,5... | collective-permute-start | bytes 73736 | tf_op jit(solution)/shard_map/ppermute | solution.py:28
  80.9 0.0 copy-done.6
  80.9 0.2 reshape.26
  81.1 0.7 copy.15.weights
  81.8 0.5 collective-permute-done.12
  82.4 0.0 collective-permute-done.13
  82.4 0.6 slice_bitcast_fusion
  83.0 2.4 %image.1 = f32[4,128]{1,0:T(4,128)} custom-call(f32[48,240]{1,0:T(8,128)} %copy.15.weights, f32[2,24,128]{2,1,0:T(8,128)} %get-tuple-element.36.centre, f32[2,24,128]{2,1,0:T(8,128)} %get-tuple-element.35.before, f32[2,24,128]{2,1,0:T(8,128)} %get-tuple-element.34.after), custom_call_target="tpu_custom_call" | custom-call | tf_op jit(solution)/shard_map/image/pallas_call | solution.py:551
  85.4 0.0 collective-permute-done.8.refs_5_
  85.4 0.0 collective-permute-done.7.refs_4_
  85.4 0.0 copy-start.3
  85.4 1.0 copy-done.3
  86.4 25.3 %steps_lower.1 = f32[3,640,128]{2,1,0:T(8,128)} custom-call(f32[5]{0:T(128)} %decay.3, f32[5]{0:T(128)} %gain.3, f32[8,88,128]{2,1,0:T(8,128)} %get-tuple-element.25.strips, f32[56,8,128]{2,1,0:T(8,128)} %copy-done.2, f32[56,32,128]{2,1,0:T(8,128)} %get-tuple-element.26.refs_0_, f32[46,40,128]{2,1,0:T(8,128)} %copy-done, ...), custom_call_target="tpu_custom_call", output_to_operand_aliasing={{}: (10, {})} | custom-call | bytes 45000000 | tf_op jit(solution)/shard_map/steps_lower/pallas_call | solution.py:480
  (4 shorter events, 0.1 us)
Async XLA Ops:
  4.2 12.6 %collective-permute-start = (f32[8,80,128]{2,1,0:T(8,128)}, f32[8,80,128]{2,1,0:T(8,128)S(1)}, u32[]{:S(2)}, u32[]{:S(2)}) collective-permute-start(f32[8,80,128]{2,1,0:T(8,128)} %get-tuple-element.18), channel_id=1, source_target_pairs={{0,2},{2,4},{4,6},{6,0},{1,3},{3,5},{5,7},{7,1},{8,10},{10,12},{12... | collective-permute-start | bytes 983048 | tf_op jit(solution)/shard_map/ppermute | solution.py:28
  5.9 11.0 %collective-permute-start.1 = (f32[8,80,128]{2,1,0:T(8,128)}, f32[8,80,128]{2,1,0:T(8,128)S(1)}, u32[]{:S(2)}, u32[]{:S(2)}) collective-permute-start(f32[8,80,128]{2,1,0:T(8,128)} %get-tuple-element.18), channel_id=1, source_target_pairs={{0,6},{2,0},{4,2},{6,4},{1,7},{3,1},{5,3},{7,5},{8,14},{10,8},{12,... | collective-permute-start | bytes 983048 | tf_op jit(solution)/shard_map/ppermute | solution.py:28
  7.5 9.3 %collective-permute-start.4 = (f32[56,8,128]{2,1,0:T(8,128)}, f32[56,8,128]{2,1,0:T(8,128)S(1)}, u32[]{:S(2)}, u32[]{:S(2)}) collective-permute-start(f32[56,8,128]{2,1,0:T(8,128)} %get-tuple-element.20), channel_id=1, source_target_pairs={{0,1},{1,0},{2,3},{3,2},{4,5},{5,4},{6,7},{7,6},{8,9},{9,8},{10,11... | collective-permute-start | bytes 688136 | tf_op jit(solution)/shard_map/ppermute | solution.py:28
  8.0 8.8 %collective-permute-start.2 = (f32[8,8,128]{2,1,0:T(8,128)}, f32[8,8,128]{2,1,0:T(8,128)S(1)}, u32[]{:S(2)}, u32[]{:S(2)}) collective-permute-start(f32[8,8,128]{2,1,0:T(8,128)} %get-tuple-element.19), channel_id=1, source_target_pairs={{0,3},{1,2},{2,5},{3,4},{4,7},{5,6},{6,1},{7,0},{8,11},{9,10},{10,... | collective-permute-start | bytes 98312 | tf_op jit(solution)/shard_map/ppermute | solution.py:36
  9.4 7.5 %collective-permute-start.3 = (f32[8,8,128]{2,1,0:T(8,128)}, f32[8,8,128]{2,1,0:T(8,128)S(1)}, u32[]{:S(2)}, u32[]{:S(2)}) collective-permute-start(f32[8,8,128]{2,1,0:T(8,128)} %get-tuple-element.19), channel_id=1, source_target_pairs={{0,7},{1,6},{2,1},{3,0},{4,3},{5,2},{6,5},{7,4},{8,15},{9,14},{10,... | collective-permute-start | bytes 98312 | tf_op jit(solution)/shard_map/ppermute | solution.py:36
  16.8 0.6 copy-start.7
  16.8 0.6 copy-start.8
  16.8 0.7 copy-start.2
  16.9 0.8 copy-start.4
  16.9 1.0 copy-start.5
  20.2 25.8 %collective-permute-start.5 = (f32[46,40,128]{2,1,0:T(8,128)}, f32[46,40,128]{2,1,0:T(8,128)S(1)}, u32[]{:S(2)}, u32[]{:S(2)}) collective-permute-start(f32[46,40,128]{2,1,0:T(8,128)} %get-tuple-element.27), channel_id=1, source_target_pairs={{0,8},{8,16},{16,24},{24,32},{32,40},{40,48},{48,56},{56,64},{64,7... | collective-permute-start | bytes 2826248 | tf_op jit(solution)/shard_map/ppermute | solution.py:28
  20.2 25.7 %collective-permute-start.6 = (f32[43,40,128]{2,1,0:T(8,128)}, f32[43,40,128]{2,1,0:T(8,128)S(1)}, u32[]{:S(2)}, u32[]{:S(2)}) collective-permute-start(f32[43,40,128]{2,1,0:T(8,128)} %get-tuple-element.28), channel_id=1, source_target_pairs={{0,120},{8,0},{16,8},{24,16},{32,24},{40,32},{48,40},{56,48},{64,5... | collective-permute-start | bytes 2641928 | tf_op jit(solution)/shard_map/ppermute | solution.py:28
  25.6 59.8 %collective-permute-start.7 = (f32[46,48,128]{2,1,0:T(8,128)}, f32[46,48,128]{2,1,0:T(8,128)S(1)}, u32[]{:S(2)}, u32[]{:S(2)}) collective-permute-start(f32[46,48,128]{2,1,0:T(8,128)} %get-tuple-element.30), channel_id=1, source_target_pairs={{0,8},{8,16},{16,24},{24,32},{32,40},{40,48},{48,56},{56,64},{64,7... | collective-permute-start | bytes 3391496 | tf_op jit(solution)/shard_map/ppermute | solution.py:28
  25.6 59.8 %collective-permute-start.8 = (f32[43,48,128]{2,1,0:T(8,128)}, f32[43,48,128]{2,1,0:T(8,128)}, u32[]{:S(2)}, u32[]{:S(2)}) collective-permute-start(f32[43,48,128]{2,1,0:T(8,128)} %get-tuple-element.31), channel_id=1, source_target_pairs={{0,120},{8,0},{16,8},{24,16},{32,24},{40,32},{48,40},{56,48},{64,5... | collective-permute-start | bytes 3170312 | tf_op jit(solution)/shard_map/ppermute | solution.py:28
  45.9 0.9 copy-start.1
  45.9 1.2 %copy-start = (f32[46,40,128]{2,1,0:T(8,128)}, f32[46,40,128]{2,1,0:T(8,128)S(1)}, u32[]{:S(2)}) copy-start(f32[46,40,128]{2,1,0:T(8,128)S(1)} %collective-permute-done.5.refs_1_) | copy-start | bytes 2826244
  47.2 33.7 %copy-start.6 = (f32[2,24,15,15]{1,0,3,2:T(2,128)S(1)}, f32[2,24,15,15]{1,0,3,2:T(2,128)}, u32[]{:S(2)}) copy-start(f32[2,24,15,15]{1,0,3,2:T(2,128)} %param.11) | copy-start | bytes 129604
  65.6 4.4 %collective-permute-start.9 = (f32[2,8,128]{2,1,0:T(8,128)}, f32[2,8,128]{2,1,0:T(8,128)S(1)}, u32[]{:S(2)}, u32[]{:S(2)}) collective-permute-start(f32[2,8,128]{2,1,0:T(8,128)} %get-tuple-element.33), channel_id=1, source_target_pairs={{1,0},{3,2},{5,4},{7,6},{9,8},{11,10},{13,12},{15,14},{17,16},{19,... | collective-permute-start | bytes 24584 | tf_op jit(solution)/shard_map/ppermute | solution.py:586
  70.6 4.9 %collective-permute-start.10 = (f32[2,8,128]{2,1,0:T(8,128)S(1)}, f32[2,8,128]{2,1,0:T(8,128)S(1)}, u32[]{:S(2)}, u32[]{:S(2)}) collective-permute-start(f32[2,8,128]{2,1,0:T(8,128)S(1)} %broadcast_select_fusion), channel_id=1, source_target_pairs={{0,2},{2,4},{4,6},{6,0},{1,3},{3,5},{5,7},{7,1},{8,10},{10,12},{12... | collective-permute-start | bytes 24584 | tf_op jit(solution)/shard_map/ppermute | solution.py:28
  70.6 4.9 %collective-permute-start.11 = (f32[2,8,128]{2,1,0:T(8,128)S(1)}, f32[2,8,128]{2,1,0:T(8,128)S(1)}, u32[]{:S(2)}, u32[]{:S(2)}) collective-permute-start(f32[2,8,128]{2,1,0:T(8,128)S(1)} %broadcast_select_fusion), channel_id=1, source_target_pairs={{0,6},{2,0},{4,2},{6,4},{1,7},{3,1},{5,3},{7,5},{8,14},{10,8},{12,... | collective-permute-start | bytes 24584 | tf_op jit(solution)/shard_map/ppermute | solution.py:28
  75.5 6.9 %collective-permute-start.12 = (f32[3,2,8,128]{3,2,1,0:T(8,128)S(1)}, f32[3,2,8,128]{3,2,1,0:T(8,128)S(1)}, u32[]{:S(2)}, u32[]{:S(2)}) collective-permute-start(f32[3,2,8,128]{3,2,1,0:T(8,128)S(1)} %pad_maximum_fusion.1), channel_id=1, source_target_pairs={{0,8},{8,16},{16,24},{24,32},{32,40},{40,48},{48,56},{56,64},{64,7... | collective-permute-start | bytes 73736 | tf_op jit(solution)/shard_map/ppermute | solution.py:28
  75.5 6.9 %collective-permute-start.13 = (f32[3,2,8,128]{3,2,1,0:T(8,128)S(1)}, f32[3,2,8,128]{3,2,1,0:T(8,128)S(1)}, u32[]{:S(2)}, u32[]{:S(2)}) collective-permute-start(f32[3,2,8,128]{3,2,1,0:T(8,128)S(1)} %pad_maximum_fusion.1), channel_id=1, source_target_pairs={{0,120},{8,0},{16,8},{24,16},{32,24},{40,32},{48,40},{56,48},{64,5... | collective-permute-start | bytes 73736 | tf_op jit(solution)/shard_map/ppermute | solution.py:28
  85.4 1.0 copy-start.3

commit v3 on v2

--- a/solution.py
+++ b/solution.py
@@ -15,9 +15,9 @@
 ROWS = 8 + 2 * W
 BASE = 4
 HELD = BASE + ROWS + 2
-CUT = 6
+CUT = 7
 LAG = 4
-VMEM = 56 * 1024 * 1024
+VMEM = 63 * 1024 * 1024
 F32 = jnp.float32
 HBM = pl.BlockSpec(memory_space=pl.ANY)
 LOCAL = pl.BlockSpec(memory_space=pltpu.VMEM)
@@ -49,7 +49,7 @@
 
 
 def cost(us):
-    return pl.CostEstimate(flops=0, bytes_accessed=int(us * 3e6), transcendentals=0)
+    return pl.CostEstimate(flops=int(us * 1e9), bytes_accessed=int(us * 3e6), transcendentals=0)
 
 
 def plane_of(r, c):
@@ -122,78 +122,70 @@
     )(el, mg, mat)
 
 
-def pack_kernel(el, mg, mat, own_u, up_u, down_u, own_l, up_l, down_l, ext, matv, planes, sems):
-    loads = [(mat, matv)]
+def pack_kernel(first, last, el, mg, mat, *refs):
+    if first:
+        own, up, down, ext, matv, planes, sems = refs
+    else:
+        strips, own, up, down, ext, matv, planes, sems = refs
+    tiles = last - first
+    here = pl.ds(64 * first, 64 * tiles)
+    loads = [(mat.at[here], matv)]
     for c, (which, comp) in enumerate(SOURCE):
-        loads.append(((el, mg)[which].at[comp], ext.at[c]))
+        loads.append(((el, mg)[which].at[comp, here], ext.at[c]))
     copy_all(loads, sems)
 
-    def rows_of(first, last):
-        def row(r, _):
-            for t in range(first, last):
-                rows = pl.ds(64 * t + r, 8, stride=8)
-                for c in range(NC):
-                    if c == 6:
-                        v = matv[rows, :].astype(F32)
-                    else:
-                        v = ext[c, rows, :]
-                        if c >= 3:
-                            v = v * 2.0
-                    planes[plane_of(r, c), 8 * t : 8 * t + 8, :] = v
-            return 0
-
-        lax.fori_loop(0, 8, row, 0)
-
-    def sends(first, last, own, up, down):
-        z, to = pl.ds(8 * first, 8 * (last - first)), pl.ds(0, 8 * (last - first))
-        pairs = [(planes.at[:, z], own)]
-        for a, b, n in ((6, 0, 18), (30, 18, 2), (33, 20, 15), (51, 35, 5)):
-            pairs.append((planes.at[pl.ds(a, n), z], up.at[pl.ds(b, n), to]))
-        for a, b, n in ((0, 0, 17), (24, 17, 15), (48, 32, 5)):
-            pairs.append((planes.at[pl.ds(a, n), z], down.at[pl.ds(b, n), to]))
-        return pairs
-
-    rows_of(CUT, 10)
-    pairs = sends(CUT, 10, own_u, up_u, down_u)
-    upper = [pltpu.make_async_copy(a, b, sems.at[i]) for i, (a, b) in enumerate(pairs)]
-    for copy in upper:
-        copy.start()
-    rows_of(0, CUT)
-    pairs = sends(0, CUT, own_l, up_l, down_l)
-    lower = [pltpu.make_async_copy(a, b, sems.at[8 + i]) for i, (a, b) in enumerate(pairs)]
-    for copy in lower:
-        copy.start()
-    for copy in upper + lower:
-        copy.wait()
-
-
-def pack(el, mg, mat):
-    shapes = []
-    for layers, more in ((8 * (10 - CUT), 8), (8 * CUT, 0)):
-        shapes += [
+    def row(r, _):
+        for t in range(tiles):
+            rows = pl.ds(64 * t + r, 8, stride=8)
+            for c in range(NC):
+                if c == 6:
+                    v = matv[rows, :].astype(F32)
+                else:
+                    v = ext[c, rows, :]
+                    if c >= 3:
+                        v = v * 2.0
+                planes[plane_of(r, c), 8 * t : 8 * t + 8, :] = v
+        return 0
+
+    lax.fori_loop(0, 8, row, 0)
+    z = pl.ds(0, 8 * tiles)
+    pairs = [(planes, own)]
+    for a, b, n in ((6, 0, 18), (30, 18, 2), (33, 20, 15), (51, 35, 5)):
+        pairs.append((planes.at[pl.ds(a, n)], up.at[pl.ds(b, n), z]))
+    for a, b, n in ((0, 0, 17), (24, 17, 15), (48, 32, 5)):
+        pairs.append((planes.at[pl.ds(a, n)], down.at[pl.ds(b, n), z]))
+    if not first:
+        pairs.append((strips.at[pl.ds(8 - W, W), z], up.at[pl.ds(40, W)]))
+        pairs.append((strips.at[pl.ds(0, W), z], down.at[pl.ds(37, W)]))
+    copy_all(pairs, sems)
+
+
+def pack(first, last, el, mg, mat, *strips):
+    layers = 8 * (last - first)
+    sent = layers + 8 if first else layers
+    return pl.pallas_call(
+        functools.partial(pack_kernel, first, last),
+        out_shape=[
             jax.ShapeDtypeStruct((8 * NC, layers, 128), F32),
-            jax.ShapeDtypeStruct((40 + W, layers + more, 128), F32),
-            jax.ShapeDtypeStruct((37 + W, layers + more, 128), F32),
-        ]
-    return pl.pallas_call(
-        pack_kernel,
-        out_shape=shapes,
-        in_specs=[HBM] * 3,
-        out_specs=[HBM] * 6,
+            jax.ShapeDtypeStruct((40 + W, sent, 128), F32),
+            jax.ShapeDtypeStruct((37 + W, sent, 128), F32),
+        ],
+        in_specs=[HBM] * 3 + [LOCAL] * len(strips),
+        out_specs=[HBM] * 3,
         scratch_shapes=[
-            pltpu.VMEM((6, 640, 128), F32),
-            pltpu.VMEM((640, 128), jnp.int32),
-            pltpu.VMEM((8 * NC, 80, 128), F32),
-            pltpu.SemaphoreType.DMA((16,)),
+            pltpu.VMEM((6, 8 * layers, 128), F32),
+            pltpu.VMEM((8 * layers, 128), jnp.int32),
+            pltpu.VMEM((8 * NC, layers, 128), F32),
+            pltpu.SemaphoreType.DMA((10,)),
         ],
         compiler_params=params(),
-        cost_estimate=cost(5),
-        name="pack",
-    )(el, mg, mat)
+        cost_estimate=cost(3),
+        name="pack_upper" if first else "pack_lower",
+    )(el, mg, mat, *strips)
 
 
 def fill_kernel(from_low, from_high, edge_low, edge_high, edge, *refs):
-    strips, up_u, down_u, up_l, down_l, halo, sems = refs[4:]
+    strips, up_u, down_u, halo, sems = refs[2:]
     lane = lax.broadcasted_iota(jnp.int32, (8, 80, 128), 2)
     halo[:, 0:80, :] = jnp.where(lane % 16 < 8, from_high[...], from_low[...])
     lane = lax.broadcasted_iota(jnp.int32, (8, 8, 128), 2)
@@ -210,8 +202,6 @@
         )
         for a, b, n in parts:
             pairs.append((edge.at[pl.ds(a, n)], message.at[pl.ds(b, n), pl.ds(nu, 8)]))
-    for message, first, count in ((up_l, 8 - W, 40), (down_l, 0, 37)):
-        pairs.append((halo.at[pl.ds(first, W), pl.ds(0, nl)], message.at[pl.ds(count, W)]))
     copy_all(pairs, sems)
 
 
@@ -221,10 +211,10 @@
     return pl.pallas_call(
         fill_kernel,
         out_shape=shapes,
-        in_specs=[LOCAL] * 5 + [HBM] * 4,
-        out_specs=[HBM] * 5,
-        scratch_shapes=[pltpu.VMEM((8, 88, 128), F32), pltpu.SemaphoreType.DMA((12,))],
-        input_output_aliases={5 + i: 1 + i for i in range(4)},
+        in_specs=[LOCAL] * 5 + [HBM] * 2,
+        out_specs=[HBM] * 3,
+        scratch_shapes=[pltpu.VMEM((8, 88, 128), F32), pltpu.SemaphoreType.DMA((10,))],
+        input_output_aliases={5: 1, 6: 2},
         compiler_params=params(),
         cost_estimate=cost(1),
         name="fill",
@@ -298,8 +288,9 @@
         return 0
 
     lax.fori_loop(0, HELD, ends, 0)
-    for copy in copies:
-        copy.wait()
+    strip_copies = [i for g in range(len(groups)) for i in range(13 * g, 13 * g + 3)]
+    for i in strip_copies:
+        copies[i].wait()
 
     def unpack(r, _):
         at = BASE + r
@@ -317,6 +308,9 @@
         return 0
 
     lax.fori_loop(0, ROWS, unpack, 0)
+    for i, copy in enumerate(copies):
+        if i not in strip_copies:
+            copy.wait()
     hz = 8 * halo
 
     @pl.when(jnp.logical_not(counts))
@@ -352,16 +346,22 @@
     last, first_lane = lane == 127, lane == 0
     units = [(row, t) for row in range(2) for t in range(tiles)]
 
-    def first_turn(i, _):
+    def turn_two(which, r0):
         kept = []
         for row, t in units:
-            r = BASE + 2 * i + row
             for j, c in enumerate((X, Z)):
-                pair = [pltpu.roll(e[3 * r + c, 8 + 8 * t : 16 + 8 * t, :], 127, 1) for e in es[0]]
-                kept.append((4 * r + 2 * j, 8 * t, pair))
+                pair = [
+                    pltpu.roll(e[3 * r0 + (3 * row + c), 8 + 8 * t : 16 + 8 * t, :], 127, 1)
+                    for e in es[which]
+                ]
+                kept.append((4 * row + 2 * j, 8 * t, pair))
+        y = yes[which]
         for i, z, (a, b) in kept:
-            ya[i, z : z + 8, :] = jnp.where(last, b, a)
-            ya[i + 1, z : z + 8, :] = jnp.where(last, a, b)
+            y[4 * r0 + i, z : z + 8, :] = jnp.where(last, b, a)
+            y[4 * r0 + (i + 1), z : z + 8, :] = jnp.where(last, a, b)
+
+    def first_turn(i, _):
+        turn_two(0, BASE + 2 * i)
         return 0
 
     lax.fori_loop(0, ROWS // 2, first_turn, 0)
@@ -371,43 +371,42 @@
         base = start + 2 * m
         b3, b4 = 3 * base, 4 * base
         waiting = []
+        jobs = [(ms, row, t) for row, t in units] + [(es, row, t) for row, t in units]
+        jobs = jobs if with_e else []
+
+        def turn():
+            refs, row, t = jobs.pop(0)
+            z = 8 * t
+            if refs is ms:
+                pairs = [
+                    [pltpu.roll(f[b3 + (3 * (row - 2) + c), 8 + z : 16 + z, :], 1, 1) for f in ms[new]]
+                    for c in (X, Z)
+                ]
+                waiting.append((ym, 0, 4 * row, z, pairs, first_lane))
+            else:
+                pairs = [
+                    [pltpu.roll(f[b3 + (3 * (row - 4) + c), 8 + z : 16 + z, :], 127, 1) for f in es[new]]
+                    for c in (X, Z)
+                ]
+                waiting.append((yes[new], b4, 4 * (row - 4), z, pairs, last))
 
         def keep():
-            for y, b, i, z, (a, c), edge_lane in waiting.pop(0):
-                y[b + i, z : z + 8, :] = jnp.where(edge_lane, c, a)
-                y[b + (i + 1), z : z + 8, :] = jnp.where(edge_lane, a, c)
-
-        for row, t in units if with_e else ():
-            e, z = row - 2, 8 * t
-            turned = [[], []]
-            for k in range(2):
-
-                def magnetic(c, r=e, shift=0):
-                    return ms[new][k][b3 + (3 * r + c), 8 + z + shift : 16 + z + shift, :]
-
-                def electric(c):
-                    return es[old][k][b3 + (3 * e + c), 8 + z : 16 + z, :]
-
-                mx_y = ym[4 * row + k, z : z + 8, :]
-                mz_y = ym[4 * row + 2 + k, z : z + 8, :]
-                mx, my, mz = magnetic(X), magnetic(Y), magnetic(Z)
-                d = ds_[k][base + e, z : z + 8, :]
-                g = gs[k][base + e, z : z + 8, :]
-                ex = d * electric(X) + g * ((mz - mz_y) - (my - magnetic(Y, e, -1)))
-                ey = d * electric(Y) + g * ((mx - magnetic(X, e, -1)) - (mz - magnetic(Z, e - 1)))
-                ez = d * electric(Z) + g * ((my - magnetic(Y, e - 1)) - (mx - mx_y))
-                for c, v in ((X, ex), (Y, ey), (Z, ez)):
-                    es[new][k][b3 + (3 * e + c), 8 + z : 16 + z, :] = v
-                turned[0].append(pltpu.roll(ex, 127, 1))
-                turned[1].append(pltpu.roll(ez, 127, 1))
-            waiting.append(
-                [(yes[new], b4, 4 * e + 2 * j, z, turned[j], last) for j in range(2)]
-            )
-            if len(waiting) > LAG:
-                keep()
+            y, b, i, z, pairs, edge_lane = waiting.pop(0)
+            for j, (v0, v1) in enumerate(pairs):
+                y[b + (i + 2 * j), z : z + 8, :] = jnp.where(edge_lane, v1, v0)
+                y[b + (i + 2 * j + 1), z : z + 8, :] = jnp.where(edge_lane, v0, v1)
+
+        def pace():
+            for _ in range(2):
+                if jobs:
+                    turn()
+            for _ in range(2):
+                if len(waiting) > LAG or (waiting and not jobs):
+                    keep()
+
         for row, t in units if with_m else ():
+            pace()
             z = 8 * t
-            turned = [[], []]
             for k in range(2):
 
                 def electric(c, r=row, shift=0):
@@ -427,13 +426,32 @@
                 mx, my, mz = magnetic(X) - cx, magnetic(Y) - cy, magnetic(Z) - cz
                 for c, v in ((X, mx), (Y, my), (Z, mz)):
                     ms[new][k][b3 + (3 * row + c), 8 + z : 16 + z, :] = v
-                turned[0].append(pltpu.roll(mx, 1, 1))
-                turned[1].append(pltpu.roll(mz, 1, 1))
-            waiting.append([(ym, 0, 4 * row + 2 * j, z, turned[j], first_lane) for j in range(2)])
+        while jobs:
+            turn()
             if len(waiting) > LAG:
                 keep()
         while waiting:
             keep()
+        for row, t in units if with_e else ():
+            e, z = row - 2, 8 * t
+            for k in range(2):
+
+                def magnetic(c, r=e, shift=0):
+                    return ms[new][k][b3 + (3 * r + c), 8 + z + shift : 16 + z + shift, :]
+
+                def electric(c):
+                    return es[old][k][b3 + (3 * e + c), 8 + z : 16 + z, :]
+
+                mx_y = ym[4 * row + k, z : z + 8, :]
+                mz_y = ym[4 * row + 2 + k, z : z + 8, :]
+                mx, my, mz = magnetic(X), magnetic(Y), magnetic(Z)
+                d = ds_[k][base + e, z : z + 8, :]
+                g = gs[k][base + e, z : z + 8, :]
+                ex = d * electric(X) + g * ((mz - mz_y) - (my - magnetic(Y, e, -1)))
+                ey = d * electric(Y) + g * ((mx - magnetic(X, e, -1)) - (mz - magnetic(Z, e - 1)))
+                ez = d * electric(Z) + g * ((my - magnetic(Y, e - 1)) - (mx - mx_y))
+                for c, v in ((X, ex), (Y, ey), (Z, ez)):
+                    es[new][k][b3 + (3 * e + c), 8 + z : 16 + z, :] = v
         return start
 
     def two_steps(s, _):
@@ -443,6 +461,7 @@
             block(old, False, True, 0, start)
             lax.fori_loop(1, W - 1 + left, functools.partial(block, old, True, True), start)
             block(old, True, False, W - 1 + left, start)
+            turn_two(1 - old, start + 2 * (W - 2 + left))
         return 0
 
     lax.fori_loop(0, STEPS // 2, two_steps, 0)
@@ -493,7 +512,7 @@
         ],
         input_output_aliases=aliases,
         compiler_params=params(),
-        cost_estimate=cost(15),
+        cost_estimate=cost(100),
         name="steps_upper" if upper else "steps_lower",
     )(decay, gain, *sides, *arrays)
 
@@ -574,11 +593,10 @@
     edge = around(edge, "gz", 1)
     from_low, from_high = around(strips, "gy", 1), around(strips, "gy", -1)
     edge_low, edge_high = beyond(edge_strips, 1), beyond(edge_strips, -1)
-    own_u, up_u, down_u, own_l, up_l, down_l = pack(el, mg, mat)
-    strips, up_u, down_u, up_l, down_l = fill(
-        from_low, from_high, edge_low, edge_high, edge, [up_u, down_u, up_l, down_l]
-    )
+    own_u, up_u, down_u = pack(CUT, 10, el, mg, mat)
+    strips, up_u, down_u = fill(from_low, from_high, edge_low, edge_high, edge, [up_u, down_u])
     low_u, high_u = around(up_u, "gx", 1), around(down_u, "gx", -1)
+    own_l, up_l, down_l = pack(0, CUT, el, mg, mat, strips)
     low_l, high_l = around(up_l, "gx", 1), around(down_l, "gx", -1)
 
     sides = [strips, edge]
@@ -586,11 +604,12 @@
     top = lax.ppermute(plane, "gz", [(1, 0)])
     top = jnp.where(lax.axis_index("gz") == 1, plane, top)
     top = jnp.stack([top, around(top, "gy", 1), around(top, "gy", -1)])
+    top, low_l, high_l = lax.optimization_barrier((top, low_l, high_l))
     top = jnp.concatenate([around(top, "gx", 1), top, around(top, "gx", -1)], 2)
-    image = image_of(weights, top[0], top[1], top[2])
     (field,) = run_steps(
         False, decay, gain, sides, [own_u, low_u, high_u, own_l, low_l, high_l, field]
     )
+    image = image_of(weights, top[0], top[1], top[2])
     return (field.reshape(3, 80, 8, 128), image)
 
 

time: 114 us -> 110 us (0.965)
  waiting for transfers between devices: 19.1 us -> 17.3 us
  local copies, waits for them, and re-layouts: 4.74 us -> 3.36 us
    ppermute x11, waiting for transfers between devices: 17.2 us -> 10.7 us  [around(): lax.ppermute(value, axis, [(i, (i + steps) % count) for i in range(count)])]
    ppermute x1, waiting for transfers between devices: 1.56 us -> 6.59 us  [on_device(): top = lax.ppermute(plane, 'gz', [(1, 0)])]
    pallas_call x1 -> x2, Pallas kernels: 4.34 us -> 7.59 us  [pack(): pl.pallas_call(functools.partial(pack_kernel, first, last), out_shape=[ja...]
    pallas_call x2, Pallas kernels: 43.7 us -> 40.6 us  [run_steps(): pl.pallas_call(functools.partial(steps_kernel, upper), out_shape=out_shap...]
    unnamed x18 -> x16, local copies, waits for them, and re-layouts: 3.18 us -> 1.8 us
  transfers between devices with their start and end apart: 14 -> 14, of which waited for: 5 -> 4; matrix products, arithmetic and copies ran while one was open for 2% -> 2% of each run, Pallas kernels for 22% -> 45%
where the time goes in v3:
time: 110 us; the launch traced here: 108 us
  Pallas kernels  56.4 us (51%)
  starting transfers between devices  29.6 us (27%)
  waiting for transfers between devices  17.3 us (16%)
  local copies, waits for them, and re-layouts  3.36 us (3%)
    pallas_call x2, Pallas kernels, run_steps(): pl.pallas_call(functools.partial(steps_kernel, upper), out_shape=out_shap...  40.6 us
    ppermute x11, starting transfers between devices, around(): lax.ppermute(value, axis, [(i, (i + steps) % count) for i in range(count)])  23.3 us
    ppermute x11, waiting for transfers between devices, around(): lax.ppermute(value, axis, [(i, (i + steps) % count) for i in range(count)])  10.7 us
    pallas_call x2, Pallas kernels, pack(): pl.pallas_call(functools.partial(pack_kernel, first, last), out_shape=[ja...  7.59 us
    ppermute x1, waiting for transfers between devices, on_device(): top = lax.ppermute(plane, 'gz', [(1, 0)])  6.59 us
    ppermute x2, starting transfers between devices, beyond(): return lax.ppermute(value, ('gy', 'gz'), pairs)  4.14 us
    pallas_call x1, Pallas kernels, own_strips(): pl.pallas_call(strip_kernel, out_shape=[jax.ShapeDtypeStruct((8, 80, 128)...  3.61 us
    pallas_call x1, Pallas kernels, image_of(): pl.pallas_call(image_kernel, out_shape=jax.ShapeDtypeStruct((4, 128), jnp...  2.38 us
  transfers between devices with their start and end apart: 14, of which 4 were waited for; matrix products, arithmetic and copies ran while one was open for 2% of the time, Pallas kernels for 45%

profile of v3, /device:TPU:2, one launch (start us, length us, event | category | flops | bytes accessed | tf_op | source)
XLA Modules:
  0.0 108.1 jit_solution(2965208836930859891)
XLA Ops:
  0.6 3.6 %own_strips.1 = (f32[8,80,128]{2,1,0:T(8,128)}, f32[56,8,128]{2,1,0:T(8,128)}, f32[8,8,128]{2,1,0:T(8,128)}) custom-call(f32[3,640,128]{2,1,0:T(8,128)} %bitcast.22, f32[3,640,128]{2,1,0:T(8,128)} %bitcast.25, s32[640,128]{1,0:T(8,128)} %bitcast.28), custom_call_target="tpu_custom_call" | custom-call | flops 3000000000 | bytes 9000000 | tf_op jit(solution)/shard_map/own_strips/pallas_call | solution.py:105
  4.2 1.6 %collective-permute-start = (f32[8,80,128]{2,1,0:T(8,128)}, f32[8,80,128]{2,1,0:T(8,128)S(1)}, u32[]{:S(2)}, u32[]{:S(2)}) collective-permute-start(f32[8,80,128]{2,1,0:T(8,128)} %get-tuple-element.19), channel_id=1, source_target_pairs={{0,2},{2,4},{4,6},{6,0},{1,3},{3,5},{5,7},{7,1},{8,10},{10,12},{12... | collective-permute-start | bytes 983048 | tf_op jit(solution)/shard_map/ppermute | solution.py:28
  5.9 1.7 %collective-permute-start.1 = (f32[8,80,128]{2,1,0:T(8,128)}, f32[8,80,128]{2,1,0:T(8,128)S(1)}, u32[]{:S(2)}, u32[]{:S(2)}) collective-permute-start(f32[8,80,128]{2,1,0:T(8,128)} %get-tuple-element.19), channel_id=1, source_target_pairs={{0,6},{2,0},{4,2},{6,4},{1,7},{3,1},{5,3},{7,5},{8,14},{10,8},{12,... | collective-permute-start | bytes 983048 | tf_op jit(solution)/shard_map/ppermute | solution.py:28
  7.6 0.3 collective-permute-start.2
  7.9 3.8 %collective-permute-start.3 = (f32[8,8,128]{2,1,0:T(8,128)}, f32[8,8,128]{2,1,0:T(8,128)S(1)}, u32[]{:S(2)}, u32[]{:S(2)}) collective-permute-start(f32[8,8,128]{2,1,0:T(8,128)} %get-tuple-element.20), channel_id=1, source_target_pairs={{0,7},{1,6},{2,1},{3,0},{4,3},{5,2},{6,5},{7,4},{8,15},{9,14},{10,... | collective-permute-start | bytes 98312 | tf_op jit(solution)/shard_map/ppermute | solution.py:36
  11.7 0.5 collective-permute-start.4
  12.1 2.6 %pack_upper.1 = (f32[56,24,128]{2,1,0:T(8,128)}, f32[46,32,128]{2,1,0:T(8,128)}, f32[43,32,128]{2,1,0:T(8,128)}) custom-call(f32[3,640,128]{2,1,0:T(8,128)} %bitcast.23, f32[3,640,128]{2,1,0:T(8,128)} %bitcast.26, s32[640,128]{1,0:T(8,128)} %bitcast.29), custom_call_target="tpu_custom_call" | custom-call | flops 3000000000 | bytes 9000000 | tf_op jit(solution)/shard_map/pack_upper/pallas_call | solution.py:166
  14.8 0.0 collective-permute-done.2.edge_low
  14.8 0.0 copy-start.5
  14.8 0.0 collective-permute-done.3.edge_high
  14.8 0.0 copy-start.6
  14.8 3.8 %collective-permute-done.4.edge = f32[56,8,128]{2,1,0:T(8,128)S(1)} collective-permute-done((f32[56,8,128]{2,1,0:T(8,128)}, f32[56,8,128]{2,1,0:T(8,128)S(1)}, u32[]{:S(2)}, u32[]{:S(2)}) %collective-permute-start.4) | collective-permute-done | bytes 229408 | tf_op jit(solution)/shard_map/ppermute | solution.py:28
  18.6 0.0 copy-start.4
  18.6 0.0 collective-permute-done.from_low
  18.6 0.0 copy-start.2
  18.6 0.0 collective-permute-done.1.from_high
  18.6 0.0 copy-start.3
  18.6 0.0 copy-done.5
  18.6 0.0 copy-done.6
  18.7 0.7 copy-done.4
  19.3 0.1 copy-done.2
  19.5 0.1 copy-done.3
  19.6 2.2 %fill.1 = (f32[8,88,128]{2,1,0:T(8,128)}, f32[46,32,128]{2,1,0:T(8,128)}, f32[43,32,128]{2,1,0:T(8,128)}) custom-call(f32[8,80,128]{2,1,0:T(8,128)} %copy-done.2, f32[8,80,128]{2,1,0:T(8,128)} %copy-done.3, f32[8,8,128]{2,1,0:T(8,128)} %copy-done.5, f32[8,8,128]{2,1,0:T(8,128)} %copy-done.6, ...), custom_call_target="tpu_custom_call", output_to_operand_aliasing={{1}: (5, {}), {2}: (6, {})} | custom-call | flops 1000000000 | bytes 3000000 | tf_op jit(solution)/shard_map/fill/pallas_call | solution.py:211
  21.8 0.1 collective-permute-start.5
  21.9 5.3 %collective-permute-start.6 = (f32[43,32,128]{2,1,0:T(8,128)}, f32[43,32,128]{2,1,0:T(8,128)}, u32[]{:S(2)}, u32[]{:S(2)}) collective-permute-start(f32[43,32,128]{2,1,0:T(8,128)} %get-tuple-element.27), channel_id=1, source_target_pairs={{0,120},{8,0},{16,8},{24,16},{32,24},{40,32},{48,40},{56,48},{64,5... | collective-permute-start | bytes 2113544 | tf_op jit(solution)/shard_map/ppermute | solution.py:28
  27.2 5.0 %pack_lower.1 = (f32[56,56,128]{2,1,0:T(8,128)}, f32[46,56,128]{2,1,0:T(8,128)}, f32[43,56,128]{2,1,0:T(8,128)}) custom-call(f32[3,640,128]{2,1,0:T(8,128)} %bitcast.24, f32[3,640,128]{2,1,0:T(8,128)} %bitcast.27, s32[640,128]{1,0:T(8,128)} %bitcast.30, f32[8,88,128]{2,1,0:T(8,128)} %get-tuple-element.24.refs_0_.strips), custom_call_target="tpu_custom_call" | custom-call | flops 3000000000 | bytes 9000000 | tf_op jit(solution)/shard_map/pack_lower/pallas_call | solution.py:166
  32.2 0.1 collective-permute-start.10
  32.3 5.3 %collective-permute-start.11 = (f32[43,56,128]{2,1,0:T(8,128)}, f32[43,56,128]{2,1,0:T(8,128)}, u32[]{:S(2)}, u32[]{:S(2)}) collective-permute-start(f32[43,56,128]{2,1,0:T(8,128)} %get-tuple-element.31), channel_id=1, source_target_pairs={{0,120},{8,0},{16,8},{24,16},{32,24},{40,32},{48,40},{56,48},{64,5... | collective-permute-start | bytes 3698696 | tf_op jit(solution)/shard_map/ppermute | solution.py:28
  37.6 6.1 %collective-permute-done.6.refs_2_ = f32[43,32,128]{2,1,0:T(8,128)} collective-permute-done((f32[43,32,128]{2,1,0:T(8,128)}, f32[43,32,128]{2,1,0:T(8,128)}, u32[]{:S(2)}, u32[]{:S(2)}) %collective-permute-start.6) | collective-permute-done | bytes 704544 | tf_op jit(solution)/shard_map/ppermute | solution.py:28
  43.8 0.0 collective-permute-done.5.refs_1_
  43.8 0.0 copy-start.1
  43.8 0.9 copy-done.1
  44.6 0.0 copy-start
  44.6 14.4 %steps_upper.1 = (f32[3,640,128]{2,1,0:T(8,128)}, f32[2,8,128]{2,1,0:T(8,128)}) custom-call(f32[5]{0:T(128)} %decay.3, f32[5]{0:T(128)} %gain.3, f32[8,88,128]{2,1,0:T(8,128)} %get-tuple-element.24.refs_0_.strips, f32[56,8,128]{2,1,0:T(8,128)} %copy-done.4, f32[56,24,128]{2,1,0:T(8,128)} %get-tuple-element.25.refs_0_, f32[46,32,128]{2,1,0:T(8,128)} %copy-done.1, ...), custom_call_target="tpu_custom_call" | custom-call | flops 99999997952 | bytes 300000000 | tf_op jit(solution)/shard_map/steps_upper/pallas_call | solution.py:499
  59.1 2.2 %collective-permute-start.7 = (f32[2,8,128]{2,1,0:T(8,128)}, f32[2,8,128]{2,1,0:T(8,128)S(1)}, u32[]{:S(2)}, u32[]{:S(2)}) collective-permute-start(f32[2,8,128]{2,1,0:T(8,128)} %get-tuple-element.29), channel_id=1, source_target_pairs={{1,0},{3,2},{5,4},{7,6},{9,8},{11,10},{13,12},{15,14},{17,16},{19,... | collective-permute-start | bytes 24584 | tf_op jit(solution)/shard_map/ppermute | solution.py:604
  61.3 6.6 %collective-permute-done.7 = f32[2,8,128]{2,1,0:T(8,128)S(1)} collective-permute-done((f32[2,8,128]{2,1,0:T(8,128)}, f32[2,8,128]{2,1,0:T(8,128)S(1)}, u32[]{:S(2)}, u32[]{:S(2)}) %collective-permute-start.7) | collective-permute-done | bytes 8224 | tf_op jit(solution)/shard_map/ppermute | solution.py:604
  67.9 0.7 broadcast_select_fusion
  68.6 0.0 collective-permute-start.8
  68.6 3.2 %collective-permute-start.9 = (f32[2,8,128]{2,1,0:T(8,128)S(1)}, f32[2,8,128]{2,1,0:T(8,128)S(1)}, u32[]{:S(2)}, u32[]{:S(2)}) collective-permute-start(f32[2,8,128]{2,1,0:T(8,128)S(1)} %broadcast_select_fusion), channel_id=1, source_target_pairs={{0,6},{2,0},{4,2},{6,4},{1,7},{3,1},{5,3},{7,5},{8,14},{10,8},{12,... | collective-permute-start | bytes 24584 | tf_op jit(solution)/shard_map/ppermute | solution.py:28
  71.8 0.0 copy-done
  71.8 0.2 reshape.26
  72.0 0.7 copy.13.weights
  72.7 0.7 collective-permute-done.8
  73.4 0.0 collective-permute-done.9
  73.4 0.0 collective-permute-done.11.refs_5_
  73.4 0.0 collective-permute-done.10.refs_4_
  73.4 0.1 collective-permute-start.12
  73.5 5.3 %collective-permute-start.13 = (f32[3,2,8,128]{3,2,1,0:T(8,128)S(1)}, f32[3,2,8,128]{3,2,1,0:T(8,128)S(1)}, u32[]{:S(2)}, u32[]{:S(2)}) collective-permute-start(f32[3,2,8,128]{3,2,1,0:T(8,128)S(1)} %pad_maximum_fusion), channel_id=1, source_target_pairs={{0,120},{8,0},{16,8},{24,16},{32,24},{40,32},{48,40},{56,48},{64,5... | collective-permute-start | bytes 73736 | tf_op jit(solution)/shard_map/ppermute | solution.py:28
  78.9 26.2 %steps_lower.1 = f32[3,640,128]{2,1,0:T(8,128)} custom-call(f32[5]{0:T(128)} %decay.3, f32[5]{0:T(128)} %gain.3, f32[8,88,128]{2,1,0:T(8,128)} %get-tuple-element.24.refs_0_.strips, f32[56,8,128]{2,1,0:T(8,128)} %copy-done.4, f32[56,24,128]{2,1,0:T(8,128)} %get-tuple-element.25.refs_0_, f32[46,32,128]{2,1,0:T(8,128)} %copy-done.1, ...), custom_call_target="tpu_custom_call", output_to_operand_aliasing={{}: (10, {})} | custom-call | flops 99999997952 | bytes 300000000 | tf_op jit(solution)/shard_map/steps_lower/pallas_call | solution.py:499
  105.1 0.0 collective-permute-done.12
  105.1 0.0 collective-permute-done.13
  105.1 0.6 slice_bitcast_fusion
  105.7 2.4 %image.1 = f32[4,128]{1,0:T(4,128)} custom-call(f32[48,240]{1,0:T(8,128)} %copy.13.weights, f32[2,24,128]{2,1,0:T(8,128)} %get-tuple-element.38.centre, f32[2,24,128]{2,1,0:T(8,128)} %get-tuple-element.37.before, f32[2,24,128]{2,1,0:T(8,128)} %get-tuple-element.36.after), custom_call_target="tpu_custom_call" | custom-call | tf_op jit(solution)/shard_map/image/pallas_call | solution.py:570
  (6 shorter events, 0.1 us)
Async XLA Ops:
  4.2 14.4 %collective-permute-start = (f32[8,80,128]{2,1,0:T(8,128)}, f32[8,80,128]{2,1,0:T(8,128)S(1)}, u32[]{:S(2)}, u32[]{:S(2)}) collective-permute-start(f32[8,80,128]{2,1,0:T(8,128)} %get-tuple-element.19), channel_id=1, source_target_pairs={{0,2},{2,4},{4,6},{6,0},{1,3},{3,5},{5,7},{7,1},{8,10},{10,12},{12... | collective-permute-start | bytes 983048 | tf_op jit(solution)/shard_map/ppermute | solution.py:28
  5.9 12.7 %collective-permute-start.1 = (f32[8,80,128]{2,1,0:T(8,128)}, f32[8,80,128]{2,1,0:T(8,128)S(1)}, u32[]{:S(2)}, u32[]{:S(2)}) collective-permute-start(f32[8,80,128]{2,1,0:T(8,128)} %get-tuple-element.19), channel_id=1, source_target_pairs={{0,6},{2,0},{4,2},{6,4},{1,7},{3,1},{5,3},{7,5},{8,14},{10,8},{12,... | collective-permute-start | bytes 983048 | tf_op jit(solution)/shard_map/ppermute | solution.py:28
  7.6 7.2 %collective-permute-start.2 = (f32[8,8,128]{2,1,0:T(8,128)}, f32[8,8,128]{2,1,0:T(8,128)S(1)}, u32[]{:S(2)}, u32[]{:S(2)}) collective-permute-start(f32[8,8,128]{2,1,0:T(8,128)} %get-tuple-element.20), channel_id=1, source_target_pairs={{0,3},{1,2},{2,5},{3,4},{4,7},{5,6},{6,1},{7,0},{8,11},{9,10},{10,... | collective-permute-start | bytes 98312 | tf_op jit(solution)/shard_map/ppermute | solution.py:36
  7.9 6.9 %collective-permute-start.3 = (f32[8,8,128]{2,1,0:T(8,128)}, f32[8,8,128]{2,1,0:T(8,128)S(1)}, u32[]{:S(2)}, u32[]{:S(2)}) collective-permute-start(f32[8,8,128]{2,1,0:T(8,128)} %get-tuple-element.20), channel_id=1, source_target_pairs={{0,7},{1,6},{2,1},{3,0},{4,3},{5,2},{6,5},{7,4},{8,15},{9,14},{10,... | collective-permute-start | bytes 98312 | tf_op jit(solution)/shard_map/ppermute | solution.py:36
  11.7 6.9 %collective-permute-start.4 = (f32[56,8,128]{2,1,0:T(8,128)}, f32[56,8,128]{2,1,0:T(8,128)S(1)}, u32[]{:S(2)}, u32[]{:S(2)}) collective-permute-start(f32[56,8,128]{2,1,0:T(8,128)} %get-tuple-element.21), channel_id=1, source_target_pairs={{0,1},{1,0},{2,3},{3,2},{4,5},{5,4},{6,7},{7,6},{8,9},{9,8},{10,11... | collective-permute-start | bytes 688136 | tf_op jit(solution)/shard_map/ppermute | solution.py:28
  14.8 3.9 %copy-start.5 = (f32[8,8,128]{2,1,0:T(8,128)}, f32[8,8,128]{2,1,0:T(8,128)S(1)}, u32[]{:S(2)}) copy-start(f32[8,8,128]{2,1,0:T(8,128)S(1)} %collective-permute-done.2.edge_low) | copy-start | bytes 98308
  14.8 3.9 %copy-start.6 = (f32[8,8,128]{2,1,0:T(8,128)}, f32[8,8,128]{2,1,0:T(8,128)S(1)}, u32[]{:S(2)}) copy-start(f32[8,8,128]{2,1,0:T(8,128)S(1)} %collective-permute-done.3.edge_high) | copy-start | bytes 98308
  18.6 0.7 copy-start.4
  18.6 0.8 copy-start.2
  18.6 0.9 copy-start.3
  21.8 22.0 %collective-permute-start.5 = (f32[46,32,128]{2,1,0:T(8,128)}, f32[46,32,128]{2,1,0:T(8,128)S(1)}, u32[]{:S(2)}, u32[]{:S(2)}) collective-permute-start(f32[46,32,128]{2,1,0:T(8,128)} %get-tuple-element.26), channel_id=1, source_target_pairs={{0,8},{8,16},{16,24},{24,32},{32,40},{40,48},{48,56},{56,64},{64,7... | collective-permute-start | bytes 2261000 | tf_op jit(solution)/shard_map/ppermute | solution.py:28
  21.9 21.9 %collective-permute-start.6 = (f32[43,32,128]{2,1,0:T(8,128)}, f32[43,32,128]{2,1,0:T(8,128)}, u32[]{:S(2)}, u32[]{:S(2)}) collective-permute-start(f32[43,32,128]{2,1,0:T(8,128)} %get-tuple-element.27), channel_id=1, source_target_pairs={{0,120},{8,0},{16,8},{24,16},{32,24},{40,32},{48,40},{56,48},{64,5... | collective-permute-start | bytes 2113544 | tf_op jit(solution)/shard_map/ppermute | solution.py:28
  32.2 41.2 %collective-permute-start.10 = (f32[46,56,128]{2,1,0:T(8,128)}, f32[46,56,128]{2,1,0:T(8,128)}, u32[]{:S(2)}, u32[]{:S(2)}) collective-permute-start(f32[46,56,128]{2,1,0:T(8,128)} %get-tuple-element.30), channel_id=1, source_target_pairs={{0,8},{8,16},{16,24},{24,32},{32,40},{40,48},{48,56},{56,64},{64,7... | collective-permute-start | bytes 3956744 | tf_op jit(solution)/shard_map/ppermute | solution.py:28
  32.3 41.1 %collective-permute-start.11 = (f32[43,56,128]{2,1,0:T(8,128)}, f32[43,56,128]{2,1,0:T(8,128)}, u32[]{:S(2)}, u32[]{:S(2)}) collective-permute-start(f32[43,56,128]{2,1,0:T(8,128)} %get-tuple-element.31), channel_id=1, source_target_pairs={{0,120},{8,0},{16,8},{24,16},{32,24},{40,32},{48,40},{56,48},{64,5... | collective-permute-start | bytes 3698696 | tf_op jit(solution)/shard_map/ppermute | solution.py:28
  43.8 0.9 copy-start.1
  44.6 27.2 %copy-start = (f32[2,24,15,15]{1,0,3,2:T(2,128)S(1)}, f32[2,24,15,15]{1,0,3,2:T(2,128)}, u32[]{:S(2)}) copy-start(f32[2,24,15,15]{1,0,3,2:T(2,128)} %param.11) | copy-start | bytes 129604
  59.1 8.8 %collective-permute-start.7 = (f32[2,8,128]{2,1,0:T(8,128)}, f32[2,8,128]{2,1,0:T(8,128)S(1)}, u32[]{:S(2)}, u32[]{:S(2)}) collective-permute-start(f32[2,8,128]{2,1,0:T(8,128)} %get-tuple-element.29), channel_id=1, source_target_pairs={{1,0},{3,2},{5,4},{7,6},{9,8},{11,10},{13,12},{15,14},{17,16},{19,... | collective-permute-start | bytes 24584 | tf_op jit(solution)/shard_map/ppermute | solution.py:604
  68.6 4.9 %collective-permute-start.8 = (f32[2,8,128]{2,1,0:T(8,128)S(1)}, f32[2,8,128]{2,1,0:T(8,128)S(1)}, u32[]{:S(2)}, u32[]{:S(2)}) collective-permute-start(f32[2,8,128]{2,1,0:T(8,128)S(1)} %broadcast_select_fusion), channel_id=1, source_target_pairs={{0,2},{2,4},{4,6},{6,0},{1,3},{3,5},{5,7},{7,1},{8,10},{10,12},{12... | collective-permute-start | bytes 24584 | tf_op jit(solution)/shard_map/ppermute | solution.py:28
  68.6 4.9 %collective-permute-start.9 = (f32[2,8,128]{2,1,0:T(8,128)S(1)}, f32[2,8,128]{2,1,0:T(8,128)S(1)}, u32[]{:S(2)}, u32[]{:S(2)}) collective-permute-start(f32[2,8,128]{2,1,0:T(8,128)S(1)} %broadcast_select_fusion), channel_id=1, source_target_pairs={{0,6},{2,0},{4,2},{6,4},{1,7},{3,1},{5,3},{7,5},{8,14},{10,8},{12,... | collective-permute-start | bytes 24584 | tf_op jit(solution)/shard_map/ppermute | solution.py:28
  73.4 31.6 %collective-permute-start.12 = (f32[3,2,8,128]{3,2,1,0:T(8,128)S(1)}, f32[3,2,8,128]{3,2,1,0:T(8,128)S(1)}, u32[]{:S(2)}, u32[]{:S(2)}) collective-permute-start(f32[3,2,8,128]{3,2,1,0:T(8,128)S(1)} %pad_maximum_fusion), channel_id=1, source_target_pairs={{0,8},{8,16},{16,24},{24,32},{32,40},{40,48},{48,56},{56,64},{64,7... | collective-permute-start | bytes 73736 | tf_op jit(solution)/shard_map/ppermute | solution.py:28
  73.5 31.6 %collective-permute-start.13 = (f32[3,2,8,128]{3,2,1,0:T(8,128)S(1)}, f32[3,2,8,128]{3,2,1,0:T(8,128)S(1)}, u32[]{:S(2)}, u32[]{:S(2)}) collective-permute-start(f32[3,2,8,128]{3,2,1,0:T(8,128)S(1)} %pad_maximum_fusion), channel_id=1, source_target_pairs={{0,120},{8,0},{16,8},{24,16},{32,24},{40,32},{48,40},{56,48},{64,5... | collective-permute-start | bytes 73736 | tf_op jit(solution)/shard_map/ppermute | solution.py:28

commit v4 on v3

--- a/solution.py
+++ b/solution.py
@@ -16,6 +16,7 @@
 BASE = 4
 HELD = BASE + ROWS + 2
 CUT = 7
+HIGH = 11 - CUT
 LAG = 4
 VMEM = 63 * 1024 * 1024
 F32 = jnp.float32
@@ -162,13 +163,13 @@
 
 def pack(first, last, el, mg, mat, *strips):
     layers = 8 * (last - first)
-    sent = layers + 8 if first else layers
+    more = 0 if first else W
     return pl.pallas_call(
         functools.partial(pack_kernel, first, last),
         out_shape=[
             jax.ShapeDtypeStruct((8 * NC, layers, 128), F32),
-            jax.ShapeDtypeStruct((40 + W, sent, 128), F32),
-            jax.ShapeDtypeStruct((37 + W, sent, 128), F32),
+            jax.ShapeDtypeStruct((40 + more, layers, 128), F32),
+            jax.ShapeDtypeStruct((37 + more, layers, 128), F32),
         ],
         in_specs=[HBM] * 3 + [LOCAL] * len(strips),
         out_specs=[HBM] * 3,
@@ -179,49 +180,44 @@
             pltpu.SemaphoreType.DMA((10,)),
         ],
         compiler_params=params(),
-        cost_estimate=cost(3),
+        cost_estimate=cost(20 if first else 3),
         name="pack_upper" if first else "pack_lower",
     )(el, mg, mat, *strips)
 
 
-def fill_kernel(from_low, from_high, edge_low, edge_high, edge, *refs):
-    strips, up_u, down_u, halo, sems = refs[2:]
+def corner_kernel(from_low, from_high, edge_low, edge_high, edge, strips, up, down):
     lane = lax.broadcasted_iota(jnp.int32, (8, 80, 128), 2)
-    halo[:, 0:80, :] = jnp.where(lane % 16 < 8, from_high[...], from_low[...])
+    strips[:, 0:80, :] = jnp.where(lane % 16 < 8, from_high[...], from_low[...])
     lane = lax.broadcasted_iota(jnp.int32, (8, 8, 128), 2)
-    halo[:, 80:88, :] = jnp.where(lane % 16 < 8, edge_high[...], edge_low[...])
-    nu, nl = 8 * (10 - CUT), 8 * CUT
-    pairs = [(halo, strips)]
-    for message, first, count, parts in (
-        (up_u, 8 - W, 40, ((6, 0, 18), (30, 18, 2), (33, 20, 15), (51, 35, 5))),
-        (down_u, 0, 37, ((0, 0, 17), (24, 17, 15), (48, 32, 5))),
-    ):
-        rows = pl.ds(first, W)
-        pairs.append(
-            (halo.at[rows, pl.ds(nl, nu + 8)], message.at[pl.ds(count, W), pl.ds(0, nu + 8)])
-        )
-        for a, b, n in parts:
-            pairs.append((edge.at[pl.ds(a, n)], message.at[pl.ds(b, n), pl.ds(nu, 8)]))
-    copy_all(pairs, sems)
-
-
-def fill(from_low, from_high, edge_low, edge_high, edge, messages):
-    shapes = [jax.ShapeDtypeStruct((8, 88, 128), F32)]
-    shapes += [jax.ShapeDtypeStruct(m.shape, F32) for m in messages]
+    strips[:, 80:88, :] = jnp.where(lane % 16 < 8, edge_high[...], edge_low[...])
+    for a, b, n in ((6, 0, 18), (30, 18, 2), (33, 20, 15), (51, 35, 5)):
+        up[b : b + n] = edge[a : a + n]
+    for a, b, n in ((0, 0, 17), (24, 17, 15), (48, 32, 5)):
+        down[b : b + n] = edge[a : a + n]
+    for r in range(W):
+        for t in range(HIGH):
+            z = 8 * (CUT + t)
+            up[40 + HIGH * r + t] = strips[8 - W + r, z : z + 8, :]
+            down[37 + HIGH * r + t] = strips[r, z : z + 8, :]
+
+
+def corners(from_low, from_high, edge_low, edge_high, edge):
     return pl.pallas_call(
-        fill_kernel,
-        out_shape=shapes,
-        in_specs=[LOCAL] * 5 + [HBM] * 2,
-        out_specs=[HBM] * 3,
-        scratch_shapes=[pltpu.VMEM((8, 88, 128), F32), pltpu.SemaphoreType.DMA((10,))],
-        input_output_aliases={5: 1, 6: 2},
+        corner_kernel,
+        out_shape=[
+            jax.ShapeDtypeStruct((8, 88, 128), F32),
+            jax.ShapeDtypeStruct((40 + W * HIGH, 8, 128), F32),
+            jax.ShapeDtypeStruct((37 + W * HIGH, 8, 128), F32),
+        ],
+        in_specs=[LOCAL] * 5,
+        out_specs=[LOCAL] * 3,
         compiler_params=params(),
         cost_estimate=cost(1),
-        name="fill",
-    )(from_low, from_high, edge_low, edge_high, edge, *messages)
-
-
-def steps_kernel(upper, decay, gain, strips, edge, *refs):
+        name="corners",
+    )(from_low, from_high, edge_low, edge_high, edge)
+
+
+def steps_kernel(upper, decay, gain, low_c, high_c, strips, edge, *refs):
     gz = lax.axis_index("gz")
     nu, nl = 8 * (10 - CUT), 8 * CUT
     own_u, low_u, high_u = refs[:3]
@@ -237,41 +233,51 @@
             ((own_u, low_u, high_u), 0, 16, 8 + nl, nl),
         ]
     on = 9 - CUT if upper else CUT + 1
-    sets.append(((edge, low_u, high_u), nu, 8, 8 * halo, 80))
     ea0, ea1, eb0, eb1, ma0, ma1, mb0, mb1, d0, d1, g0, g1, ya, yb, ym, sv, stage, sems = scratch
     es, ms, yes = ((ea0, ea1), (eb0, eb1)), ((ma0, ma1), (mb0, mb1)), (ya, yb)
     ds_, gs = (d0, d1), (g0, g1)
 
     first, mid, last_ = BASE, BASE + W, BASE + W + 8
-    groups = []
+    hz = 8 * halo
+    moves = [(strips.at[:, pl.ds(80, 8)], sv.at[pl.ds(W, 8), pl.ds(hz, 8)])]
     for (own, low, high), start, layers, to, strip in sets:
-        src, zf, zd = pl.ds(start, layers), pl.ds(8 + to, layers), pl.ds(to, layers)
-        mine = pl.ds(0, 8) if own is edge else src
-        moves = [
-            (strips.at[:, pl.ds(strip, layers)], sv.at[pl.ds(W, 8), zd]),
-            (low.at[pl.ds(40, W), src], sv.at[pl.ds(0, W), zd]),
-            (high.at[pl.ds(37, W), src], sv.at[pl.ds(W + 8, W), zd]),
-        ]
-        for ref, a, n, dst, b, z in (
-            (own, 0, 24, ea0, 3 * mid, zf),
-            (own, 24, 24, ma0, 3 * mid, zf),
-            (own, 48, 8, d0, mid, zd),
-            (low, 0, 18, ea0, 3 * first, zf),
-            (low, 18, 2, ma0, 3 * first, zf),
-            (low, 20, 15, ma0, 3 * first + 3, zf),
-            (low, 35, 5, d0, first + 1, zd),
-            (high, 0, 17, ea0, 3 * last_, zf),
-            (high, 17, 15, ma0, 3 * last_, zf),
-            (high, 32, 5, d0, last_, zd),
-        ):
-            moves.append((ref.at[pl.ds(a, n), mine if ref is own else src], dst.at[pl.ds(b, n), z]))
-        groups.append(moves)
-    copies = []
-    for moves in groups:
-        for a, b in moves:
-            copies.append(pltpu.make_async_copy(a, b, sems.at[len(copies)]))
+        zd = pl.ds(to, layers)
+        moves.append((strips.at[:, pl.ds(strip, layers)], sv.at[pl.ds(W, 8), zd]))
+        if not upper and own is own_l:
+            moves.append((low.at[pl.ds(40, W)], sv.at[pl.ds(0, W), zd]))
+            moves.append((high.at[pl.ds(37, W)], sv.at[pl.ds(W + 8, W), zd]))
+    early = len(moves)
+    own_parts = ((0, 24, ea0, 3 * mid), (24, 24, ma0, 3 * mid), (48, 8, d0, mid))
+    low_parts = (
+        (0, 18, ea0, 3 * first),
+        (18, 2, ma0, 3 * first),
+        (20, 15, ma0, 3 * first + 3),
+        (35, 5, d0, first + 1),
+    )
+    high_parts = ((0, 17, ea0, 3 * last_), (17, 15, ma0, 3 * last_), (32, 5, d0, last_))
+    for (own, low, high), start, layers, to, strip in sets:
+        for ref, parts in ((own, own_parts), (low, low_parts), (high, high_parts)):
+            for a, n, dst, b in parts:
+                z = pl.ds(to if dst is d0 else 8 + to, layers)
+                moves.append((ref.at[pl.ds(a, n), pl.ds(start, layers)], dst.at[pl.ds(b, n), z]))
+    for a, n, dst, b in own_parts:
+        z = pl.ds(hz if dst is d0 else 8 + hz, 8)
+        moves.append((edge.at[pl.ds(a, n)], dst.at[pl.ds(b, n), z]))
+    copies = [pltpu.make_async_copy(a, b, sems.at[i]) for i, (a, b) in enumerate(moves)]
     for copy in copies:
         copy.start()
+    for ref, parts in ((low_c, low_parts), (high_c, high_parts)):
+        for a, n, dst, b in parts:
+            z = hz if dst is d0 else 8 + hz
+            for i in range(n):
+                dst[b + i, z : z + 8, :] = ref[a + i]
+    here = [(t, t) for t in range(HIGH)]
+    if not upper:
+        here = [(0, HIGH - 1), (CUT + 1, 0), (CUT + 2, 1)]
+    for r in range(W):
+        for t, u in here:
+            sv[r, 8 * t : 8 * t + 8, :] = low_c[40 + HIGH * r + u]
+            sv[W + 8 + r, 8 * t : 8 * t + 8, :] = high_c[37 + HIGH * r + u]
 
     zero = jnp.zeros((8, 128), F32)
     top = 8 + 8 * tiles
@@ -288,9 +294,8 @@
         return 0
 
     lax.fori_loop(0, HELD, ends, 0)
-    strip_copies = [i for g in range(len(groups)) for i in range(13 * g, 13 * g + 3)]
-    for i in strip_copies:
-        copies[i].wait()
+    for copy in copies[:early]:
+        copy.wait()
 
     def unpack(r, _):
         at = BASE + r
@@ -308,10 +313,8 @@
         return 0
 
     lax.fori_loop(0, ROWS, unpack, 0)
-    for i, copy in enumerate(copies):
-        if i not in strip_copies:
-            copy.wait()
-    hz = 8 * halo
+    for copy in copies[early:]:
+        copy.wait()
 
     @pl.when(jnp.logical_not(counts))
     def _():
@@ -490,7 +493,7 @@
         out_shape.append(jax.ShapeDtypeStruct((2, 8, 128), F32))
         out_specs.append(LOCAL)
     else:
-        aliases = {4 + len(arrays) - 1: 0}
+        aliases = {6 + len(arrays) - 1: 0}
     tiles, on = (11 - CUT, 9 - CUT) if upper else (CUT + 3, CUT + 1)
     z = 16 + 8 * tiles
     field = pltpu.VMEM((3 * HELD, z, 128), F32)
@@ -499,7 +502,7 @@
     return pl.pallas_call(
         functools.partial(steps_kernel, upper),
         out_shape=out_shape,
-        in_specs=[smem, smem] + [HBM] * (2 + len(arrays)),
+        in_specs=[smem, smem, LOCAL, LOCAL] + [HBM] * (2 + len(arrays)),
         out_specs=out_specs,
         scratch_shapes=[field] * 8
         + [table] * 4
@@ -594,16 +597,19 @@
     from_low, from_high = around(strips, "gy", 1), around(strips, "gy", -1)
     edge_low, edge_high = beyond(edge_strips, 1), beyond(edge_strips, -1)
     own_u, up_u, down_u = pack(CUT, 10, el, mg, mat)
-    strips, up_u, down_u = fill(from_low, from_high, edge_low, edge_high, edge, [up_u, down_u])
+    up_u, down_u, edge_low, edge_high = lax.optimization_barrier(
+        (up_u, down_u, edge_low, edge_high)
+    )
     low_u, high_u = around(up_u, "gx", 1), around(down_u, "gx", -1)
+    strips, up_c, down_c = corners(from_low, from_high, edge_low, edge_high, edge)
+    low_c, high_c = around(up_c, "gx", 1), around(down_c, "gx", -1)
     own_l, up_l, down_l = pack(0, CUT, el, mg, mat, strips)
     low_l, high_l = around(up_l, "gx", 1), around(down_l, "gx", -1)
 
-    sides = [strips, edge]
+    sides = [low_c, high_c, strips, edge]
     field, plane = run_steps(True, decay, gain, sides, [own_u, low_u, high_u])
-    top = lax.ppermute(plane, "gz", [(1, 0)])
-    top = jnp.where(lax.axis_index("gz") == 1, plane, top)
-    top = jnp.stack([top, around(top, "gy", 1), around(top, "gy", -1)])
+    top = jnp.stack([plane, around(plane, "gy", 1), around(plane, "gy", -1)])
+    top = jnp.where(lax.axis_index("gz") == 1, top, lax.ppermute(top, "gz", [(1, 0)]))
     top, low_l, high_l = lax.optimization_barrier((top, low_l, high_l))
     top = jnp.concatenate([around(top, "gx", 1), top, around(top, "gx", -1)], 2)
     (field,) = run_steps(

time: 110 us -> 103 us (0.936)
  waiting for transfers between devices: 17.3 us -> 5.38 us
  starting transfers between devices: 29.6 us -> 35.8 us
  Pallas kernels: 56.4 us -> 55.1 us
    ppermute x1, waiting for transfers between devices: 6.59 us -> 0.54 us  [on_device(): lax.ppermute(top, 'gz', [(1, 0)])]
    ppermute x11 -> x13, waiting for transfers between devices: 10.7 us -> 4.83 us  [around(): lax.ppermute(value, axis, [(i, (i + steps) % count) for i in range(count)])]
    ppermute x11 -> x13, starting transfers between devices: 23.3 us -> 28.5 us  [around(): lax.ppermute(value, axis, [(i, (i + steps) % count) for i in range(count)])]
    pallas_call x2, Pallas kernels: 40.6 us -> 39.3 us  [run_steps(): pl.pallas_call(functools.partial(steps_kernel, upper), out_shape=out_shap...]
  transfers between devices with their start and end apart: 14 -> 16, of which waited for: 4 -> 3; matrix products, arithmetic and copies ran while one was open for 2% -> 2% of each run, Pallas kernels for 45% -> 48%
where the time goes in v4:
time: 103 us; the launch traced here: 101 us
  Pallas kernels  55.1 us (53%)
  starting transfers between devices  35.8 us (35%)
  waiting for transfers between devices  5.38 us (5%)
  local copies, waits for them, and re-layouts  2.94 us (3%)
  other arithmetic  1.4 us (1%)
    pallas_call x2, Pallas kernels, run_steps(): pl.pallas_call(functools.partial(steps_kernel, upper), out_shape=out_shap...  39.3 us
    ppermute x13, starting transfers between devices, around(): lax.ppermute(value, axis, [(i, (i + steps) % count) for i in range(count)])  28.5 us
    pallas_call x2, Pallas kernels, pack(): pl.pallas_call(functools.partial(pack_kernel, first, last), out_shape=[ja...  7.66 us
    ppermute x13, waiting for transfers between devices, around(): lax.ppermute(value, axis, [(i, (i + steps) % count) for i in range(count)])  4.83 us
    ppermute x2, starting transfers between devices, beyond(): return lax.ppermute(value, ('gy', 'gz'), pairs)  4.2 us
    pallas_call x1, Pallas kernels, own_strips(): pl.pallas_call(strip_kernel, out_shape=[jax.ShapeDtypeStruct((8, 80, 128)...  3.61 us
    ppermute x1, starting transfers between devices, on_device(): lax.ppermute(top, 'gz', [(1, 0)])  3.12 us
    pallas_call x1, Pallas kernels, image_of(): pl.pallas_call(image_kernel, out_shape=jax.ShapeDtypeStruct((4, 128), jnp...  2.38 us
  transfers between devices with their start and end apart: 16, of which 3 were waited for; matrix products, arithmetic and copies ran while one was open for 2% of the time, Pallas kernels for 48%

profile of v4, /device:TPU:2, one launch (start us, length us, event | category | flops | bytes accessed | tf_op | source)
XLA Modules:
  0.0 101.4 jit_solution(8283073649408422457)
XLA Ops:
  0.6 3.6 %own_strips.1 = (f32[8,80,128]{2,1,0:T(8,128)}, f32[56,8,128]{2,1,0:T(8,128)}, f32[8,8,128]{2,1,0:T(8,128)}) custom-call(f32[3,640,128]{2,1,0:T(8,128)} %bitcast.25, f32[3,640,128]{2,1,0:T(8,128)} %bitcast.28, s32[640,128]{1,0:T(8,128)} %bitcast.31), custom_call_target="tpu_custom_call" | custom-call | flops 3000000000 | bytes 9000000 | tf_op jit(solution)/shard_map/own_strips/pallas_call | solution.py:106
  4.2 1.6 %collective-permute-start.2 = (f32[8,8,128]{2,1,0:T(8,128)}, f32[8,8,128]{2,1,0:T(8,128)S(1)}, u32[]{:S(2)}, u32[]{:S(2)}) collective-permute-start(f32[8,8,128]{2,1,0:T(8,128)} %get-tuple-element.26), channel_id=1, source_target_pairs={{0,3},{1,2},{2,5},{3,4},{4,7},{5,6},{6,1},{7,0},{8,11},{9,10},{10,... | collective-permute-start | bytes 98312 | tf_op jit(solution)/shard_map/ppermute | solution.py:37
  5.9 2.6 %collective-permute-start.3 = (f32[8,8,128]{2,1,0:T(8,128)}, f32[8,8,128]{2,1,0:T(8,128)S(1)}, u32[]{:S(2)}, u32[]{:S(2)}) collective-permute-start(f32[8,8,128]{2,1,0:T(8,128)} %get-tuple-element.26), channel_id=1, source_target_pairs={{0,7},{1,6},{2,1},{3,0},{4,3},{5,2},{6,5},{7,4},{8,15},{9,14},{10,... | collective-permute-start | bytes 98312 | tf_op jit(solution)/shard_map/ppermute | solution.py:37
  8.4 0.4 collective-permute-start
  8.8 2.9 %collective-permute-start.1 = (f32[8,80,128]{2,1,0:T(8,128)}, f32[8,80,128]{2,1,0:T(8,128)}, u32[]{:S(2)}, u32[]{:S(2)}) collective-permute-start(f32[8,80,128]{2,1,0:T(8,128)} %get-tuple-element.23), channel_id=1, source_target_pairs={{0,6},{2,0},{4,2},{6,4},{1,7},{3,1},{5,3},{7,5},{8,14},{10,8},{12,... | collective-permute-start | bytes 983048 | tf_op jit(solution)/shard_map/ppermute | solution.py:29
  11.7 0.5 collective-permute-start.4
  12.1 2.6 %pack_upper.1 = (f32[56,24,128]{2,1,0:T(8,128)}, f32[40,24,128]{2,1,0:T(8,128)}, f32[37,24,128]{2,1,0:T(8,128)}) custom-call(f32[3,640,128]{2,1,0:T(8,128)} %bitcast.26, f32[3,640,128]{2,1,0:T(8,128)} %bitcast.29, s32[640,128]{1,0:T(8,128)} %bitcast.32), custom_call_target="tpu_custom_call" | custom-call | flops 20000000000 | bytes 60000000 | tf_op jit(solution)/shard_map/pack_upper/pallas_call | solution.py:167
  14.8 0.0 collective-permute-done.2.edge_low
  14.8 0.0 copy-start.3
  14.8 0.0 collective-permute-done.3.edge_high
  14.8 0.0 copy-start.4
  14.8 0.6 copy-done.4
  15.4 0.0 collective-permute-start.7
  15.4 5.4 %collective-permute-start.8 = (f32[37,24,128]{2,1,0:T(8,128)}, f32[37,24,128]{2,1,0:T(8,128)S(1)}, u32[]{:S(2)}, u32[]{:S(2)}) collective-permute-start(f32[37,24,128]{2,1,0:T(8,128)} %get-tuple-element.35), channel_id=1, source_target_pairs={{0,120},{8,0},{16,8},{24,16},{32,24},{40,32},{48,40},{56,48},{64,5... | collective-permute-start | bytes 1363976 | tf_op jit(solution)/shard_map/ppermute | solution.py:29
  20.8 0.0 collective-permute-done.4.edge
  20.8 0.0 collective-permute-done.from_low
  20.8 0.0 collective-permute-done.1.from_high
  20.8 0.0 copy-done.3
  20.8 2.1 %corners.1 = (f32[8,88,128]{2,1,0:T(8,128)}, f32[64,8,128]{2,1,0:T(8,128)}, f32[61,8,128]{2,1,0:T(8,128)}) custom-call(f32[8,80,128]{2,1,0:T(8,128)} %collective-permute-done.from_low, f32[8,80,128]{2,1,0:T(8,128)} %collective-permute-done.1.from_high, f32[8,8,128]{2,1,0:T(8,128)} %copy-done.3, f32[8,8,128]{2,1,0:T(8,128)} %copy-done.4, ...), custom_call_target="tpu_custom_call" | custom-call | flops 1000000000 | bytes 3000000 | tf_op jit(solution)/shard_map/corners/pallas_call | solution.py:205
  22.9 0.0 collective-permute-start.5
  22.9 5.4 %collective-permute-start.6 = (f32[61,8,128]{2,1,0:T(8,128)}, f32[61,8,128]{2,1,0:T(8,128)}, u32[]{:S(2)}, u32[]{:S(2)}) collective-permute-start(f32[61,8,128]{2,1,0:T(8,128)} %get-tuple-element.31), channel_id=1, source_target_pairs={{0,120},{8,0},{16,8},{24,16},{32,24},{40,32},{48,40},{56,48},{64,5... | collective-permute-start | bytes 749576 | tf_op jit(solution)/shard_map/ppermute | solution.py:29
  28.3 5.0 %pack_lower.1 = (f32[56,56,128]{2,1,0:T(8,128)}, f32[46,56,128]{2,1,0:T(8,128)}, f32[43,56,128]{2,1,0:T(8,128)}) custom-call(f32[3,640,128]{2,1,0:T(8,128)} %bitcast.27, f32[3,640,128]{2,1,0:T(8,128)} %bitcast.30, s32[640,128]{1,0:T(8,128)} %bitcast.33, f32[8,88,128]{2,1,0:T(8,128)} %get-tuple-element.32.refs_0_.strips), custom_call_target="tpu_custom_call" | custom-call | flops 3000000000 | bytes 9000000 | tf_op jit(solution)/shard_map/pack_lower/pallas_call | solution.py:167
  33.3 0.1 collective-permute-start.12
  33.4 0.0 collective-permute-done.8.refs_2_
  33.4 0.0 copy-start.2
  33.4 5.3 %collective-permute-start.13 = (f32[43,56,128]{2,1,0:T(8,128)}, f32[43,56,128]{2,1,0:T(8,128)}, u32[]{:S(2)}, u32[]{:S(2)}) collective-permute-start(f32[43,56,128]{2,1,0:T(8,128)} %get-tuple-element.39), channel_id=1, source_target_pairs={{0,120},{8,0},{16,8},{24,16},{32,24},{40,32},{48,40},{56,48},{64,5... | collective-permute-start | bytes 3698696 | tf_op jit(solution)/shard_map/ppermute | solution.py:29
  38.8 0.0 collective-permute-done.7.refs_1_
  38.8 0.0 copy-start.1
  38.8 0.0 collective-permute-done.6.high_c
  38.8 0.0 collective-permute-done.5.low_c
  38.8 0.0 copy-done.2
  38.8 0.8 copy-done.1
  39.6 0.0 copy-start
  39.6 14.2 %steps_upper.1 = (f32[3,640,128]{2,1,0:T(8,128)}, f32[2,8,128]{2,1,0:T(8,128)}) custom-call(f32[5]{0:T(128)} %decay.3, f32[5]{0:T(128)} %gain.3, f32[64,8,128]{2,1,0:T(8,128)} %collective-permute-done.5.low_c, f32[61,8,128]{2,1,0:T(8,128)} %collective-permute-done.6.high_c, f32[8,88,128]{2,1,0:T(8,128)} %get-tuple-element.32.refs_0_.strips, ...), custom_call_target="tpu_custom_call" | custom-call | flops 99999997952 | bytes 300000000 | tf_op jit(solution)/shard_map/steps_upper/pallas_call | solution.py:502
  53.8 0.1 collective-permute-start.9
  53.8 3.2 %collective-permute-start.10 = (f32[2,8,128]{2,1,0:T(8,128)}, f32[2,8,128]{2,1,0:T(8,128)S(1)}, u32[]{:S(2)}, u32[]{:S(2)}) collective-permute-start(f32[2,8,128]{2,1,0:T(8,128)} %get-tuple-element.37), channel_id=1, source_target_pairs={{0,6},{2,0},{4,2},{6,4},{1,7},{3,1},{5,3},{7,5},{8,14},{10,8},{12,... | collective-permute-start | bytes 24584 | tf_op jit(solution)/shard_map/ppermute | solution.py:29
  57.1 1.8 %collective-permute-done.9 = f32[2,8,128]{2,1,0:T(8,128)S(1)} collective-permute-done((f32[2,8,128]{2,1,0:T(8,128)}, f32[2,8,128]{2,1,0:T(8,128)S(1)}, u32[]{:S(2)}, u32[]{:S(2)}) %collective-permute-start.9) | collective-permute-done | bytes 8224 | tf_op jit(solution)/shard_map/ppermute | solution.py:29
  58.9 0.0 collective-permute-done.10
  58.9 0.7 pad_maximum_fusion
  59.6 3.1 %collective-permute-start.11 = (f32[3,2,8,128]{3,2,1,0:T(8,128)S(1)}, f32[3,2,8,128]{3,2,1,0:T(8,128)S(1)}, u32[]{:S(2)}, u32[]{:S(2)}) collective-permute-start(f32[3,2,8,128]{3,2,1,0:T(8,128)S(1)} %pad_maximum_fusion), channel_id=1, source_target_pairs={{1,0},{3,2},{5,4},{7,6},{9,8},{11,10},{13,12},{15,14},{17,16},{19,... | collective-permute-start | bytes 73736 | tf_op jit(solution)/shard_map/ppermute | solution.py:612
  62.7 0.0 copy-done
  62.8 0.2 reshape.26
  63.0 0.7 copy.11.weights
  63.7 0.5 collective-permute-done.11
  64.2 0.7 broadcast_select_fusion
  65.0 0.0 collective-permute-done.13.refs_5_
  65.0 3.0 %collective-permute-done.12.refs_4_ = f32[46,56,128]{2,1,0:T(8,128)} collective-permute-done((f32[46,56,128]{2,1,0:T(8,128)}, f32[46,56,128]{2,1,0:T(8,128)}, u32[]{:S(2)}, u32[]{:S(2)}) %collective-permute-start.12) | collective-permute-done | bytes 1318944 | tf_op jit(solution)/shard_map/ppermute | solution.py:29
  67.9 0.0 collective-permute-start.14
  67.9 5.4 %collective-permute-start.15 = (f32[3,2,8,128]{3,2,1,0:T(8,128)S(1)}, f32[3,2,8,128]{3,2,1,0:T(8,128)S(1)}, u32[]{:S(2)}, u32[]{:S(2)}) collective-permute-start(f32[3,2,8,128]{3,2,1,0:T(8,128)S(1)} %broadcast_select_fusion), channel_id=1, source_target_pairs={{0,120},{8,0},{16,8},{24,16},{32,24},{40,32},{48,40},{56,48},{64,5... | collective-permute-start | bytes 73736 | tf_op jit(solution)/shard_map/ppermute | solution.py:29
  73.3 25.1 %steps_lower.1 = f32[3,640,128]{2,1,0:T(8,128)} custom-call(f32[5]{0:T(128)} %decay.3, f32[5]{0:T(128)} %gain.3, f32[64,8,128]{2,1,0:T(8,128)} %collective-permute-done.5.low_c, f32[61,8,128]{2,1,0:T(8,128)} %collective-permute-done.6.high_c, f32[8,88,128]{2,1,0:T(8,128)} %get-tuple-element.32.refs_0_.strips, ...), custom_call_target="tpu_custom_call", output_to_operand_aliasing={{}: (12, {})} | custom-call | flops 99999997952 | bytes 300000000 | tf_op jit(solution)/shard_map/steps_lower/pallas_call | solution.py:502
  98.4 0.0 collective-permute-done.14
  98.4 0.0 collective-permute-done.15
  98.4 0.6 slice_bitcast_fusion
  99.1 2.4 %image.1 = f32[4,128]{1,0:T(4,128)} custom-call(f32[48,240]{1,0:T(8,128)} %copy.11.weights, f32[2,24,128]{2,1,0:T(8,128)} %get-tuple-element.46.centre, f32[2,24,128]{2,1,0:T(8,128)} %get-tuple-element.45.before, f32[2,24,128]{2,1,0:T(8,128)} %get-tuple-element.44.after), custom_call_target="tpu_custom_call" | custom-call | tf_op jit(solution)/shard_map/image/pallas_call | solution.py:573
  (5 shorter events, 0.1 us)
Async XLA Ops:
  4.2 10.5 %collective-permute-start.2 = (f32[8,8,128]{2,1,0:T(8,128)}, f32[8,8,128]{2,1,0:T(8,128)S(1)}, u32[]{:S(2)}, u32[]{:S(2)}) collective-permute-start(f32[8,8,128]{2,1,0:T(8,128)} %get-tuple-element.26), channel_id=1, source_target_pairs={{0,3},{1,2},{2,5},{3,4},{4,7},{5,6},{6,1},{7,0},{8,11},{9,10},{10,... | collective-permute-start | bytes 98312 | tf_op jit(solution)/shard_map/ppermute | solution.py:37
  5.9 8.9 %collective-permute-start.3 = (f32[8,8,128]{2,1,0:T(8,128)}, f32[8,8,128]{2,1,0:T(8,128)S(1)}, u32[]{:S(2)}, u32[]{:S(2)}) collective-permute-start(f32[8,8,128]{2,1,0:T(8,128)} %get-tuple-element.26), channel_id=1, source_target_pairs={{0,7},{1,6},{2,1},{3,0},{4,3},{5,2},{6,5},{7,4},{8,15},{9,14},{10,... | collective-permute-start | bytes 98312 | tf_op jit(solution)/shard_map/ppermute | solution.py:37
  8.4 12.3 %collective-permute-start = (f32[8,80,128]{2,1,0:T(8,128)}, f32[8,80,128]{2,1,0:T(8,128)}, u32[]{:S(2)}, u32[]{:S(2)}) collective-permute-start(f32[8,80,128]{2,1,0:T(8,128)} %get-tuple-element.23), channel_id=1, source_target_pairs={{0,2},{2,4},{4,6},{6,0},{1,3},{3,5},{5,7},{7,1},{8,10},{10,12},{12... | collective-permute-start | bytes 983048 | tf_op jit(solution)/shard_map/ppermute | solution.py:29
  8.8 12.0 %collective-permute-start.1 = (f32[8,80,128]{2,1,0:T(8,128)}, f32[8,80,128]{2,1,0:T(8,128)}, u32[]{:S(2)}, u32[]{:S(2)}) collective-permute-start(f32[8,80,128]{2,1,0:T(8,128)} %get-tuple-element.23), channel_id=1, source_target_pairs={{0,6},{2,0},{4,2},{6,4},{1,7},{3,1},{5,3},{7,5},{8,14},{10,8},{12,... | collective-permute-start | bytes 983048 | tf_op jit(solution)/shard_map/ppermute | solution.py:29
  11.7 9.1 %collective-permute-start.4 = (f32[56,8,128]{2,1,0:T(8,128)}, f32[56,8,128]{2,1,0:T(8,128)}, u32[]{:S(2)}, u32[]{:S(2)}) collective-permute-start(f32[56,8,128]{2,1,0:T(8,128)} %get-tuple-element.29), channel_id=1, source_target_pairs={{0,1},{1,0},{2,3},{3,2},{4,5},{5,4},{6,7},{7,6},{8,9},{9,8},{10,11... | collective-permute-start | bytes 688136 | tf_op jit(solution)/shard_map/ppermute | solution.py:29
  14.8 6.0 %copy-start.3 = (f32[8,8,128]{2,1,0:T(8,128)}, f32[8,8,128]{2,1,0:T(8,128)S(1)}, u32[]{:S(2)}) copy-start(f32[8,8,128]{2,1,0:T(8,128)S(1)} %collective-permute-done.2.edge_low) | copy-start | bytes 98308
  14.8 0.6 copy-start.4
  15.4 23.4 %collective-permute-start.7 = (f32[40,24,128]{2,1,0:T(8,128)}, f32[40,24,128]{2,1,0:T(8,128)S(1)}, u32[]{:S(2)}, u32[]{:S(2)}) collective-permute-start(f32[40,24,128]{2,1,0:T(8,128)} %get-tuple-element.34), channel_id=1, source_target_pairs={{0,8},{8,16},{16,24},{24,32},{32,40},{40,48},{48,56},{56,64},{64,7... | collective-permute-start | bytes 1474568 | tf_op jit(solution)/shard_map/ppermute | solution.py:29
  15.4 18.0 %collective-permute-start.8 = (f32[37,24,128]{2,1,0:T(8,128)}, f32[37,24,128]{2,1,0:T(8,128)S(1)}, u32[]{:S(2)}, u32[]{:S(2)}) collective-permute-start(f32[37,24,128]{2,1,0:T(8,128)} %get-tuple-element.35), channel_id=1, source_target_pairs={{0,120},{8,0},{16,8},{24,16},{32,24},{40,32},{48,40},{56,48},{64,5... | collective-permute-start | bytes 1363976 | tf_op jit(solution)/shard_map/ppermute | solution.py:29
  22.9 15.9 %collective-permute-start.5 = (f32[64,8,128]{2,1,0:T(8,128)}, f32[64,8,128]{2,1,0:T(8,128)}, u32[]{:S(2)}, u32[]{:S(2)}) collective-permute-start(f32[64,8,128]{2,1,0:T(8,128)} %get-tuple-element.30), channel_id=1, source_target_pairs={{0,8},{8,16},{16,24},{24,32},{32,40},{40,48},{48,56},{56,64},{64,7... | collective-permute-start | bytes 786440 | tf_op jit(solution)/shard_map/ppermute | solution.py:29
  22.9 15.9 %collective-permute-start.6 = (f32[61,8,128]{2,1,0:T(8,128)}, f32[61,8,128]{2,1,0:T(8,128)}, u32[]{:S(2)}, u32[]{:S(2)}) collective-permute-start(f32[61,8,128]{2,1,0:T(8,128)} %get-tuple-element.31), channel_id=1, source_target_pairs={{0,120},{8,0},{16,8},{24,16},{32,24},{40,32},{48,40},{56,48},{64,5... | collective-permute-start | bytes 749576 | tf_op jit(solution)/shard_map/ppermute | solution.py:29
  33.3 34.6 %collective-permute-start.12 = (f32[46,56,128]{2,1,0:T(8,128)}, f32[46,56,128]{2,1,0:T(8,128)}, u32[]{:S(2)}, u32[]{:S(2)}) collective-permute-start(f32[46,56,128]{2,1,0:T(8,128)} %get-tuple-element.38), channel_id=1, source_target_pairs={{0,8},{8,16},{16,24},{24,32},{32,40},{40,48},{48,56},{56,64},{64,7... | collective-permute-start | bytes 3956744 | tf_op jit(solution)/shard_map/ppermute | solution.py:29
  33.4 5.4 %copy-start.2 = (f32[37,24,128]{2,1,0:T(8,128)}, f32[37,24,128]{2,1,0:T(8,128)S(1)}, u32[]{:S(2)}) copy-start(f32[37,24,128]{2,1,0:T(8,128)S(1)} %collective-permute-done.8.refs_2_) | copy-start | bytes 1363972
  33.4 31.5 %collective-permute-start.13 = (f32[43,56,128]{2,1,0:T(8,128)}, f32[43,56,128]{2,1,0:T(8,128)}, u32[]{:S(2)}, u32[]{:S(2)}) collective-permute-start(f32[43,56,128]{2,1,0:T(8,128)} %get-tuple-element.39), channel_id=1, source_target_pairs={{0,120},{8,0},{16,8},{24,16},{32,24},{40,32},{48,40},{56,48},{64,5... | collective-permute-start | bytes 3698696 | tf_op jit(solution)/shard_map/ppermute | solution.py:29
  38.8 0.8 copy-start.1
  39.6 23.2 %copy-start = (f32[2,24,15,15]{1,0,3,2:T(2,128)S(1)}, f32[2,24,15,15]{1,0,3,2:T(2,128)}, u32[]{:S(2)}) copy-start(f32[2,24,15,15]{1,0,3,2:T(2,128)} %param.11) | copy-start | bytes 129604
  53.8 5.1 %collective-permute-start.9 = (f32[2,8,128]{2,1,0:T(8,128)}, f32[2,8,128]{2,1,0:T(8,128)S(1)}, u32[]{:S(2)}, u32[]{:S(2)}) collective-permute-start(f32[2,8,128]{2,1,0:T(8,128)} %get-tuple-element.37), channel_id=1, source_target_pairs={{0,2},{2,4},{4,6},{6,0},{1,3},{3,5},{5,7},{7,1},{8,10},{10,12},{12... | collective-permute-start | bytes 24584 | tf_op jit(solution)/shard_map/ppermute | solution.py:29
  53.8 5.1 %collective-permute-start.10 = (f32[2,8,128]{2,1,0:T(8,128)}, f32[2,8,128]{2,1,0:T(8,128)S(1)}, u32[]{:S(2)}, u32[]{:S(2)}) collective-permute-start(f32[2,8,128]{2,1,0:T(8,128)} %get-tuple-element.37), channel_id=1, source_target_pairs={{0,6},{2,0},{4,2},{6,4},{1,7},{3,1},{5,3},{7,5},{8,14},{10,8},{12,... | collective-permute-start | bytes 24584 | tf_op jit(solution)/shard_map/ppermute | solution.py:29
  59.6 4.6 %collective-permute-start.11 = (f32[3,2,8,128]{3,2,1,0:T(8,128)S(1)}, f32[3,2,8,128]{3,2,1,0:T(8,128)S(1)}, u32[]{:S(2)}, u32[]{:S(2)}) collective-permute-start(f32[3,2,8,128]{3,2,1,0:T(8,128)S(1)} %pad_maximum_fusion), channel_id=1, source_target_pairs={{1,0},{3,2},{5,4},{7,6},{9,8},{11,10},{13,12},{15,14},{17,16},{19,... | collective-permute-start | bytes 73736 | tf_op jit(solution)/shard_map/ppermute | solution.py:612
  67.9 30.5 %collective-permute-start.14 = (f32[3,2,8,128]{3,2,1,0:T(8,128)S(1)}, f32[3,2,8,128]{3,2,1,0:T(8,128)S(1)}, u32[]{:S(2)}, u32[]{:S(2)}) collective-permute-start(f32[3,2,8,128]{3,2,1,0:T(8,128)S(1)} %broadcast_select_fusion), channel_id=1, source_target_pairs={{0,8},{8,16},{16,24},{24,32},{32,40},{40,48},{48,56},{56,64},{64,7... | collective-permute-start | bytes 73736 | tf_op jit(solution)/shard_map/ppermute | solution.py:29
  67.9 30.5 %collective-permute-start.15 = (f32[3,2,8,128]{3,2,1,0:T(8,128)S(1)}, f32[3,2,8,128]{3,2,1,0:T(8,128)S(1)}, u32[]{:S(2)}, u32[]{:S(2)}) collective-permute-start(f32[3,2,8,128]{3,2,1,0:T(8,128)S(1)} %broadcast_select_fusion), channel_id=1, source_target_pairs={{0,120},{8,0},{16,8},{24,16},{32,24},{40,32},{48,40},{56,48},{64,5... | collective-permute-start | bytes 73736 | tf_op jit(solution)/shard_map/ppermute | solution.py:29

commit v5 on v4

--- a/solution.py
+++ b/solution.py
@@ -123,73 +123,90 @@
     )(el, mg, mat)
 
 
-def pack_kernel(first, last, el, mg, mat, *refs):
-    if first:
-        own, up, down, ext, matv, planes, sems = refs
-    else:
-        strips, own, up, down, ext, matv, planes, sems = refs
-    tiles = last - first
-    here = pl.ds(64 * first, 64 * tiles)
-    loads = [(mat.at[here], matv)]
+def pack_kernel(el, mg, mat, own_u, up_u, down_u, own_l, up_l, down_l, ext, matv, planes, sems):
+    loads = [(mat, matv)]
     for c, (which, comp) in enumerate(SOURCE):
-        loads.append(((el, mg)[which].at[comp, here], ext.at[c]))
+        loads.append(((el, mg)[which].at[comp], ext.at[c]))
     copy_all(loads, sems)
 
-    def row(r, _):
-        for t in range(tiles):
-            rows = pl.ds(64 * t + r, 8, stride=8)
-            for c in range(NC):
-                if c == 6:
-                    v = matv[rows, :].astype(F32)
-                else:
-                    v = ext[c, rows, :]
-                    if c >= 3:
-                        v = v * 2.0
-                planes[plane_of(r, c), 8 * t : 8 * t + 8, :] = v
-        return 0
-
-    lax.fori_loop(0, 8, row, 0)
-    z = pl.ds(0, 8 * tiles)
-    pairs = [(planes, own)]
-    for a, b, n in ((6, 0, 18), (30, 18, 2), (33, 20, 15), (51, 35, 5)):
-        pairs.append((planes.at[pl.ds(a, n)], up.at[pl.ds(b, n), z]))
-    for a, b, n in ((0, 0, 17), (24, 17, 15), (48, 32, 5)):
-        pairs.append((planes.at[pl.ds(a, n)], down.at[pl.ds(b, n), z]))
-    if not first:
-        pairs.append((strips.at[pl.ds(8 - W, W), z], up.at[pl.ds(40, W)]))
-        pairs.append((strips.at[pl.ds(0, W), z], down.at[pl.ds(37, W)]))
-    copy_all(pairs, sems)
-
-
-def pack(first, last, el, mg, mat, *strips):
-    layers = 8 * (last - first)
-    more = 0 if first else W
-    return pl.pallas_call(
-        functools.partial(pack_kernel, first, last),
-        out_shape=[
+    def rows_of(first, last):
+        def row(r, _):
+            for t in range(first, last):
+                rows = pl.ds(64 * t + r, 8, stride=8)
+                for c in range(NC):
+                    if c == 6:
+                        v = matv[rows, :].astype(F32)
+                    else:
+                        v = ext[c, rows, :]
+                        if c >= 3:
+                            v = v * 2.0
+                    planes[plane_of(r, c), 8 * t : 8 * t + 8, :] = v
+            return 0
+
+        lax.fori_loop(0, 8, row, 0)
+
+    def sends(first, last, own, up, down):
+        z = pl.ds(8 * first, 8 * (last - first))
+        pairs = []
+        for a, b, n in ((6, 0, 18), (30, 18, 2), (33, 20, 15), (51, 35, 5)):
+            pairs.append((planes.at[pl.ds(a, n), z], up.at[pl.ds(b, n)]))
+        for a, b, n in ((0, 0, 17), (24, 17, 15), (48, 32, 5)):
+            pairs.append((planes.at[pl.ds(a, n), z], down.at[pl.ds(b, n)]))
+        pairs.append((planes.at[:, z], own))
+        return pairs
+
+    rows_of(CUT, 10)
+    pairs = sends(CUT, 10, own_u, up_u, down_u)
+    upper = [pltpu.make_async_copy(a, b, sems.at[i]) for i, (a, b) in enumerate(pairs)]
+    for copy in upper:
+        copy.start()
+    rows_of(0, CUT)
+    pairs = sends(0, CUT, own_l, up_l, down_l)
+    lower = [pltpu.make_async_copy(a, b, sems.at[8 + i]) for i, (a, b) in enumerate(pairs)]
+    for copy in lower:
+        copy.start()
+    for copy in upper + lower:
+        copy.wait()
+
+
+def pack(el, mg, mat):
+    shapes = []
+    for layers, more in ((8 * (10 - CUT), 0), (8 * CUT, W)):
+        shapes += [
             jax.ShapeDtypeStruct((8 * NC, layers, 128), F32),
             jax.ShapeDtypeStruct((40 + more, layers, 128), F32),
             jax.ShapeDtypeStruct((37 + more, layers, 128), F32),
-        ],
-        in_specs=[HBM] * 3 + [LOCAL] * len(strips),
-        out_specs=[HBM] * 3,
+        ]
+    return pl.pallas_call(
+        pack_kernel,
+        out_shape=shapes,
+        in_specs=[HBM] * 3,
+        out_specs=[HBM] * 6,
         scratch_shapes=[
-            pltpu.VMEM((6, 8 * layers, 128), F32),
-            pltpu.VMEM((8 * layers, 128), jnp.int32),
-            pltpu.VMEM((8 * NC, layers, 128), F32),
-            pltpu.SemaphoreType.DMA((10,)),
+            pltpu.VMEM((6, 640, 128), F32),
+            pltpu.VMEM((640, 128), jnp.int32),
+            pltpu.VMEM((8 * NC, 80, 128), F32),
+            pltpu.SemaphoreType.DMA((16,)),
         ],
         compiler_params=params(),
-        cost_estimate=cost(20 if first else 3),
-        name="pack_upper" if first else "pack_lower",
-    )(el, mg, mat, *strips)
-
-
-def corner_kernel(from_low, from_high, edge_low, edge_high, edge, strips, up, down):
+        cost_estimate=cost(20),
+        name="pack",
+    )(el, mg, mat)
+
+
+def corner_kernel(from_low, from_high, edge_low, edge_high, edge, *refs):
+    strips, up, down, up_l, down_l, sems = refs[2:]
     lane = lax.broadcasted_iota(jnp.int32, (8, 80, 128), 2)
     strips[:, 0:80, :] = jnp.where(lane % 16 < 8, from_high[...], from_low[...])
     lane = lax.broadcasted_iota(jnp.int32, (8, 8, 128), 2)
     strips[:, 80:88, :] = jnp.where(lane % 16 < 8, edge_high[...], edge_low[...])
+    z = pl.ds(0, 8 * CUT)
+    copies = [
+        pltpu.make_async_copy(strips.at[pl.ds(8 - W, W), z], up_l.at[pl.ds(40, W)], sems.at[0]),
+        pltpu.make_async_copy(strips.at[pl.ds(0, W), z], down_l.at[pl.ds(37, W)], sems.at[1]),
+    ]
+    for copy in copies:
+        copy.start()
     for a, b, n in ((6, 0, 18), (30, 18, 2), (33, 20, 15), (51, 35, 5)):
         up[b : b + n] = edge[a : a + n]
     for a, b, n in ((0, 0, 17), (24, 17, 15), (48, 32, 5)):
@@ -199,22 +216,28 @@
             z = 8 * (CUT + t)
             up[40 + HIGH * r + t] = strips[8 - W + r, z : z + 8, :]
             down[37 + HIGH * r + t] = strips[r, z : z + 8, :]
-
-
-def corners(from_low, from_high, edge_low, edge_high, edge):
+    for copy in copies:
+        copy.wait()
+
+
+def corners(from_low, from_high, edge_low, edge_high, edge, up_l, down_l):
     return pl.pallas_call(
         corner_kernel,
         out_shape=[
             jax.ShapeDtypeStruct((8, 88, 128), F32),
             jax.ShapeDtypeStruct((40 + W * HIGH, 8, 128), F32),
             jax.ShapeDtypeStruct((37 + W * HIGH, 8, 128), F32),
+            jax.ShapeDtypeStruct(up_l.shape, F32),
+            jax.ShapeDtypeStruct(down_l.shape, F32),
         ],
-        in_specs=[LOCAL] * 5,
-        out_specs=[LOCAL] * 3,
+        in_specs=[LOCAL] * 5 + [HBM] * 2,
+        out_specs=[LOCAL] * 3 + [HBM] * 2,
+        scratch_shapes=[pltpu.SemaphoreType.DMA((2,))],
+        input_output_aliases={5: 3, 6: 4},
         compiler_params=params(),
         cost_estimate=cost(1),
         name="corners",
-    )(from_low, from_high, edge_low, edge_high, edge)
+    )(from_low, from_high, edge_low, edge_high, edge, up_l, down_l)
 
 
 def steps_kernel(upper, decay, gain, low_c, high_c, strips, edge, *refs):
@@ -374,11 +397,11 @@
         base = start + 2 * m
         b3, b4 = 3 * base, 4 * base
         waiting = []
-        jobs = [(ms, row, t) for row, t in units] + [(es, row, t) for row, t in units]
-        jobs = jobs if with_e else []
-
-        def turn():
-            refs, row, t = jobs.pop(0)
+        half = len(units) // 2
+        jobs_m = [(ms, row, t) for row, t in units] if with_e else []
+        jobs_e = [(es, row, t) for row, t in units] if with_e else []
+
+        def turn(refs, row, t):
             z = 8 * t
             if refs is ms:
                 pairs = [
@@ -399,16 +422,16 @@
                 y[b + (i + 2 * j), z : z + 8, :] = jnp.where(edge_lane, v1, v0)
                 y[b + (i + 2 * j + 1), z : z + 8, :] = jnp.where(edge_lane, v0, v1)
 
-        def pace():
-            for _ in range(2):
-                if jobs:
-                    turn()
-            for _ in range(2):
-                if len(waiting) > LAG or (waiting and not jobs):
-                    keep()
-
-        for row, t in units if with_m else ():
-            pace()
+        def settle(most):
+            while len(waiting) > most:
+                keep()
+
+        for u, (row, t) in enumerate(units if with_m else ()):
+            if jobs_m:
+                turn(*jobs_m.pop(0))
+                if u >= half:
+                    turn(*jobs_e.pop(0))
+            settle(LAG)
             z = 8 * t
             for k in range(2):
 
@@ -429,13 +452,13 @@
                 mx, my, mz = magnetic(X) - cx, magnetic(Y) - cy, magnetic(Z) - cz
                 for c, v in ((X, mx), (Y, my), (Z, mz)):
                     ms[new][k][b3 + (3 * row + c), 8 + z : 16 + z, :] = v
-        while jobs:
-            turn()
-            if len(waiting) > LAG:
-                keep()
-        while waiting:
-            keep()
+        for job in jobs_m:
+            turn(*job)
+            settle(LAG)
         for row, t in units if with_e else ():
+            if jobs_e:
+                turn(*jobs_e.pop(0))
+            settle(LAG if jobs_e else max(len(waiting) - 2, 0))
             e, z = row - 2, 8 * t
             for k in range(2):
 
@@ -455,6 +478,7 @@
                 ez = d * electric(Z) + g * ((my - magnetic(Y, e - 1)) - (mx - mx_y))
                 for c, v in ((X, ex), (Y, ey), (Z, ez)):
                     es[new][k][b3 + (3 * e + c), 8 + z : 16 + z, :] = v
+        settle(0)
         return start
 
     def two_steps(s, _):
@@ -520,8 +544,11 @@
     )(decay, gain, *sides, *arrays)
 
 
-def image_kernel(weights, centre, before, after, out, sh, rhs):
+def image_kernel(weights, own, received, out, sh, rhs):
     gz = lax.axis_index("gz")
+    centre, before, after = [
+        [jnp.where(gz == 1, own[i, c], received[i, c]) for c in range(2)] for i in range(3)
+    ]
     lane = lax.broadcasted_iota(jnp.int32, (24, 128), 1)
     for q in range(15):
         shift = q - 7
@@ -569,19 +596,19 @@
         )
 
 
-def image_of(weights, centre, before, after):
+def image_of(weights, own, received):
     return pl.pallas_call(
         image_kernel,
         out_shape=jax.ShapeDtypeStruct((4, 128), jnp.float32),
-        in_specs=[pl.BlockSpec(memory_space=pltpu.VMEM)] * 4,
-        out_specs=pl.BlockSpec(memory_space=pltpu.VMEM),
+        in_specs=[LOCAL] * 3,
+        out_specs=LOCAL,
         scratch_shapes=[
             pltpu.VMEM((15, 2, 24, 128), jnp.float32),
             pltpu.VMEM((240, 1024), jnp.float32),
         ],
         compiler_params=pltpu.CompilerParams(vmem_limit_bytes=VMEM),
         name="image",
-    )(weights, centre, before, after)
+    )(weights, own, received)
 
 
 def on_device(electric, magnetic, material, decay, gain, kernels):
@@ -596,26 +623,27 @@
     edge = around(edge, "gz", 1)
     from_low, from_high = around(strips, "gy", 1), around(strips, "gy", -1)
     edge_low, edge_high = beyond(edge_strips, 1), beyond(edge_strips, -1)
-    own_u, up_u, down_u = pack(CUT, 10, el, mg, mat)
+    own_u, up_u, down_u, own_l, up_l, down_l = pack(el, mg, mat)
     up_u, down_u, edge_low, edge_high = lax.optimization_barrier(
         (up_u, down_u, edge_low, edge_high)
     )
     low_u, high_u = around(up_u, "gx", 1), around(down_u, "gx", -1)
-    strips, up_c, down_c = corners(from_low, from_high, edge_low, edge_high, edge)
+    strips, up_c, down_c, up_l, down_l = corners(
+        from_low, from_high, edge_low, edge_high, edge, up_l, down_l
+    )
     low_c, high_c = around(up_c, "gx", 1), around(down_c, "gx", -1)
-    own_l, up_l, down_l = pack(0, CUT, el, mg, mat, strips)
     low_l, high_l = around(up_l, "gx", 1), around(down_l, "gx", -1)
 
     sides = [low_c, high_c, strips, edge]
     field, plane = run_steps(True, decay, gain, sides, [own_u, low_u, high_u])
     top = jnp.stack([plane, around(plane, "gy", 1), around(plane, "gy", -1)])
-    top = jnp.where(lax.axis_index("gz") == 1, top, lax.ppermute(top, "gz", [(1, 0)]))
+    top = jnp.concatenate([around(top, "gx", 1), top, around(top, "gx", -1)], 2)
     top, low_l, high_l = lax.optimization_barrier((top, low_l, high_l))
-    top = jnp.concatenate([around(top, "gx", 1), top, around(top, "gx", -1)], 2)
+    received = lax.ppermute(top, "gz", [(1, 0)])
     (field,) = run_steps(
         False, decay, gain, sides, [own_u, low_u, high_u, own_l, low_l, high_l, field]
     )
-    image = image_of(weights, top[0], top[1], top[2])
+    image = image_of(weights, top, received)
     return (field.reshape(3, 80, 8, 128), image)
 
 

time: 103 us -> 99.1 us (0.962); the launches traced: 101 us -> 98.7 us
  Pallas kernels: 55.1 us -> 51.8 us
    pallas_call x2 -> x1, Pallas kernels: 7.66 us -> 4.32 us  [pack(): pl.pallas_call(pack_kernel, out_shape=shapes, in_specs=[HBM] * 3, out_spe...]
    unnamed x12 -> x18, local copies, waits for them, and re-layouts: 1.38 us -> 2.19 us
  transfers between devices with their start and end apart: 16 -> 16, of which waited for: 3 -> 3; matrix products, arithmetic and copies ran while one was open for 2% -> 2% of each run, Pallas kernels for 48% -> 46%
where the time goes in v5:
time: 99.1 us; the launch traced here: 98.7 us
  Pallas kernels  51.8 us (52%)
  starting transfers between devices  36 us (36%)
  waiting for transfers between devices  5.56 us (6%)
  local copies, waits for them, and re-layouts  3.11 us (3%)
  other arithmetic  1.4 us (1%)
    pallas_call x2, Pallas kernels, run_steps(): pl.pallas_call(functools.partial(steps_kernel, upper), out_shape=out_shap...  38.5 us
    ppermute x13, starting transfers between devices, around(): lax.ppermute(value, axis, [(i, (i + steps) % count) for i in range(count)])  28.6 us
    ppermute x13, waiting for transfers between devices, around(): lax.ppermute(value, axis, [(i, (i + steps) % count) for i in range(count)])  5.55 us
    pallas_call x1, Pallas kernels, pack(): pl.pallas_call(pack_kernel, out_shape=shapes, in_specs=[HBM] * 3, out_spe...  4.32 us
    ppermute x2, starting transfers between devices, beyond(): return lax.ppermute(value, ('gy', 'gz'), pairs)  4.2 us
    pallas_call x1, Pallas kernels, own_strips(): pl.pallas_call(strip_kernel, out_shape=[jax.ShapeDtypeStruct((8, 80, 128)...  3.62 us
    ppermute x1, starting transfers between devices, on_device(): received = lax.ppermute(top, 'gz', [(1, 0)])  3.17 us
    pallas_call x1, Pallas kernels, corners(): pl.pallas_call(corner_kernel, out_shape=[jax.ShapeDtypeStruct((8, 88, 128...  2.92 us
  transfers between devices with their start and end apart: 16, of which 3 were waited for; matrix products, arithmetic and copies ran while one was open for 2% of the time, Pallas kernels for 46%

profile of v5, /device:TPU:2, one launch (start us, length us, event | category | flops | bytes accessed | tf_op | source)
XLA Modules:
  0.0 98.7 jit_solution(9255716550596817144)
XLA Ops:
  0.6 3.6 %own_strips.1 = (f32[8,80,128]{2,1,0:T(8,128)}, f32[56,8,128]{2,1,0:T(8,128)}, f32[8,8,128]{2,1,0:T(8,128)}) custom-call(f32[3,640,128]{2,1,0:T(8,128)} %bitcast.19, f32[3,640,128]{2,1,0:T(8,128)} %bitcast.21, s32[640,128]{1,0:T(8,128)} %bitcast.23), custom_call_target="tpu_custom_call" | custom-call | flops 3000000000 | bytes 9000000 | tf_op jit(solution)/shard_map/own_strips/pallas_call | solution.py:106
  4.3 1.6 %collective-permute-start.2 = (f32[8,8,128]{2,1,0:T(8,128)}, f32[8,8,128]{2,1,0:T(8,128)S(1)}, u32[]{:S(2)}, u32[]{:S(2)}) collective-permute-start(f32[8,8,128]{2,1,0:T(8,128)} %get-tuple-element.28), channel_id=1, source_target_pairs={{0,3},{1,2},{2,5},{3,4},{4,7},{5,6},{6,1},{7,0},{8,11},{9,10},{10,... | collective-permute-start | bytes 98312 | tf_op jit(solution)/shard_map/ppermute | solution.py:37
  5.9 2.6 %collective-permute-start.3 = (f32[8,8,128]{2,1,0:T(8,128)}, f32[8,8,128]{2,1,0:T(8,128)S(1)}, u32[]{:S(2)}, u32[]{:S(2)}) collective-permute-start(f32[8,8,128]{2,1,0:T(8,128)} %get-tuple-element.28), channel_id=1, source_target_pairs={{0,7},{1,6},{2,1},{3,0},{4,3},{5,2},{6,5},{7,4},{8,15},{9,14},{10,... | collective-permute-start | bytes 98312 | tf_op jit(solution)/shard_map/ppermute | solution.py:37
  8.5 0.4 collective-permute-start
  8.8 2.9 %collective-permute-start.1 = (f32[8,80,128]{2,1,0:T(8,128)}, f32[8,80,128]{2,1,0:T(8,128)}, u32[]{:S(2)}, u32[]{:S(2)}) collective-permute-start(f32[8,80,128]{2,1,0:T(8,128)} %get-tuple-element.25), channel_id=1, source_target_pairs={{0,6},{2,0},{4,2},{6,4},{1,7},{3,1},{5,3},{7,5},{8,14},{10,8},{12,... | collective-permute-start | bytes 983048 | tf_op jit(solution)/shard_map/ppermute | solution.py:29
  11.7 0.5 collective-permute-start.4
  12.1 4.3 %pack.1 = (f32[56,24,128]{2,1,0:T(8,128)}, f32[40,24,128]{2,1,0:T(8,128)}, f32[37,24,128]{2,1,0:T(8,128)}, f32[56,56,128]{2,1,0:T(8,128)}, f32[46,56,128]{2,1,0:T(8,128)}, /*index=5*/f32[43,56,128]{2,1,0:T(8,128)}) custom-call(f32[3,640,128]{2,1,0:T(8,128)} %bitcast.20, f32[3,640,128]{2,1,0:T(8,128)} %bitcast.22, s32[640,128]{1,0:T(8,128)} %bitcast.24), custom_call_target="tpu_custom_call" | custom-call | flops 20000000000 | bytes 60000000 | tf_op jit(solution)/shard_map/pack/pallas_call | solution.py:180
  16.5 0.0 collective-permute-done.2.edge_low
  16.5 0.0 copy-start.7
  16.5 0.0 collective-permute-done.3.edge_high
  16.5 0.0 copy-start.8
  16.5 0.6 copy-done.8
  17.1 0.0 collective-permute-start.7
  17.1 5.4 %collective-permute-start.8 = (f32[37,24,128]{2,1,0:T(8,128)}, f32[37,24,128]{2,1,0:T(8,128)S(1)}, u32[]{:S(2)}, u32[]{:S(2)}) collective-permute-start(f32[37,24,128]{2,1,0:T(8,128)} %get-tuple-element.39), channel_id=1, source_target_pairs={{0,120},{8,0},{16,8},{24,16},{32,24},{40,32},{48,40},{56,48},{64,5... | collective-permute-start | bytes 1363976 | tf_op jit(solution)/shard_map/ppermute | solution.py:29
  22.5 0.0 collective-permute-done.4.edge
  22.5 0.0 collective-permute-done.from_low
  22.5 0.0 collective-permute-done.1.from_high
  22.5 0.0 copy-done.7
  22.5 2.9 %corners.1 = (f32[8,88,128]{2,1,0:T(8,128)}, f32[64,8,128]{2,1,0:T(8,128)}, f32[61,8,128]{2,1,0:T(8,128)}, f32[46,56,128]{2,1,0:T(8,128)}, f32[43,56,128]{2,1,0:T(8,128)}) custom-call(f32[8,80,128]{2,1,0:T(8,128)} %collective-permute-done.from_low, f32[8,80,128]{2,1,0:T(8,128)} %collective-permute-done.1.from_high, ...), custom_call_target="tpu_custom_call", output_to_operand_aliasing={{3}: (5, {}), {4}: (6, {})} | custom-call | flops 1000000000 | bytes 3000000 | tf_op jit(solution)/shard_map/corners/pallas_call | solution.py:224
  25.4 0.1 collective-permute-start.5
  25.5 5.3 %collective-permute-start.6 = (f32[61,8,128]{2,1,0:T(8,128)}, f32[61,8,128]{2,1,0:T(8,128)S(1)}, u32[]{:S(2)}, u32[]{:S(2)}) collective-permute-start(f32[61,8,128]{2,1,0:T(8,128)} %get-tuple-element.35), channel_id=1, source_target_pairs={{0,120},{8,0},{16,8},{24,16},{32,24},{40,32},{48,40},{56,48},{64,5... | collective-permute-start | bytes 749576 | tf_op jit(solution)/shard_map/ppermute | solution.py:29
  30.9 0.0 collective-permute-start.13
  30.9 2.8 %collective-permute-done.8.refs_2_ = f32[37,24,128]{2,1,0:T(8,128)S(1)} collective-permute-done((f32[37,24,128]{2,1,0:T(8,128)}, f32[37,24,128]{2,1,0:T(8,128)S(1)}, u32[]{:S(2)}, u32[]{:S(2)}) %collective-permute-start.8) | collective-permute-done | bytes 454688 | tf_op jit(solution)/shard_map/ppermute | solution.py:29
  33.7 0.0 copy-start.4
  33.7 5.4 %collective-permute-start.14 = (f32[43,56,128]{2,1,0:T(8,128)}, f32[43,56,128]{2,1,0:T(8,128)}, u32[]{:S(2)}, u32[]{:S(2)}) collective-permute-start(f32[43,56,128]{2,1,0:T(8,128)} %get-tuple-element.43), channel_id=1, source_target_pairs={{0,120},{8,0},{16,8},{24,16},{32,24},{40,32},{48,40},{56,48},{64,5... | collective-permute-start | bytes 3698696 | tf_op jit(solution)/shard_map/ppermute | solution.py:29
  39.1 0.0 collective-permute-done.7.refs_1_
  39.1 0.0 copy-start.3
  39.1 0.0 collective-permute-done.6.high_c
  39.1 0.0 copy-start.6
  39.1 0.0 collective-permute-done.5.low_c
  39.1 0.0 copy-start.5
  39.1 0.0 copy-done.4
  39.1 0.7 copy-done.6
  39.9 0.1 copy-done.5
  39.9 0.2 copy-done.3
  40.1 0.0 copy-start.1
  40.1 14.1 %steps_upper.1 = (f32[3,640,128]{2,1,0:T(8,128)}, f32[2,8,128]{2,1,0:T(8,128)}) custom-call(f32[5]{0:T(128)} %decay.3, f32[5]{0:T(128)} %gain.3, f32[64,8,128]{2,1,0:T(8,128)} %copy-done.5, f32[61,8,128]{2,1,0:T(8,128)} %copy-done.6, f32[8,88,128]{2,1,0:T(8,128)} %get-tuple-element.36.strips, f32[56,8,128]{2,1,0:T(8,128)} %collective-permute-done.4.edge, ...), custom_call_target="tpu_custom_call" | custom-call | flops 99999997952 | bytes 300000000 | tf_op jit(solution)/shard_map/steps_upper/pallas_call | solution.py:526
  54.2 0.1 collective-permute-start.9
  54.3 3.3 %collective-permute-start.10 = (f32[2,8,128]{2,1,0:T(8,128)}, f32[2,8,128]{2,1,0:T(8,128)S(1)}, u32[]{:S(2)}, u32[]{:S(2)}) collective-permute-start(f32[2,8,128]{2,1,0:T(8,128)} %get-tuple-element.41), channel_id=1, source_target_pairs={{0,6},{2,0},{4,2},{6,4},{1,7},{3,1},{5,3},{7,5},{8,14},{10,8},{12,... | collective-permute-start | bytes 24584 | tf_op jit(solution)/shard_map/ppermute | solution.py:29
  57.5 1.8 %collective-permute-done.9 = f32[2,8,128]{2,1,0:T(8,128)S(1)} collective-permute-done((f32[2,8,128]{2,1,0:T(8,128)}, f32[2,8,128]{2,1,0:T(8,128)S(1)}, u32[]{:S(2)}, u32[]{:S(2)}) %collective-permute-start.9) | collective-permute-done | bytes 8224 | tf_op jit(solution)/shard_map/ppermute | solution.py:29
  59.3 0.0 collective-permute-done.10
  59.3 0.7 pad_maximum_fusion.1
  60.0 0.0 collective-permute-start.11
  60.0 5.4 %collective-permute-start.12 = (f32[3,2,8,128]{3,2,1,0:T(8,128)S(1)}, f32[3,2,8,128]{3,2,1,0:T(8,128)S(1)}, u32[]{:S(2)}, u32[]{:S(2)}) collective-permute-start(f32[3,2,8,128]{3,2,1,0:T(8,128)S(1)} %pad_maximum_fusion.1), channel_id=1, source_target_pairs={{0,120},{8,0},{16,8},{24,16},{32,24},{40,32},{48,40},{56,48},{64,5... | collective-permute-start | bytes 73736 | tf_op jit(solution)/shard_map/ppermute | solution.py:29
  65.4 0.0 copy-done.1
  65.4 0.2 reshape.26
  65.6 0.7 copy.13.weights
  66.3 0.9 collective-permute-done.11
  67.2 0.0 collective-permute-done.12
  67.2 0.7 pad_maximum_fusion.own
  67.9 0.0 copy-start
  67.9 0.0 collective-permute-done.14.refs_5_
  67.9 0.0 collective-permute-done.13.refs_4_
  68.0 3.2 %collective-permute-start.15 = (f32[3,2,24,128]{3,2,1,0:T(8,128)S(1)}, f32[3,2,24,128]{3,2,1,0:T(8,128)S(1)}, u32[]{:S(2)}, u32[]{:S(2)}) collective-permute-start(f32[3,2,24,128]{3,2,1,0:T(8,128)S(1)} %pad_maximum_fusion.own), channel_id=1, source_target_pairs={{1,0},{3,2},{5,4},{7,6},{9,8},{11,10},{13,12},{15,14},{17,16},{19,... | collective-permute-start | bytes 221192 | tf_op jit(solution)/shard_map/ppermute | solution.py:642
  71.1 24.4 %steps_lower.1 = f32[3,640,128]{2,1,0:T(8,128)} custom-call(f32[5]{0:T(128)} %decay.3, f32[5]{0:T(128)} %gain.3, f32[64,8,128]{2,1,0:T(8,128)} %copy-done.5, f32[61,8,128]{2,1,0:T(8,128)} %copy-done.6, f32[8,88,128]{2,1,0:T(8,128)} %get-tuple-element.36.strips, f32[56,8,128]{2,1,0:T(8,128)} %collective-permute-done.4.edge, ...), custom_call_target="tpu_custom_call", output_to_operand_aliasing={{}: (12, {})} | custom-call | flops 99999997952 | bytes 300000000 | tf_op jit(solution)/shard_map/steps_lower/pallas_call | solution.py:526
  95.5 0.0 copy-done
  95.5 0.0 collective-permute-done.15.received
  95.6 0.0 copy-start.2
  95.6 0.6 copy-done.2
  96.2 2.5 %image.1 = f32[4,128]{1,0:T(4,128)} custom-call(f32[48,240]{1,0:T(8,128)} %copy.13.weights, f32[3,2,24,128]{3,2,1,0:T(8,128)} %copy-done, f32[3,2,24,128]{3,2,1,0:T(8,128)} %copy-done.2), custom_call_target="tpu_custom_call" | custom-call | tf_op jit(solution)/shard_map/image/pallas_call | solution.py:600
  (2 shorter events, 0.1 us)
Async XLA Ops:
  4.3 12.2 %collective-permute-start.2 = (f32[8,8,128]{2,1,0:T(8,128)}, f32[8,8,128]{2,1,0:T(8,128)S(1)}, u32[]{:S(2)}, u32[]{:S(2)}) collective-permute-start(f32[8,8,128]{2,1,0:T(8,128)} %get-tuple-element.28), channel_id=1, source_target_pairs={{0,3},{1,2},{2,5},{3,4},{4,7},{5,6},{6,1},{7,0},{8,11},{9,10},{10,... | collective-permute-start | bytes 98312 | tf_op jit(solution)/shard_map/ppermute | solution.py:37
  5.9 10.6 %collective-permute-start.3 = (f32[8,8,128]{2,1,0:T(8,128)}, f32[8,8,128]{2,1,0:T(8,128)S(1)}, u32[]{:S(2)}, u32[]{:S(2)}) collective-permute-start(f32[8,8,128]{2,1,0:T(8,128)} %get-tuple-element.28), channel_id=1, source_target_pairs={{0,7},{1,6},{2,1},{3,0},{4,3},{5,2},{6,5},{7,4},{8,15},{9,14},{10,... | collective-permute-start | bytes 98312 | tf_op jit(solution)/shard_map/ppermute | solution.py:37
  8.5 14.0 %collective-permute-start = (f32[8,80,128]{2,1,0:T(8,128)}, f32[8,80,128]{2,1,0:T(8,128)}, u32[]{:S(2)}, u32[]{:S(2)}) collective-permute-start(f32[8,80,128]{2,1,0:T(8,128)} %get-tuple-element.25), channel_id=1, source_target_pairs={{0,2},{2,4},{4,6},{6,0},{1,3},{3,5},{5,7},{7,1},{8,10},{10,12},{12... | collective-permute-start | bytes 983048 | tf_op jit(solution)/shard_map/ppermute | solution.py:29
  8.8 13.7 %collective-permute-start.1 = (f32[8,80,128]{2,1,0:T(8,128)}, f32[8,80,128]{2,1,0:T(8,128)}, u32[]{:S(2)}, u32[]{:S(2)}) collective-permute-start(f32[8,80,128]{2,1,0:T(8,128)} %get-tuple-element.25), channel_id=1, source_target_pairs={{0,6},{2,0},{4,2},{6,4},{1,7},{3,1},{5,3},{7,5},{8,14},{10,8},{12,... | collective-permute-start | bytes 983048 | tf_op jit(solution)/shard_map/ppermute | solution.py:29
  11.7 10.8 %collective-permute-start.4 = (f32[56,8,128]{2,1,0:T(8,128)}, f32[56,8,128]{2,1,0:T(8,128)}, u32[]{:S(2)}, u32[]{:S(2)}) collective-permute-start(f32[56,8,128]{2,1,0:T(8,128)} %get-tuple-element.31), channel_id=1, source_target_pairs={{0,1},{1,0},{2,3},{3,2},{4,5},{5,4},{6,7},{7,6},{8,9},{9,8},{10,11... | collective-permute-start | bytes 688136 | tf_op jit(solution)/shard_map/ppermute | solution.py:29
  16.5 6.0 %copy-start.7 = (f32[8,8,128]{2,1,0:T(8,128)}, f32[8,8,128]{2,1,0:T(8,128)S(1)}, u32[]{:S(2)}) copy-start(f32[8,8,128]{2,1,0:T(8,128)S(1)} %collective-permute-done.2.edge_low) | copy-start | bytes 98308
  16.5 0.6 copy-start.8
  17.1 22.0 %collective-permute-start.7 = (f32[40,24,128]{2,1,0:T(8,128)}, f32[40,24,128]{2,1,0:T(8,128)S(1)}, u32[]{:S(2)}, u32[]{:S(2)}) collective-permute-start(f32[40,24,128]{2,1,0:T(8,128)} %get-tuple-element.38), channel_id=1, source_target_pairs={{0,8},{8,16},{16,24},{24,32},{32,40},{40,48},{48,56},{56,64},{64,7... | collective-permute-start | bytes 1474568 | tf_op jit(solution)/shard_map/ppermute | solution.py:29
  17.1 16.6 %collective-permute-start.8 = (f32[37,24,128]{2,1,0:T(8,128)}, f32[37,24,128]{2,1,0:T(8,128)S(1)}, u32[]{:S(2)}, u32[]{:S(2)}) collective-permute-start(f32[37,24,128]{2,1,0:T(8,128)} %get-tuple-element.39), channel_id=1, source_target_pairs={{0,120},{8,0},{16,8},{24,16},{32,24},{40,32},{48,40},{56,48},{64,5... | collective-permute-start | bytes 1363976 | tf_op jit(solution)/shard_map/ppermute | solution.py:29
  25.4 13.7 %collective-permute-start.5 = (f32[64,8,128]{2,1,0:T(8,128)}, f32[64,8,128]{2,1,0:T(8,128)S(1)}, u32[]{:S(2)}, u32[]{:S(2)}) collective-permute-start(f32[64,8,128]{2,1,0:T(8,128)} %get-tuple-element.34), channel_id=1, source_target_pairs={{0,8},{8,16},{16,24},{24,32},{32,40},{40,48},{48,56},{56,64},{64,7... | collective-permute-start | bytes 786440 | tf_op jit(solution)/shard_map/ppermute | solution.py:29
  25.5 13.6 %collective-permute-start.6 = (f32[61,8,128]{2,1,0:T(8,128)}, f32[61,8,128]{2,1,0:T(8,128)S(1)}, u32[]{:S(2)}, u32[]{:S(2)}) collective-permute-start(f32[61,8,128]{2,1,0:T(8,128)} %get-tuple-element.35), channel_id=1, source_target_pairs={{0,120},{8,0},{16,8},{24,16},{32,24},{40,32},{48,40},{56,48},{64,5... | collective-permute-start | bytes 749576 | tf_op jit(solution)/shard_map/ppermute | solution.py:29
  30.9 37.1 %collective-permute-start.13 = (f32[46,56,128]{2,1,0:T(8,128)}, f32[46,56,128]{2,1,0:T(8,128)}, u32[]{:S(2)}, u32[]{:S(2)}) collective-permute-start(f32[46,56,128]{2,1,0:T(8,128)} %get-tuple-element.42), channel_id=1, source_target_pairs={{0,8},{8,16},{16,24},{24,32},{32,40},{40,48},{48,56},{56,64},{64,7... | collective-permute-start | bytes 3956744 | tf_op jit(solution)/shard_map/ppermute | solution.py:29
  33.7 5.5 %copy-start.4 = (f32[37,24,128]{2,1,0:T(8,128)}, f32[37,24,128]{2,1,0:T(8,128)S(1)}, u32[]{:S(2)}) copy-start(f32[37,24,128]{2,1,0:T(8,128)S(1)} %collective-permute-done.8.refs_2_) | copy-start | bytes 1363972
  33.7 34.3 %collective-permute-start.14 = (f32[43,56,128]{2,1,0:T(8,128)}, f32[43,56,128]{2,1,0:T(8,128)}, u32[]{:S(2)}, u32[]{:S(2)}) collective-permute-start(f32[43,56,128]{2,1,0:T(8,128)} %get-tuple-element.43), channel_id=1, source_target_pairs={{0,120},{8,0},{16,8},{24,16},{32,24},{40,32},{48,40},{56,48},{64,5... | collective-permute-start | bytes 3698696 | tf_op jit(solution)/shard_map/ppermute | solution.py:29
  39.1 1.0 %copy-start.3 = (f32[40,24,128]{2,1,0:T(8,128)}, f32[40,24,128]{2,1,0:T(8,128)S(1)}, u32[]{:S(2)}) copy-start(f32[40,24,128]{2,1,0:T(8,128)S(1)} %collective-permute-done.7.refs_1_) | copy-start | bytes 1474564
  39.1 0.8 copy-start.6
  39.1 0.8 copy-start.5
  40.1 25.3 %copy-start.1 = (f32[2,24,15,15]{1,0,3,2:T(2,128)S(1)}, f32[2,24,15,15]{1,0,3,2:T(2,128)}, u32[]{:S(2)}) copy-start(f32[2,24,15,15]{1,0,3,2:T(2,128)} %param.11) | copy-start | bytes 129604
  54.2 5.1 %collective-permute-start.9 = (f32[2,8,128]{2,1,0:T(8,128)}, f32[2,8,128]{2,1,0:T(8,128)S(1)}, u32[]{:S(2)}, u32[]{:S(2)}) collective-permute-start(f32[2,8,128]{2,1,0:T(8,128)} %get-tuple-element.41), channel_id=1, source_target_pairs={{0,2},{2,4},{4,6},{6,0},{1,3},{3,5},{5,7},{7,1},{8,10},{10,12},{12... | collective-permute-start | bytes 24584 | tf_op jit(solution)/shard_map/ppermute | solution.py:29
  54.3 5.1 %collective-permute-start.10 = (f32[2,8,128]{2,1,0:T(8,128)}, f32[2,8,128]{2,1,0:T(8,128)S(1)}, u32[]{:S(2)}, u32[]{:S(2)}) collective-permute-start(f32[2,8,128]{2,1,0:T(8,128)} %get-tuple-element.41), channel_id=1, source_target_pairs={{0,6},{2,0},{4,2},{6,4},{1,7},{3,1},{5,3},{7,5},{8,14},{10,8},{12,... | collective-permute-start | bytes 24584 | tf_op jit(solution)/shard_map/ppermute | solution.py:29
  60.0 7.2 %collective-permute-start.11 = (f32[3,2,8,128]{3,2,1,0:T(8,128)S(1)}, f32[3,2,8,128]{3,2,1,0:T(8,128)S(1)}, u32[]{:S(2)}, u32[]{:S(2)}) collective-permute-start(f32[3,2,8,128]{3,2,1,0:T(8,128)S(1)} %pad_maximum_fusion.1), channel_id=1, source_target_pairs={{0,8},{8,16},{16,24},{24,32},{32,40},{40,48},{48,56},{56,64},{64,7... | collective-permute-start | bytes 73736 | tf_op jit(solution)/shard_map/ppermute | solution.py:29
  60.0 7.2 %collective-permute-start.12 = (f32[3,2,8,128]{3,2,1,0:T(8,128)S(1)}, f32[3,2,8,128]{3,2,1,0:T(8,128)S(1)}, u32[]{:S(2)}, u32[]{:S(2)}) collective-permute-start(f32[3,2,8,128]{3,2,1,0:T(8,128)S(1)} %pad_maximum_fusion.1), channel_id=1, source_target_pairs={{0,120},{8,0},{16,8},{24,16},{32,24},{40,32},{48,40},{56,48},{64,5... | collective-permute-start | bytes 73736 | tf_op jit(solution)/shard_map/ppermute | solution.py:29
  67.9 27.6 %copy-start = (f32[3,2,24,128]{3,2,1,0:T(8,128)}, f32[3,2,24,128]{3,2,1,0:T(8,128)S(1)}, u32[]{:S(2)}) copy-start(f32[3,2,24,128]{3,2,1,0:T(8,128)S(1)} %pad_maximum_fusion.own) | copy-start | bytes 221188
  68.0 27.6 %collective-permute-start.15 = (f32[3,2,24,128]{3,2,1,0:T(8,128)S(1)}, f32[3,2,24,128]{3,2,1,0:T(8,128)S(1)}, u32[]{:S(2)}, u32[]{:S(2)}) collective-permute-start(f32[3,2,24,128]{3,2,1,0:T(8,128)S(1)} %pad_maximum_fusion.own), channel_id=1, source_target_pairs={{1,0},{3,2},{5,4},{7,6},{9,8},{11,10},{13,12},{15,14},{17,16},{19,... | collective-permute-start | bytes 221192 | tf_op jit(solution)/shard_map/ppermute | solution.py:642
  95.6 0.6 copy-start.2

commit v6 on v5

--- a/solution.py
+++ b/solution.py
@@ -15,7 +15,7 @@
 ROWS = 8 + 2 * W
 BASE = 4
 HELD = BASE + ROWS + 2
-CUT = 7
+CUT = 8
 HIGH = 11 - CUT
 LAG = 4
 VMEM = 63 * 1024 * 1024
@@ -320,22 +320,24 @@
     for copy in copies[:early]:
         copy.wait()
 
-    def unpack(r, _):
-        at = BASE + r
-        for t in range(tiles):
-            z = 8 * t
-            v = sv[r, z : z + 8, :]
-            for c in range(NC):
-                turned = pltpu.roll(v, 128 - 16 * c, 1) if c else v
-                if c < 3:
-                    ea1[3 * at + c, 8 + z : 16 + z, :] = turned
-                elif c < 6:
-                    ma1[3 * at + c - 3, 8 + z : 16 + z, :] = turned
-                else:
-                    d1[at, z : z + 8, :] = turned
+    def unpack(i, _):
+        for row in range(2):
+            r = 2 * i + row
+            at = BASE + r
+            for t in range(tiles):
+                z = 8 * t
+                v = sv[r, z : z + 8, :]
+                for c in range(NC):
+                    turned = pltpu.roll(v, 128 - 16 * c, 1) if c else v
+                    if c < 3:
+                        ea1[3 * at + c, 8 + z : 16 + z, :] = turned
+                    elif c < 6:
+                        ma1[3 * at + c - 3, 8 + z : 16 + z, :] = turned
+                    else:
+                        d1[at, z : z + 8, :] = turned
         return 0
 
-    lax.fori_loop(0, ROWS, unpack, 0)
+    lax.fori_loop(0, ROWS // 2, unpack, 0)
     for copy in copies[early:]:
         copy.wait()
 
@@ -350,7 +352,11 @@
 
     live = jnp.where(counts, 1.0, 0.0).astype(F32)
 
-    def tables(r, _):
+    lane = lax.broadcasted_iota(jnp.int32, (8, 128), 1)
+    last, first_lane = lane == 127, lane == 0
+    units = [(row, t) for row in range(2) for t in range(tiles)]
+
+    def tables(r):
         for t in range(tiles):
             z = 8 * t
             for d, g in zip(ds_, gs):
@@ -364,15 +370,8 @@
                     d_cells, g_cells = d_cells * live, g_cells * live
                 d[r, z : z + 8, :] = d_cells
                 g[r, z : z + 8, :] = g_cells
-        return 0
-
-    lax.fori_loop(BASE + 1, BASE + ROWS - 1, tables, 0)
-
-    lane = lax.broadcasted_iota(jnp.int32, (8, 128), 1)
-    last, first_lane = lane == 127, lane == 0
-    units = [(row, t) for row in range(2) for t in range(tiles)]
-
-    def turn_two(which, r0):
+
+    def turn_two(which, r0, beside=None):
         kept = []
         for row, t in units:
             for j, c in enumerate((X, Z)):
@@ -381,13 +380,21 @@
                     for e in es[which]
                 ]
                 kept.append((4 * row + 2 * j, 8 * t, pair))
+        if beside:
+            beside()
         y = yes[which]
         for i, z, (a, b) in kept:
             y[4 * r0 + i, z : z + 8, :] = jnp.where(last, b, a)
             y[4 * r0 + (i + 1), z : z + 8, :] = jnp.where(last, a, b)
 
     def first_turn(i, _):
-        turn_two(0, BASE + 2 * i)
+        r0 = BASE + 2 * i
+
+        def both():
+            tables(r0)
+            tables(r0 + 1)
+
+        turn_two(0, r0, both)
         return 0
 
     lax.fori_loop(0, ROWS // 2, first_turn, 0)
@@ -485,8 +492,8 @@
         for old in range(2):
             left = STEPS - 1 - old - 2 * s
             start = BASE + W - left - 2
-            block(old, False, True, 0, start)
-            lax.fori_loop(1, W - 1 + left, functools.partial(block, old, True, True), start)
+            lax.fori_loop(0, 2, functools.partial(block, old, False, True), start)
+            lax.fori_loop(2, W - 1 + left, functools.partial(block, old, True, True), start)
             block(old, True, False, W - 1 + left, start)
             turn_two(1 - old, start + 2 * (W - 2 + left))
         return 0
@@ -634,6 +641,7 @@
     low_c, high_c = around(up_c, "gx", 1), around(down_c, "gx", -1)
     low_l, high_l = around(up_l, "gx", 1), around(down_l, "gx", -1)
 
+    low_u, high_u, weights = lax.optimization_barrier((low_u, high_u, weights))
     sides = [low_c, high_c, strips, edge]
     field, plane = run_steps(True, decay, gain, sides, [own_u, low_u, high_u])
     top = jnp.stack([plane, around(plane, "gy", 1), around(plane, "gy", -1)])

time: 99.1 us -> 104 us (1.049)
  waiting for transfers between devices: 5.56 us -> 10.3 us
    ppermute x13, waiting for transfers between devices: 5.55 us -> 10.3 us  [around(): lax.ppermute(value, axis, [(i, (i + steps) % count) for i in range(count)])]
    unnamed x18 -> x20, local copies, waits for them, and re-layouts: 2.19 us -> 2.3 us
  transfers between devices with their start and end apart: 16 -> 16, of which waited for: 3 -> 3; matrix products, arithmetic and copies ran while one was open for 2% -> 2% of each run, Pallas kernels for 46% -> 44%
where the time goes in v6:
time: 104 us
  Pallas kernels  51.5 us (50%)
  starting transfers between devices  36.3 us (35%)
  waiting for transfers between devices  10.3 us (10%)
  local copies, waits for them, and re-layouts  3.22 us (3%)
  other arithmetic  1.4 us (1%)
    pallas_call x2, Pallas kernels, run_steps(): pl.pallas_call(functools.partial(steps_kernel, upper), out_shape=out_shap...  38.2 us
    ppermute x13, starting transfers between devices, around(): lax.ppermute(value, axis, [(i, (i + steps) % count) for i in range(count)])  28.6 us
    ppermute x13, waiting for transfers between devices, around(): lax.ppermute(value, axis, [(i, (i + steps) % count) for i in range(count)])  10.3 us
    pallas_call x1, Pallas kernels, pack(): pl.pallas_call(pack_kernel, out_shape=shapes, in_specs=[HBM] * 3, out_spe...  4.37 us
    ppermute x2, starting transfers between devices, beyond(): return lax.ppermute(value, ('gy', 'gz'), pairs)  4.2 us
    pallas_call x1, Pallas kernels, own_strips(): pl.pallas_call(strip_kernel, out_shape=[jax.ShapeDtypeStruct((8, 80, 128)...  3.56 us
    ppermute x1, starting transfers between devices, on_device(): received = lax.ppermute(top, 'gz', [(1, 0)])  3.54 us
    pallas_call x1, Pallas kernels, corners(): pl.pallas_call(corner_kernel, out_shape=[jax.ShapeDtypeStruct((8, 88, 128...  2.93 us
  transfers between devices with their start and end apart: 16, of which 3 were waited for; matrix products, arithmetic and copies ran while one was open for 2% of the time, Pallas kernels for 44%

profile of v6, /device:TPU:2, one launch (start us, length us, event | category | flops | bytes accessed | tf_op | source)
XLA Modules:
  0.0 103.7 jit_solution(15331508017632920171)
XLA Ops:
  0.6 3.6 %own_strips.1 = (f32[8,80,128]{2,1,0:T(8,128)}, f32[56,8,128]{2,1,0:T(8,128)}, f32[8,8,128]{2,1,0:T(8,128)}) custom-call(f32[3,640,128]{2,1,0:T(8,128)} %bitcast.19, f32[3,640,128]{2,1,0:T(8,128)} %bitcast.21, s32[640,128]{1,0:T(8,128)} %bitcast.23), custom_call_target="tpu_custom_call" | custom-call | flops 3000000000 | bytes 9000000 | tf_op jit(solution)/shard_map/own_strips/pallas_call | solution.py:106
  4.2 1.6 %collective-permute-start.2 = (f32[8,8,128]{2,1,0:T(8,128)}, f32[8,8,128]{2,1,0:T(8,128)S(1)}, u32[]{:S(2)}, u32[]{:S(2)}) collective-permute-start(f32[8,8,128]{2,1,0:T(8,128)} %get-tuple-element.31), channel_id=1, source_target_pairs={{0,3},{1,2},{2,5},{3,4},{4,7},{5,6},{6,1},{7,0},{8,11},{9,10},{10,... | collective-permute-start | bytes 98312 | tf_op jit(solution)/shard_map/ppermute | solution.py:37
  5.8 2.6 %collective-permute-start.3 = (f32[8,8,128]{2,1,0:T(8,128)}, f32[8,8,128]{2,1,0:T(8,128)S(1)}, u32[]{:S(2)}, u32[]{:S(2)}) collective-permute-start(f32[8,8,128]{2,1,0:T(8,128)} %get-tuple-element.31), channel_id=1, source_target_pairs={{0,7},{1,6},{2,1},{3,0},{4,3},{5,2},{6,5},{7,4},{8,15},{9,14},{10,... | collective-permute-start | bytes 98312 | tf_op jit(solution)/shard_map/ppermute | solution.py:37
  8.4 0.4 collective-permute-start
  8.8 2.9 %collective-permute-start.1 = (f32[8,80,128]{2,1,0:T(8,128)}, f32[8,80,128]{2,1,0:T(8,128)S(1)}, u32[]{:S(2)}, u32[]{:S(2)}) collective-permute-start(f32[8,80,128]{2,1,0:T(8,128)} %get-tuple-element.28), channel_id=1, source_target_pairs={{0,6},{2,0},{4,2},{6,4},{1,7},{3,1},{5,3},{7,5},{8,14},{10,8},{12,... | collective-permute-start | bytes 983048 | tf_op jit(solution)/shard_map/ppermute | solution.py:29
  11.6 0.5 collective-permute-start.4
  12.1 4.4 %pack.1 = (f32[56,16,128]{2,1,0:T(8,128)}, f32[40,16,128]{2,1,0:T(8,128)}, f32[37,16,128]{2,1,0:T(8,128)}, f32[56,64,128]{2,1,0:T(8,128)}, f32[46,64,128]{2,1,0:T(8,128)}, /*index=5*/f32[43,64,128]{2,1,0:T(8,128)}) custom-call(f32[3,640,128]{2,1,0:T(8,128)} %bitcast.20, f32[3,640,128]{2,1,0:T(8,128)} %bitcast.22, s32[640,128]{1,0:T(8,128)} %bitcast.24), custom_call_target="tpu_custom_call" | custom-call | flops 20000000000 | bytes 60000000 | tf_op jit(solution)/shard_map/pack/pallas_call | solution.py:180
  16.5 0.0 collective-permute-done.2.edge_low
  16.5 0.0 copy-start.6
  16.5 0.0 collective-permute-done.3.edge_high
  16.5 0.0 copy-start.7
  16.5 0.1 collective-permute-start.7
  16.6 5.3 %collective-permute-start.8 = (f32[37,16,128]{2,1,0:T(8,128)}, f32[37,16,128]{2,1,0:T(8,128)}, u32[]{:S(2)}, u32[]{:S(2)}) collective-permute-start(f32[37,16,128]{2,1,0:T(8,128)} %get-tuple-element.42), channel_id=1, source_target_pairs={{0,120},{8,0},{16,8},{24,16},{32,24},{40,32},{48,40},{56,48},{64,5... | collective-permute-start | bytes 909320 | tf_op jit(solution)/shard_map/ppermute | solution.py:29
  21.9 0.0 collective-permute-done.4.edge
  21.9 0.0 copy-start.4
  21.9 0.0 collective-permute-done.from_low
  22.0 0.0 copy-start
  22.0 0.0 collective-permute-done.1.from_high
  22.0 0.0 copy-start.1
  22.0 0.7 copy-done.4
  22.6 0.0 copy-done.6
  22.6 0.0 copy-done.7
  22.6 0.1 copy-done
  22.7 0.1 copy-done.1
  22.9 0.0 copy-start.3
  22.9 2.9 %corners.1 = (f32[8,88,128]{2,1,0:T(8,128)}, f32[58,8,128]{2,1,0:T(8,128)}, f32[55,8,128]{2,1,0:T(8,128)}, f32[46,64,128]{2,1,0:T(8,128)}, f32[43,64,128]{2,1,0:T(8,128)}) custom-call(f32[8,80,128]{2,1,0:T(8,128)} %copy-done, f32[8,80,128]{2,1,0:T(8,128)} %copy-done.1, f32[8,8,128]{2,1,0:T(8,128)} %copy-done.6, ...), custom_call_target="tpu_custom_call", output_to_operand_aliasing={{3}: (5, {}), {4}: (6, {})} | custom-call | flops 1000000000 | bytes 3000000 | tf_op jit(solution)/shard_map/corners/pallas_call | solution.py:224
  25.8 0.1 collective-permute-start.5
  25.9 5.3 %collective-permute-start.6 = (f32[55,8,128]{2,1,0:T(8,128)}, f32[55,8,128]{2,1,0:T(8,128)S(1)}, u32[]{:S(2)}, u32[]{:S(2)}) collective-permute-start(f32[55,8,128]{2,1,0:T(8,128)} %get-tuple-element.38), channel_id=1, source_target_pairs={{0,120},{8,0},{16,8},{24,16},{32,24},{40,32},{48,40},{56,48},{64,5... | collective-permute-start | bytes 675848 | tf_op jit(solution)/shard_map/ppermute | solution.py:29
  31.2 0.0 copy-done.3
  31.2 0.2 reshape.25
  31.5 0.1 collective-permute-start.13
  31.6 0.0 collective-permute-done.8.refs_2_
  31.6 5.3 %collective-permute-start.14 = (f32[43,64,128]{2,1,0:T(8,128)}, f32[43,64,128]{2,1,0:T(8,128)}, u32[]{:S(2)}, u32[]{:S(2)}) collective-permute-start(f32[43,64,128]{2,1,0:T(8,128)} %get-tuple-element.48), channel_id=1, source_target_pairs={{0,120},{8,0},{16,8},{24,16},{32,24},{40,32},{48,40},{56,48},{64,5... | collective-permute-start | bytes 4227080 | tf_op jit(solution)/shard_map/ppermute | solution.py:29
  36.9 0.0 collective-permute-done.7.refs_1_
  36.9 0.6 collective-permute-done.6.high_c
  37.5 0.0 copy-start.9
  37.5 0.0 collective-permute-done.5.low_c
  37.5 0.0 copy-start.8
  37.5 0.7 copy-done.9
  38.2 0.1 copy-done.8
  38.3 12.0 %steps_upper.1 = (f32[3,640,128]{2,1,0:T(8,128)}, f32[2,8,128]{2,1,0:T(8,128)}) custom-call(f32[5]{0:T(128)} %decay.3, f32[5]{0:T(128)} %gain.3, f32[58,8,128]{2,1,0:T(8,128)} %copy-done.8, f32[55,8,128]{2,1,0:T(8,128)} %copy-done.9, f32[8,88,128]{2,1,0:T(8,128)} %get-tuple-element.39.strips, f32[56,8,128]{2,1,0:T(8,128)} %copy-done.4, ...), custom_call_target="tpu_custom_call" | custom-call | flops 99999997952 | bytes 300000000 | tf_op jit(solution)/shard_map/steps_upper/pallas_call | solution.py:533
  50.3 0.1 collective-permute-start.9
  50.4 3.2 %collective-permute-start.10 = (f32[2,8,128]{2,1,0:T(8,128)}, f32[2,8,128]{2,1,0:T(8,128)S(1)}, u32[]{:S(2)}, u32[]{:S(2)}) collective-permute-start(f32[2,8,128]{2,1,0:T(8,128)} %get-tuple-element.46), channel_id=1, source_target_pairs={{0,6},{2,0},{4,2},{6,4},{1,7},{3,1},{5,3},{7,5},{8,14},{10,8},{12,... | collective-permute-start | bytes 24584 | tf_op jit(solution)/shard_map/ppermute | solution.py:29
  53.6 1.8 %collective-permute-done.9 = f32[2,8,128]{2,1,0:T(8,128)S(1)} collective-permute-done((f32[2,8,128]{2,1,0:T(8,128)}, f32[2,8,128]{2,1,0:T(8,128)S(1)}, u32[]{:S(2)}, u32[]{:S(2)}) %collective-permute-start.9) | collective-permute-done | bytes 8224 | tf_op jit(solution)/shard_map/ppermute | solution.py:29
  55.5 0.0 collective-permute-done.10
  55.5 0.7 pad_maximum_fusion.1
  56.2 0.0 collective-permute-start.11
  56.2 5.4 %collective-permute-start.12 = (f32[3,2,8,128]{3,2,1,0:T(8,128)S(1)}, f32[3,2,8,128]{3,2,1,0:T(8,128)S(1)}, u32[]{:S(2)}, u32[]{:S(2)}) collective-permute-start(f32[3,2,8,128]{3,2,1,0:T(8,128)S(1)} %pad_maximum_fusion.1), channel_id=1, source_target_pairs={{0,120},{8,0},{16,8},{24,16},{32,24},{40,32},{48,40},{56,48},{64,5... | collective-permute-start | bytes 73736 | tf_op jit(solution)/shard_map/ppermute | solution.py:29
  61.5 0.7 copy.13.weights
  62.2 7.9 %collective-permute-done.11 = f32[3,2,8,128]{3,2,1,0:T(8,128)S(1)} collective-permute-done((f32[3,2,8,128]{3,2,1,0:T(8,128)S(1)}, f32[3,2,8,128]{3,2,1,0:T(8,128)S(1)}, u32[]{:S(2)}, u32[]{:S(2)}) %collective-permute-start.11) | collective-permute-done | bytes 24608 | tf_op jit(solution)/shard_map/ppermute | solution.py:29
  70.1 0.0 collective-permute-done.12
  70.1 0.7 pad_maximum_fusion.own
  70.8 0.0 copy-start.2
  70.8 0.0 collective-permute-done.14.refs_5_
  70.8 0.0 collective-permute-done.13.refs_4_
  70.8 3.5 %collective-permute-start.15 = (f32[3,2,24,128]{3,2,1,0:T(8,128)S(1)}, f32[3,2,24,128]{3,2,1,0:T(8,128)S(1)}, u32[]{:S(2)}, u32[]{:S(2)}) collective-permute-start(f32[3,2,24,128]{3,2,1,0:T(8,128)S(1)} %pad_maximum_fusion.own), channel_id=1, source_target_pairs={{1,0},{3,2},{5,4},{7,6},{9,8},{11,10},{13,12},{15,14},{17,16},{19,... | collective-permute-start | bytes 221192 | tf_op jit(solution)/shard_map/ppermute | solution.py:650
  74.3 26.2 %steps_lower.1 = f32[3,640,128]{2,1,0:T(8,128)} custom-call(f32[5]{0:T(128)} %decay.3, f32[5]{0:T(128)} %gain.3, f32[58,8,128]{2,1,0:T(8,128)} %copy-done.8, f32[55,8,128]{2,1,0:T(8,128)} %copy-done.9, f32[8,88,128]{2,1,0:T(8,128)} %get-tuple-element.39.strips, f32[56,8,128]{2,1,0:T(8,128)} %copy-done.4, ...), custom_call_target="tpu_custom_call", output_to_operand_aliasing={{}: (12, {})} | custom-call | flops 99999997952 | bytes 300000000 | tf_op jit(solution)/shard_map/steps_lower/pallas_call | solution.py:533
  100.5 0.0 copy-done.2
  100.5 0.0 collective-permute-done.15.received
  100.5 0.0 copy-start.5
  100.6 0.6 copy-done.5
  101.2 2.5 %image.1 = f32[4,128]{1,0:T(4,128)} custom-call(f32[48,240]{1,0:T(8,128)} %copy.13.weights, f32[3,2,24,128]{3,2,1,0:T(8,128)} %copy-done.2, f32[3,2,24,128]{3,2,1,0:T(8,128)} %copy-done.5), custom_call_target="tpu_custom_call" | custom-call | tf_op jit(solution)/shard_map/image/pallas_call | solution.py:607
  (2 shorter events, 0.1 us)
Async XLA Ops:
  4.2 12.3 %collective-permute-start.2 = (f32[8,8,128]{2,1,0:T(8,128)}, f32[8,8,128]{2,1,0:T(8,128)S(1)}, u32[]{:S(2)}, u32[]{:S(2)}) collective-permute-start(f32[8,8,128]{2,1,0:T(8,128)} %get-tuple-element.31), channel_id=1, source_target_pairs={{0,3},{1,2},{2,5},{3,4},{4,7},{5,6},{6,1},{7,0},{8,11},{9,10},{10,... | collective-permute-start | bytes 98312 | tf_op jit(solution)/shard_map/ppermute | solution.py:37
  5.8 10.7 %collective-permute-start.3 = (f32[8,8,128]{2,1,0:T(8,128)}, f32[8,8,128]{2,1,0:T(8,128)S(1)}, u32[]{:S(2)}, u32[]{:S(2)}) collective-permute-start(f32[8,8,128]{2,1,0:T(8,128)} %get-tuple-element.31), channel_id=1, source_target_pairs={{0,7},{1,6},{2,1},{3,0},{4,3},{5,2},{6,5},{7,4},{8,15},{9,14},{10,... | collective-permute-start | bytes 98312 | tf_op jit(solution)/shard_map/ppermute | solution.py:37
  8.4 13.5 %collective-permute-start = (f32[8,80,128]{2,1,0:T(8,128)}, f32[8,80,128]{2,1,0:T(8,128)S(1)}, u32[]{:S(2)}, u32[]{:S(2)}) collective-permute-start(f32[8,80,128]{2,1,0:T(8,128)} %get-tuple-element.28), channel_id=1, source_target_pairs={{0,2},{2,4},{4,6},{6,0},{1,3},{3,5},{5,7},{7,1},{8,10},{10,12},{12... | collective-permute-start | bytes 983048 | tf_op jit(solution)/shard_map/ppermute | solution.py:29
  8.8 13.2 %collective-permute-start.1 = (f32[8,80,128]{2,1,0:T(8,128)}, f32[8,80,128]{2,1,0:T(8,128)S(1)}, u32[]{:S(2)}, u32[]{:S(2)}) collective-permute-start(f32[8,80,128]{2,1,0:T(8,128)} %get-tuple-element.28), channel_id=1, source_target_pairs={{0,6},{2,0},{4,2},{6,4},{1,7},{3,1},{5,3},{7,5},{8,14},{10,8},{12,... | collective-permute-start | bytes 983048 | tf_op jit(solution)/shard_map/ppermute | solution.py:29
  11.6 10.3 %collective-permute-start.4 = (f32[56,8,128]{2,1,0:T(8,128)}, f32[56,8,128]{2,1,0:T(8,128)S(1)}, u32[]{:S(2)}, u32[]{:S(2)}) collective-permute-start(f32[56,8,128]{2,1,0:T(8,128)} %get-tuple-element.34), channel_id=1, source_target_pairs={{0,1},{1,0},{2,3},{3,2},{4,5},{5,4},{6,7},{7,6},{8,9},{9,8},{10,11... | collective-permute-start | bytes 688136 | tf_op jit(solution)/shard_map/ppermute | solution.py:29
  16.5 6.2 %copy-start.6 = (f32[8,8,128]{2,1,0:T(8,128)}, f32[8,8,128]{2,1,0:T(8,128)S(1)}, u32[]{:S(2)}) copy-start(f32[8,8,128]{2,1,0:T(8,128)S(1)} %collective-permute-done.2.edge_low) | copy-start | bytes 98308
  16.5 6.1 %copy-start.7 = (f32[8,8,128]{2,1,0:T(8,128)}, f32[8,8,128]{2,1,0:T(8,128)S(1)}, u32[]{:S(2)}) copy-start(f32[8,8,128]{2,1,0:T(8,128)S(1)} %collective-permute-done.3.edge_high) | copy-start | bytes 98308
  16.5 20.4 %collective-permute-start.7 = (f32[40,16,128]{2,1,0:T(8,128)}, f32[40,16,128]{2,1,0:T(8,128)}, u32[]{:S(2)}, u32[]{:S(2)}) collective-permute-start(f32[40,16,128]{2,1,0:T(8,128)} %get-tuple-element.41), channel_id=1, source_target_pairs={{0,8},{8,16},{16,24},{24,32},{32,40},{40,48},{48,56},{56,64},{64,7... | collective-permute-start | bytes 983048 | tf_op jit(solution)/shard_map/ppermute | solution.py:29
  16.6 15.0 %collective-permute-start.8 = (f32[37,16,128]{2,1,0:T(8,128)}, f32[37,16,128]{2,1,0:T(8,128)}, u32[]{:S(2)}, u32[]{:S(2)}) collective-permute-start(f32[37,16,128]{2,1,0:T(8,128)} %get-tuple-element.42), channel_id=1, source_target_pairs={{0,120},{8,0},{16,8},{24,16},{32,24},{40,32},{48,40},{56,48},{64,5... | collective-permute-start | bytes 909320 | tf_op jit(solution)/shard_map/ppermute | solution.py:29
  21.9 0.7 copy-start.4
  22.0 0.8 copy-start
  22.0 0.9 copy-start.1
  22.9 8.4 %copy-start.3 = (f32[2,24,15,15]{1,0,3,2:T(2,128)S(1)}, f32[2,24,15,15]{1,0,3,2:T(2,128)}, u32[]{:S(2)}) copy-start(f32[2,24,15,15]{1,0,3,2:T(2,128)} %param.11) | copy-start | bytes 129604
  25.8 11.7 %collective-permute-start.5 = (f32[58,8,128]{2,1,0:T(8,128)}, f32[58,8,128]{2,1,0:T(8,128)S(1)}, u32[]{:S(2)}, u32[]{:S(2)}) collective-permute-start(f32[58,8,128]{2,1,0:T(8,128)} %get-tuple-element.37), channel_id=1, source_target_pairs={{0,8},{8,16},{16,24},{24,32},{32,40},{40,48},{48,56},{56,64},{64,7... | collective-permute-start | bytes 712712 | tf_op jit(solution)/shard_map/ppermute | solution.py:29
  25.9 11.6 %collective-permute-start.6 = (f32[55,8,128]{2,1,0:T(8,128)}, f32[55,8,128]{2,1,0:T(8,128)S(1)}, u32[]{:S(2)}, u32[]{:S(2)}) collective-permute-start(f32[55,8,128]{2,1,0:T(8,128)} %get-tuple-element.38), channel_id=1, source_target_pairs={{0,120},{8,0},{16,8},{24,16},{32,24},{40,32},{48,40},{56,48},{64,5... | collective-permute-start | bytes 675848 | tf_op jit(solution)/shard_map/ppermute | solution.py:29
  31.5 39.3 %collective-permute-start.13 = (f32[46,64,128]{2,1,0:T(8,128)}, f32[46,64,128]{2,1,0:T(8,128)}, u32[]{:S(2)}, u32[]{:S(2)}) collective-permute-start(f32[46,64,128]{2,1,0:T(8,128)} %get-tuple-element.47), channel_id=1, source_target_pairs={{0,8},{8,16},{16,24},{24,32},{32,40},{40,48},{48,56},{56,64},{64,7... | collective-permute-start | bytes 4521992 | tf_op jit(solution)/shard_map/ppermute | solution.py:29
  31.6 39.2 %collective-permute-start.14 = (f32[43,64,128]{2,1,0:T(8,128)}, f32[43,64,128]{2,1,0:T(8,128)}, u32[]{:S(2)}, u32[]{:S(2)}) collective-permute-start(f32[43,64,128]{2,1,0:T(8,128)} %get-tuple-element.48), channel_id=1, source_target_pairs={{0,120},{8,0},{16,8},{24,16},{32,24},{40,32},{48,40},{56,48},{64,5... | collective-permute-start | bytes 4227080 | tf_op jit(solution)/shard_map/ppermute | solution.py:29
  37.5 0.7 copy-start.9
  37.5 0.8 copy-start.8
  50.3 5.1 %collective-permute-start.9 = (f32[2,8,128]{2,1,0:T(8,128)}, f32[2,8,128]{2,1,0:T(8,128)S(1)}, u32[]{:S(2)}, u32[]{:S(2)}) collective-permute-start(f32[2,8,128]{2,1,0:T(8,128)} %get-tuple-element.46), channel_id=1, source_target_pairs={{0,2},{2,4},{4,6},{6,0},{1,3},{3,5},{5,7},{7,1},{8,10},{10,12},{12... | collective-permute-start | bytes 24584 | tf_op jit(solution)/shard_map/ppermute | solution.py:29
  50.4 5.1 %collective-permute-start.10 = (f32[2,8,128]{2,1,0:T(8,128)}, f32[2,8,128]{2,1,0:T(8,128)S(1)}, u32[]{:S(2)}, u32[]{:S(2)}) collective-permute-start(f32[2,8,128]{2,1,0:T(8,128)} %get-tuple-element.46), channel_id=1, source_target_pairs={{0,6},{2,0},{4,2},{6,4},{1,7},{3,1},{5,3},{7,5},{8,14},{10,8},{12,... | collective-permute-start | bytes 24584 | tf_op jit(solution)/shard_map/ppermute | solution.py:29
  56.2 13.9 %collective-permute-start.11 = (f32[3,2,8,128]{3,2,1,0:T(8,128)S(1)}, f32[3,2,8,128]{3,2,1,0:T(8,128)S(1)}, u32[]{:S(2)}, u32[]{:S(2)}) collective-permute-start(f32[3,2,8,128]{3,2,1,0:T(8,128)S(1)} %pad_maximum_fusion.1), channel_id=1, source_target_pairs={{0,8},{8,16},{16,24},{24,32},{32,40},{40,48},{48,56},{56,64},{64,7... | collective-permute-start | bytes 73736 | tf_op jit(solution)/shard_map/ppermute | solution.py:29
  56.2 13.9 %collective-permute-start.12 = (f32[3,2,8,128]{3,2,1,0:T(8,128)S(1)}, f32[3,2,8,128]{3,2,1,0:T(8,128)S(1)}, u32[]{:S(2)}, u32[]{:S(2)}) collective-permute-start(f32[3,2,8,128]{3,2,1,0:T(8,128)S(1)} %pad_maximum_fusion.1), channel_id=1, source_target_pairs={{0,120},{8,0},{16,8},{24,16},{32,24},{40,32},{48,40},{56,48},{64,5... | collective-permute-start | bytes 73736 | tf_op jit(solution)/shard_map/ppermute | solution.py:29
  70.8 29.7 %copy-start.2 = (f32[3,2,24,128]{3,2,1,0:T(8,128)}, f32[3,2,24,128]{3,2,1,0:T(8,128)S(1)}, u32[]{:S(2)}) copy-start(f32[3,2,24,128]{3,2,1,0:T(8,128)S(1)} %pad_maximum_fusion.own) | copy-start | bytes 221188
  70.8 29.7 %collective-permute-start.15 = (f32[3,2,24,128]{3,2,1,0:T(8,128)S(1)}, f32[3,2,24,128]{3,2,1,0:T(8,128)S(1)}, u32[]{:S(2)}, u32[]{:S(2)}) collective-permute-start(f32[3,2,24,128]{3,2,1,0:T(8,128)S(1)} %pad_maximum_fusion.own), channel_id=1, source_target_pairs={{1,0},{3,2},{5,4},{7,6},{9,8},{11,10},{13,12},{15,14},{17,16},{19,... | collective-permute-start | bytes 221192 | tf_op jit(solution)/shard_map/ppermute | solution.py:650
  100.5 0.6 copy-start.5

commit v7 on v4

--- a/solution.py
+++ b/solution.py
@@ -15,7 +15,7 @@
 ROWS = 8 + 2 * W
 BASE = 4
 HELD = BASE + ROWS + 2
-CUT = 7
+CUT = 6
 HIGH = 11 - CUT
 LAG = 4
 VMEM = 63 * 1024 * 1024
@@ -297,22 +297,24 @@
     for copy in copies[:early]:
         copy.wait()
 
-    def unpack(r, _):
-        at = BASE + r
-        for t in range(tiles):
-            z = 8 * t
-            v = sv[r, z : z + 8, :]
-            for c in range(NC):
-                turned = pltpu.roll(v, 128 - 16 * c, 1) if c else v
-                if c < 3:
-                    ea1[3 * at + c, 8 + z : 16 + z, :] = turned
-                elif c < 6:
-                    ma1[3 * at + c - 3, 8 + z : 16 + z, :] = turned
-                else:
-                    d1[at, z : z + 8, :] = turned
+    def unpack(i, _):
+        for row in range(2):
+            r = 2 * i + row
+            at = BASE + r
+            for t in range(tiles):
+                z = 8 * t
+                v = sv[r, z : z + 8, :]
+                for c in range(NC):
+                    turned = pltpu.roll(v, 128 - 16 * c, 1) if c else v
+                    if c < 3:
+                        ea1[3 * at + c, 8 + z : 16 + z, :] = turned
+                    elif c < 6:
+                        ma1[3 * at + c - 3, 8 + z : 16 + z, :] = turned
+                    else:
+                        d1[at, z : z + 8, :] = turned
         return 0
 
-    lax.fori_loop(0, ROWS, unpack, 0)
+    lax.fori_loop(0, ROWS // 2, unpack, 0)
     for copy in copies[early:]:
         copy.wait()
 
@@ -327,7 +329,11 @@
 
     live = jnp.where(counts, 1.0, 0.0).astype(F32)
 
-    def tables(r, _):
+    lane = lax.broadcasted_iota(jnp.int32, (8, 128), 1)
+    last, first_lane = lane == 127, lane == 0
+    units = [(row, t) for row in range(2) for t in range(tiles)]
+
+    def tables(r):
         for t in range(tiles):
             z = 8 * t
             for d, g in zip(ds_, gs):
@@ -341,15 +347,8 @@
                     d_cells, g_cells = d_cells * live, g_cells * live
                 d[r, z : z + 8, :] = d_cells
                 g[r, z : z + 8, :] = g_cells
-        return 0
-
-    lax.fori_loop(BASE + 1, BASE + ROWS - 1, tables, 0)
-
-    lane = lax.broadcasted_iota(jnp.int32, (8, 128), 1)
-    last, first_lane = lane == 127, lane == 0
-    units = [(row, t) for row in range(2) for t in range(tiles)]
-
-    def turn_two(which, r0):
+
+    def turn_two(which, r0, beside=None):
         kept = []
         for row, t in units:
             for j, c in enumerate((X, Z)):
@@ -358,13 +357,21 @@
                     for e in es[which]
                 ]
                 kept.append((4 * row + 2 * j, 8 * t, pair))
+        if beside:
+            beside()
         y = yes[which]
         for i, z, (a, b) in kept:
             y[4 * r0 + i, z : z + 8, :] = jnp.where(last, b, a)
             y[4 * r0 + (i + 1), z : z + 8, :] = jnp.where(last, a, b)
 
     def first_turn(i, _):
-        turn_two(0, BASE + 2 * i)
+        r0 = BASE + 2 * i
+
+        def both():
+            tables(r0)
+            tables(r0 + 1)
+
+        turn_two(0, r0, both)
         return 0
 
     lax.fori_loop(0, ROWS // 2, first_turn, 0)
@@ -374,11 +381,11 @@
         base = start + 2 * m
         b3, b4 = 3 * base, 4 * base
         waiting = []
-        jobs = [(ms, row, t) for row, t in units] + [(es, row, t) for row, t in units]
-        jobs = jobs if with_e else []
-
-        def turn():
-            refs, row, t = jobs.pop(0)
+        half = len(units) // 2
+        jobs_m = [(ms, row, t) for row, t in units] if with_e else []
+        jobs_e = [(es, row, t) for row, t in units] if with_e else []
+
+        def turn(refs, row, t):
             z = 8 * t
             if refs is ms:
                 pairs = [
@@ -399,16 +406,16 @@
                 y[b + (i + 2 * j), z : z + 8, :] = jnp.where(edge_lane, v1, v0)
                 y[b + (i + 2 * j + 1), z : z + 8, :] = jnp.where(edge_lane, v0, v1)
 
-        def pace():
-            for _ in range(2):
-                if jobs:
-                    turn()
-            for _ in range(2):
-                if len(waiting) > LAG or (waiting and not jobs):
-                    keep()
-
-        for row, t in units if with_m else ():
-            pace()
+        def settle(most):
+            while len(waiting) > most:
+                keep()
+
+        for u, (row, t) in enumerate(units if with_m else ()):
+            if jobs_m:
+                turn(*jobs_m.pop(0))
+                if u >= half:
+                    turn(*jobs_e.pop(0))
+            settle(LAG)
             z = 8 * t
             for k in range(2):
 
@@ -429,13 +436,13 @@
                 mx, my, mz = magnetic(X) - cx, magnetic(Y) - cy, magnetic(Z) - cz
                 for c, v in ((X, mx), (Y, my), (Z, mz)):
                     ms[new][k][b3 + (3 * row + c), 8 + z : 16 + z, :] = v
-        while jobs:
-            turn()
-            if len(waiting) > LAG:
-                keep()
-        while waiting:
-            keep()
+        for job in jobs_m:
+            turn(*job)
+            settle(LAG)
         for row, t in units if with_e else ():
+            if jobs_e:
+                turn(*jobs_e.pop(0))
+            settle(LAG if jobs_e else max(len(waiting) - 2, 0))
             e, z = row - 2, 8 * t
             for k in range(2):
 
@@ -455,14 +462,15 @@
                 ez = d * electric(Z) + g * ((my - magnetic(Y, e - 1)) - (mx - mx_y))
                 for c, v in ((X, ex), (Y, ey), (Z, ez)):
                     es[new][k][b3 + (3 * e + c), 8 + z : 16 + z, :] = v
+        settle(0)
         return start
 
     def two_steps(s, _):
         for old in range(2):
             left = STEPS - 1 - old - 2 * s
             start = BASE + W - left - 2
-            block(old, False, True, 0, start)
-            lax.fori_loop(1, W - 1 + left, functools.partial(block, old, True, True), start)
+            lax.fori_loop(0, 2, functools.partial(block, old, False, True), start)
+            lax.fori_loop(2, W - 1 + left, functools.partial(block, old, True, True), start)
             block(old, True, False, W - 1 + left, start)
             turn_two(1 - old, start + 2 * (W - 2 + left))
         return 0
@@ -520,8 +528,11 @@
     )(decay, gain, *sides, *arrays)
 
 
-def image_kernel(weights, centre, before, after, out, sh, rhs):
+def image_kernel(weights, own, received, out, sh, rhs):
     gz = lax.axis_index("gz")
+    centre, before, after = [
+        [jnp.where(gz == 1, own[i, c], received[i, c]) for c in range(2)] for i in range(3)
+    ]
     lane = lax.broadcasted_iota(jnp.int32, (24, 128), 1)
     for q in range(15):
         shift = q - 7
@@ -569,19 +580,19 @@
         )
 
 
-def image_of(weights, centre, before, after):
+def image_of(weights, own, received):
     return pl.pallas_call(
         image_kernel,
         out_shape=jax.ShapeDtypeStruct((4, 128), jnp.float32),
-        in_specs=[pl.BlockSpec(memory_space=pltpu.VMEM)] * 4,
-        out_specs=pl.BlockSpec(memory_space=pltpu.VMEM),
+        in_specs=[LOCAL] * 3,
+        out_specs=LOCAL,
         scratch_shapes=[
             pltpu.VMEM((15, 2, 24, 128), jnp.float32),
             pltpu.VMEM((240, 1024), jnp.float32),
         ],
         compiler_params=pltpu.CompilerParams(vmem_limit_bytes=VMEM),
         name="image",
-    )(weights, centre, before, after)
+    )(weights, own, received)
 
 
 def on_device(electric, magnetic, material, decay, gain, kernels):
@@ -597,8 +608,8 @@
     from_low, from_high = around(strips, "gy", 1), around(strips, "gy", -1)
     edge_low, edge_high = beyond(edge_strips, 1), beyond(edge_strips, -1)
     own_u, up_u, down_u = pack(CUT, 10, el, mg, mat)
-    up_u, down_u, edge_low, edge_high = lax.optimization_barrier(
-        (up_u, down_u, edge_low, edge_high)
+    up_u, down_u, edge, edge_low, edge_high = lax.optimization_barrier(
+        (up_u, down_u, edge, edge_low, edge_high)
     )
     low_u, high_u = around(up_u, "gx", 1), around(down_u, "gx", -1)
     strips, up_c, down_c = corners(from_low, from_high, edge_low, edge_high, edge)
@@ -606,16 +617,17 @@
     own_l, up_l, down_l = pack(0, CUT, el, mg, mat, strips)
     low_l, high_l = around(up_l, "gx", 1), around(down_l, "gx", -1)
 
+    low_u, high_u, weights = lax.optimization_barrier((low_u, high_u, weights))
     sides = [low_c, high_c, strips, edge]
     field, plane = run_steps(True, decay, gain, sides, [own_u, low_u, high_u])
     top = jnp.stack([plane, around(plane, "gy", 1), around(plane, "gy", -1)])
-    top = jnp.where(lax.axis_index("gz") == 1, top, lax.ppermute(top, "gz", [(1, 0)]))
+    top = jnp.concatenate([around(top, "gx", 1), top, around(top, "gx", -1)], 2)
     top, low_l, high_l = lax.optimization_barrier((top, low_l, high_l))
-    top = jnp.concatenate([around(top, "gx", 1), top, around(top, "gx", -1)], 2)
+    received = lax.ppermute(top, "gz", [(1, 0)])
     (field,) = run_steps(
         False, decay, gain, sides, [own_u, low_u, high_u, own_l, low_l, high_l, field]
     )
-    image = image_of(weights, top[0], top[1], top[2])
+    image = image_of(weights, top, received)
     return (field.reshape(3, 80, 8, 128), image)
 
 

time: 103 us -> 107 us (1.039)
  waiting for transfers between devices: 5.38 us -> 19.6 us
  starting transfers between devices: 35.8 us -> 29.7 us
  Pallas kernels: 55.1 us -> 52.7 us
    ppermute x13, waiting for transfers between devices: 4.83 us -> 19.5 us  [around(): lax.ppermute(value, axis, [(i, (i + steps) % count) for i in range(count)])]
    ppermute x13, starting transfers between devices: 28.5 us -> 23.9 us  [around(): lax.ppermute(value, axis, [(i, (i + steps) % count) for i in range(count)])]
    pallas_call x2, Pallas kernels: 39.3 us -> 36.9 us  [run_steps(): pl.pallas_call(functools.partial(steps_kernel, upper), out_shape=out_shap...]
    ppermute x2, starting transfers between devices: 4.2 us -> 3.06 us  [beyond(): return lax.ppermute(value, ('gy', 'gz'), pairs)]
  transfers between devices with their start and end apart: 16 -> 16, of which waited for: 3 -> 7; matrix products, arithmetic and copies ran while one was open for 2% -> 2% of each run, Pallas kernels for 48% -> 44%
where the time goes in v7:
time: 107 us; the launch traced here: 106 us
  Pallas kernels  52.7 us (49%)
  starting transfers between devices  29.7 us (28%)
  waiting for transfers between devices  19.6 us (18%)
  local copies, waits for them, and re-layouts  2.26 us (2%)
  other arithmetic  1.4 us (1%)
    pallas_call x2, Pallas kernels, run_steps(): pl.pallas_call(functools.partial(steps_kernel, upper), out_shape=out_shap...  36.9 us
    ppermute x13, starting transfers between devices, around(): lax.ppermute(value, axis, [(i, (i + steps) % count) for i in range(count)])  23.9 us
    ppermute x13, waiting for transfers between devices, around(): lax.ppermute(value, axis, [(i, (i + steps) % count) for i in range(count)])  19.5 us
    pallas_call x2, Pallas kernels, pack(): pl.pallas_call(functools.partial(pack_kernel, first, last), out_shape=[ja...  7.52 us
    pallas_call x1, Pallas kernels, own_strips(): pl.pallas_call(strip_kernel, out_shape=[jax.ShapeDtypeStruct((8, 80, 128)...  3.58 us
    ppermute x2, starting transfers between devices, beyond(): return lax.ppermute(value, ('gy', 'gz'), pairs)  3.06 us
    ppermute x1, starting transfers between devices, on_device(): received = lax.ppermute(top, 'gz', [(1, 0)])  2.79 us
    pallas_call x1, Pallas kernels, image_of(): pl.pallas_call(image_kernel, out_shape=jax.ShapeDtypeStruct((4, 128), jnp...  2.52 us
  transfers between devices with their start and end apart: 16, of which 7 were waited for; matrix products, arithmetic and copies ran while one was open for 2% of the time, Pallas kernels for 44%

profile of v7, /device:TPU:2, one launch (start us, length us, event | category | flops | bytes accessed | tf_op | source)
XLA Modules:
  0.0 106.5 jit_solution(3645216181515200528)
XLA Ops:
  0.6 3.6 %own_strips.1 = (f32[8,80,128]{2,1,0:T(8,128)}, f32[56,8,128]{2,1,0:T(8,128)}, f32[8,8,128]{2,1,0:T(8,128)}) custom-call(f32[3,640,128]{2,1,0:T(8,128)} %bitcast.19, f32[3,640,128]{2,1,0:T(8,128)} %bitcast.22, s32[640,128]{1,0:T(8,128)} %bitcast.25), custom_call_target="tpu_custom_call" | custom-call | flops 3000000000 | bytes 9000000 | tf_op jit(solution)/shard_map/own_strips/pallas_call | solution.py:106
  4.2 3.1 %collective-permute-start.4 = (f32[8,8,128]{2,1,0:T(8,128)}, f32[8,8,128]{2,1,0:T(8,128)S(1)}, u32[]{:S(2)}, u32[]{:S(2)}) collective-permute-start(f32[8,8,128]{2,1,0:T(8,128)} %get-tuple-element.31), channel_id=1, source_target_pairs={{0,7},{1,6},{2,1},{3,0},{4,3},{5,2},{6,5},{7,4},{8,15},{9,14},{10,... | collective-permute-start | bytes 98312 | tf_op jit(solution)/shard_map/ppermute | solution.py:37
  7.3 0.0 collective-permute-start.3
  7.3 4.2 %collective-permute-start.1 = (f32[8,80,128]{2,1,0:T(8,128)}, f32[8,80,128]{2,1,0:T(8,128)}, u32[]{:S(2)}, u32[]{:S(2)}) collective-permute-start(f32[8,80,128]{2,1,0:T(8,128)} %get-tuple-element.27), channel_id=1, source_target_pairs={{0,6},{2,0},{4,2},{6,4},{1,7},{3,1},{5,3},{7,5},{8,14},{10,8},{12,... | collective-permute-start | bytes 983048 | tf_op jit(solution)/shard_map/ppermute | solution.py:29
  11.4 0.0 collective-permute-start
  11.4 0.5 collective-permute-start.2
  12.0 2.9 %pack_upper.1 = (f32[56,32,128]{2,1,0:T(8,128)}, f32[40,32,128]{2,1,0:T(8,128)}, f32[37,32,128]{2,1,0:T(8,128)}) custom-call(f32[3,640,128]{2,1,0:T(8,128)} %bitcast.20, f32[3,640,128]{2,1,0:T(8,128)} %bitcast.23, s32[640,128]{1,0:T(8,128)} %bitcast.26), custom_call_target="tpu_custom_call" | custom-call | flops 20000000000 | bytes 60000000 | tf_op jit(solution)/shard_map/pack_upper/pallas_call | solution.py:167
  14.9 0.0 collective-permute-done.4.edge_high
  14.9 0.0 copy-start.5
  14.9 0.0 collective-permute-done.3.edge_low
  14.9 0.0 copy-start.6
  14.9 3.2 %collective-permute-done.2.edge = f32[56,8,128]{2,1,0:T(8,128)S(1)} collective-permute-done((f32[56,8,128]{2,1,0:T(8,128)}, f32[56,8,128]{2,1,0:T(8,128)S(1)}, u32[]{:S(2)}, u32[]{:S(2)}) %collective-permute-start.2) | collective-permute-done | bytes 229408 | tf_op jit(solution)/shard_map/ppermute | solution.py:29
  18.2 0.0 copy-start.4
  18.2 0.7 copy-done.4
  18.9 0.0 copy-start.1
  18.9 0.0 collective-permute-start.7
  18.9 5.4 %collective-permute-start.8 = (f32[37,32,128]{2,1,0:T(8,128)}, f32[37,32,128]{2,1,0:T(8,128)}, u32[]{:S(2)}, u32[]{:S(2)}) collective-permute-start(f32[37,32,128]{2,1,0:T(8,128)} %get-tuple-element.40), channel_id=1, source_target_pairs={{0,120},{8,0},{16,8},{24,16},{32,24},{40,32},{48,40},{56,48},{64,5... | collective-permute-start | bytes 1818632 | tf_op jit(solution)/shard_map/ppermute | solution.py:29
  24.2 0.0 collective-permute-done.1.from_high
  24.2 0.0 collective-permute-done.from_low
  24.2 0.0 copy-done.5
  24.2 0.0 copy-done.6
  24.2 2.2 %corners.1 = (f32[8,88,128]{2,1,0:T(8,128)}, f32[70,8,128]{2,1,0:T(8,128)}, f32[67,8,128]{2,1,0:T(8,128)}) custom-call(f32[8,80,128]{2,1,0:T(8,128)} %collective-permute-done.from_low, f32[8,80,128]{2,1,0:T(8,128)} %collective-permute-done.1.from_high, f32[8,8,128]{2,1,0:T(8,128)} %copy-done.6, f32[8,8,128]{2,1,0:T(8,128)} %copy-done.5, f32[56,8,128]{2,1,0:T(8,128)} %copy-done.4), custom_call_target="tpu_custom_call" | custom-call | flops 1000000000 | bytes 3000000 | tf_op jit(solution)/shard_map/corners/pallas_call | solution.py:205
  26.4 0.0 collective-permute-start.5
  26.4 0.0 copy-done.1
  26.4 0.2 reshape.25
  26.7 5.4 %collective-permute-start.6 = (f32[67,8,128]{2,1,0:T(8,128)}, f32[67,8,128]{2,1,0:T(8,128)}, u32[]{:S(2)}, u32[]{:S(2)}) collective-permute-start(f32[67,8,128]{2,1,0:T(8,128)} %get-tuple-element.36), channel_id=1, source_target_pairs={{0,120},{8,0},{16,8},{24,16},{32,24},{40,32},{48,40},{56,48},{64,5... | collective-permute-start | bytes 823304 | tf_op jit(solution)/shard_map/ppermute | solution.py:29
  32.1 4.6 %pack_lower.1 = (f32[56,48,128]{2,1,0:T(8,128)}, f32[46,48,128]{2,1,0:T(8,128)}, f32[43,48,128]{2,1,0:T(8,128)}) custom-call(f32[3,640,128]{2,1,0:T(8,128)} %bitcast.21, f32[3,640,128]{2,1,0:T(8,128)} %bitcast.24, s32[640,128]{1,0:T(8,128)} %bitcast.27, f32[8,88,128]{2,1,0:T(8,128)} %get-tuple-element.37.refs_0_.strips), custom_call_target="tpu_custom_call" | custom-call | flops 3000000000 | bytes 9000000 | tf_op jit(solution)/shard_map/pack_lower/pallas_call | solution.py:167
  36.7 0.1 collective-permute-start.14
  36.8 1.6 %collective-permute-done.8.refs_2_ = f32[37,32,128]{2,1,0:T(8,128)} collective-permute-done((f32[37,32,128]{2,1,0:T(8,128)}, f32[37,32,128]{2,1,0:T(8,128)}, u32[]{:S(2)}, u32[]{:S(2)}) %collective-permute-start.8) | collective-permute-done | bytes 606240 | tf_op jit(solution)/shard_map/ppermute | solution.py:29
  38.4 0.8 collective-permute-start.13
  39.2 0.0 collective-permute-done.7.refs_1_
  39.2 0.0 copy-start.3
  39.2 3.5 %collective-permute-done.6.high_c = f32[67,8,128]{2,1,0:T(8,128)} collective-permute-done((f32[67,8,128]{2,1,0:T(8,128)}, f32[67,8,128]{2,1,0:T(8,128)}, u32[]{:S(2)}, u32[]{:S(2)}) %collective-permute-start.6) | collective-permute-done | bytes 274464 | tf_op jit(solution)/shard_map/ppermute | solution.py:29
  42.7 0.0 collective-permute-done.5.low_c
  42.7 0.0 copy-done.3
  42.7 15.1 %steps_upper.1 = (f32[3,640,128]{2,1,0:T(8,128)}, f32[2,8,128]{2,1,0:T(8,128)}) custom-call(f32[5]{0:T(128)} %decay.3, f32[5]{0:T(128)} %gain.3, f32[70,8,128]{2,1,0:T(8,128)} %collective-permute-done.5.low_c, f32[67,8,128]{2,1,0:T(8,128)} %collective-permute-done.6.high_c, f32[8,88,128]{2,1,0:T(8,128)} %get-tuple-element.37.refs_0_.strips, ...), custom_call_target="tpu_custom_call" | custom-call | flops 99999997952 | bytes 300000000 | tf_op jit(solution)/shard_map/steps_upper/pallas_call | solution.py:510
  57.8 3.0 %collective-permute-start.10 = (f32[2,8,128]{2,1,0:T(8,128)}, f32[2,8,128]{2,1,0:T(8,128)S(1)}, u32[]{:S(2)}, u32[]{:S(2)}) collective-permute-start(f32[2,8,128]{2,1,0:T(8,128)} %get-tuple-element.44), channel_id=1, source_target_pairs={{0,6},{2,0},{4,2},{6,4},{1,7},{3,1},{5,3},{7,5},{8,14},{10,8},{12,... | collective-permute-start | bytes 24584 | tf_op jit(solution)/shard_map/ppermute | solution.py:29
  60.9 0.0 collective-permute-start.9
  60.9 1.6 %collective-permute-done.10 = f32[2,8,128]{2,1,0:T(8,128)S(1)} collective-permute-done((f32[2,8,128]{2,1,0:T(8,128)}, f32[2,8,128]{2,1,0:T(8,128)S(1)}, u32[]{:S(2)}, u32[]{:S(2)}) %collective-permute-start.10) | collective-permute-done | bytes 8224 | tf_op jit(solution)/shard_map/ppermute | solution.py:29
  62.4 3.5 %collective-permute-done.9 = f32[2,8,128]{2,1,0:T(8,128)S(1)} collective-permute-done((f32[2,8,128]{2,1,0:T(8,128)}, f32[2,8,128]{2,1,0:T(8,128)S(1)}, u32[]{:S(2)}, u32[]{:S(2)}) %collective-permute-start.9) | collective-permute-done | bytes 8224 | tf_op jit(solution)/shard_map/ppermute | solution.py:29
  65.9 0.7 pad_maximum_fusion.1
  66.6 4.5 %collective-permute-start.12 = (f32[3,2,8,128]{3,2,1,0:T(8,128)S(1)}, f32[3,2,8,128]{3,2,1,0:T(8,128)S(1)}, u32[]{:S(2)}, u32[]{:S(2)}) collective-permute-start(f32[3,2,8,128]{3,2,1,0:T(8,128)S(1)} %pad_maximum_fusion.1), channel_id=1, source_target_pairs={{0,120},{8,0},{16,8},{24,16},{32,24},{40,32},{48,40},{56,48},{64,5... | collective-permute-start | bytes 73736 | tf_op jit(solution)/shard_map/ppermute | solution.py:29
  71.1 0.0 collective-permute-start.11
  71.1 0.7 copy.11.weights
  71.8 0.8 collective-permute-done.12
  72.7 5.3 %collective-permute-done.11 = f32[3,2,8,128]{3,2,1,0:T(8,128)S(1)} collective-permute-done((f32[3,2,8,128]{3,2,1,0:T(8,128)S(1)}, f32[3,2,8,128]{3,2,1,0:T(8,128)S(1)}, u32[]{:S(2)}, u32[]{:S(2)}) %collective-permute-start.11) | collective-permute-done | bytes 24608 | tf_op jit(solution)/shard_map/ppermute | solution.py:29
  78.0 0.7 pad_maximum_fusion.own
  78.7 0.0 copy-start
  78.7 0.0 collective-permute-done.14.refs_5_
  78.7 0.0 collective-permute-done.13.refs_4_
  78.7 2.8 %collective-permute-start.15 = (f32[3,2,24,128]{3,2,1,0:T(8,128)S(1)}, f32[3,2,24,128]{3,2,1,0:T(8,128)S(1)}, u32[]{:S(2)}, u32[]{:S(2)}) collective-permute-start(f32[3,2,24,128]{3,2,1,0:T(8,128)S(1)} %pad_maximum_fusion.own), channel_id=1, source_target_pairs={{1,0},{3,2},{5,4},{7,6},{9,8},{11,10},{13,12},{15,14},{17,16},{19,... | collective-permute-start | bytes 221192 | tf_op jit(solution)/shard_map/ppermute | solution.py:626
  81.5 21.8 %steps_lower.1 = f32[3,640,128]{2,1,0:T(8,128)} custom-call(f32[5]{0:T(128)} %decay.3, f32[5]{0:T(128)} %gain.3, f32[70,8,128]{2,1,0:T(8,128)} %collective-permute-done.5.low_c, f32[67,8,128]{2,1,0:T(8,128)} %collective-permute-done.6.high_c, f32[8,88,128]{2,1,0:T(8,128)} %get-tuple-element.37.refs_0_.strips, ...), custom_call_target="tpu_custom_call", output_to_operand_aliasing={{}: (12, {})} | custom-call | flops 99999997952 | bytes 300000000 | tf_op jit(solution)/shard_map/steps_lower/pallas_call | solution.py:510
  103.3 0.0 copy-done
  103.3 0.0 collective-permute-done.15.received
  103.3 0.0 copy-start.2
  103.3 0.6 copy-done.2
  103.9 2.5 %image.1 = f32[4,128]{1,0:T(4,128)} custom-call(f32[48,240]{1,0:T(8,128)} %copy.11.weights, f32[3,2,24,128]{3,2,1,0:T(8,128)} %copy-done, f32[3,2,24,128]{3,2,1,0:T(8,128)} %copy-done.2), custom_call_target="tpu_custom_call" | custom-call | tf_op jit(solution)/shard_map/image/pallas_call | solution.py:584
  (2 shorter events, 0.1 us)
Async XLA Ops:
  4.2 10.7 %collective-permute-start.4 = (f32[8,8,128]{2,1,0:T(8,128)}, f32[8,8,128]{2,1,0:T(8,128)S(1)}, u32[]{:S(2)}, u32[]{:S(2)}) collective-permute-start(f32[8,8,128]{2,1,0:T(8,128)} %get-tuple-element.31), channel_id=1, source_target_pairs={{0,7},{1,6},{2,1},{3,0},{4,3},{5,2},{6,5},{7,4},{8,15},{9,14},{10,... | collective-permute-start | bytes 98312 | tf_op jit(solution)/shard_map/ppermute | solution.py:37
  7.3 7.6 %collective-permute-start.3 = (f32[8,8,128]{2,1,0:T(8,128)}, f32[8,8,128]{2,1,0:T(8,128)S(1)}, u32[]{:S(2)}, u32[]{:S(2)}) collective-permute-start(f32[8,8,128]{2,1,0:T(8,128)} %get-tuple-element.31), channel_id=1, source_target_pairs={{0,3},{1,2},{2,5},{3,4},{4,7},{5,6},{6,1},{7,0},{8,11},{9,10},{10,... | collective-permute-start | bytes 98312 | tf_op jit(solution)/shard_map/ppermute | solution.py:37
  7.3 16.9 %collective-permute-start.1 = (f32[8,80,128]{2,1,0:T(8,128)}, f32[8,80,128]{2,1,0:T(8,128)}, u32[]{:S(2)}, u32[]{:S(2)}) collective-permute-start(f32[8,80,128]{2,1,0:T(8,128)} %get-tuple-element.27), channel_id=1, source_target_pairs={{0,6},{2,0},{4,2},{6,4},{1,7},{3,1},{5,3},{7,5},{8,14},{10,8},{12,... | collective-permute-start | bytes 983048 | tf_op jit(solution)/shard_map/ppermute | solution.py:29
  11.4 12.8 %collective-permute-start = (f32[8,80,128]{2,1,0:T(8,128)}, f32[8,80,128]{2,1,0:T(8,128)}, u32[]{:S(2)}, u32[]{:S(2)}) collective-permute-start(f32[8,80,128]{2,1,0:T(8,128)} %get-tuple-element.27), channel_id=1, source_target_pairs={{0,2},{2,4},{4,6},{6,0},{1,3},{3,5},{5,7},{7,1},{8,10},{10,12},{12... | collective-permute-start | bytes 983048 | tf_op jit(solution)/shard_map/ppermute | solution.py:29
  11.4 6.7 %collective-permute-start.2 = (f32[56,8,128]{2,1,0:T(8,128)}, f32[56,8,128]{2,1,0:T(8,128)S(1)}, u32[]{:S(2)}, u32[]{:S(2)}) collective-permute-start(f32[56,8,128]{2,1,0:T(8,128)} %get-tuple-element.30), channel_id=1, source_target_pairs={{0,1},{1,0},{2,3},{3,2},{4,5},{5,4},{6,7},{7,6},{8,9},{9,8},{10,11... | collective-permute-start | bytes 688136 | tf_op jit(solution)/shard_map/ppermute | solution.py:29
  14.9 9.3 %copy-start.5 = (f32[8,8,128]{2,1,0:T(8,128)}, f32[8,8,128]{2,1,0:T(8,128)S(1)}, u32[]{:S(2)}) copy-start(f32[8,8,128]{2,1,0:T(8,128)S(1)} %collective-permute-done.4.edge_high) | copy-start | bytes 98308
  14.9 9.3 %copy-start.6 = (f32[8,8,128]{2,1,0:T(8,128)}, f32[8,8,128]{2,1,0:T(8,128)S(1)}, u32[]{:S(2)}) copy-start(f32[8,8,128]{2,1,0:T(8,128)S(1)} %collective-permute-done.3.edge_low) | copy-start | bytes 98308
  18.2 0.7 copy-start.4
  18.9 7.6 %copy-start.1 = (f32[2,24,15,15]{1,0,3,2:T(2,128)S(1)}, f32[2,24,15,15]{1,0,3,2:T(2,128)}, u32[]{:S(2)}) copy-start(f32[2,24,15,15]{1,0,3,2:T(2,128)} %param.11) | copy-start | bytes 129604
  18.9 20.3 %collective-permute-start.7 = (f32[40,32,128]{2,1,0:T(8,128)}, f32[40,32,128]{2,1,0:T(8,128)S(1)}, u32[]{:S(2)}, u32[]{:S(2)}) collective-permute-start(f32[40,32,128]{2,1,0:T(8,128)} %get-tuple-element.39), channel_id=1, source_target_pairs={{0,8},{8,16},{16,24},{24,32},{32,40},{40,48},{48,56},{56,64},{64,7... | collective-permute-start | bytes 1966088 | tf_op jit(solution)/shard_map/ppermute | solution.py:29
  18.9 19.5 %collective-permute-start.8 = (f32[37,32,128]{2,1,0:T(8,128)}, f32[37,32,128]{2,1,0:T(8,128)}, u32[]{:S(2)}, u32[]{:S(2)}) collective-permute-start(f32[37,32,128]{2,1,0:T(8,128)} %get-tuple-element.40), channel_id=1, source_target_pairs={{0,120},{8,0},{16,8},{24,16},{32,24},{40,32},{48,40},{56,48},{64,5... | collective-permute-start | bytes 1818632 | tf_op jit(solution)/shard_map/ppermute | solution.py:29
  26.4 16.3 %collective-permute-start.5 = (f32[70,8,128]{2,1,0:T(8,128)}, f32[70,8,128]{2,1,0:T(8,128)}, u32[]{:S(2)}, u32[]{:S(2)}) collective-permute-start(f32[70,8,128]{2,1,0:T(8,128)} %get-tuple-element.35), channel_id=1, source_target_pairs={{0,8},{8,16},{16,24},{24,32},{32,40},{40,48},{48,56},{56,64},{64,7... | collective-permute-start | bytes 860168 | tf_op jit(solution)/shard_map/ppermute | solution.py:29
  26.7 16.0 %collective-permute-start.6 = (f32[67,8,128]{2,1,0:T(8,128)}, f32[67,8,128]{2,1,0:T(8,128)}, u32[]{:S(2)}, u32[]{:S(2)}) collective-permute-start(f32[67,8,128]{2,1,0:T(8,128)} %get-tuple-element.36), channel_id=1, source_target_pairs={{0,120},{8,0},{16,8},{24,16},{32,24},{40,32},{48,40},{56,48},{64,5... | collective-permute-start | bytes 823304 | tf_op jit(solution)/shard_map/ppermute | solution.py:29
  36.7 42.0 %collective-permute-start.14 = (f32[43,48,128]{2,1,0:T(8,128)}, f32[43,48,128]{2,1,0:T(8,128)}, u32[]{:S(2)}, u32[]{:S(2)}) collective-permute-start(f32[43,48,128]{2,1,0:T(8,128)} %get-tuple-element.46), channel_id=1, source_target_pairs={{0,120},{8,0},{16,8},{24,16},{32,24},{40,32},{48,40},{56,48},{64,5... | collective-permute-start | bytes 3170312 | tf_op jit(solution)/shard_map/ppermute | solution.py:29
  38.4 40.3 %collective-permute-start.13 = (f32[46,48,128]{2,1,0:T(8,128)}, f32[46,48,128]{2,1,0:T(8,128)}, u32[]{:S(2)}, u32[]{:S(2)}) collective-permute-start(f32[46,48,128]{2,1,0:T(8,128)} %get-tuple-element.45), channel_id=1, source_target_pairs={{0,8},{8,16},{16,24},{24,32},{32,40},{40,48},{48,56},{56,64},{64,7... | collective-permute-start | bytes 3391496 | tf_op jit(solution)/shard_map/ppermute | solution.py:29
  39.2 3.5 %copy-start.3 = (f32[40,32,128]{2,1,0:T(8,128)}, f32[40,32,128]{2,1,0:T(8,128)S(1)}, u32[]{:S(2)}) copy-start(f32[40,32,128]{2,1,0:T(8,128)S(1)} %collective-permute-done.7.refs_1_) | copy-start | bytes 1966084
  57.8 4.6 %collective-permute-start.10 = (f32[2,8,128]{2,1,0:T(8,128)}, f32[2,8,128]{2,1,0:T(8,128)S(1)}, u32[]{:S(2)}, u32[]{:S(2)}) collective-permute-start(f32[2,8,128]{2,1,0:T(8,128)} %get-tuple-element.44), channel_id=1, source_target_pairs={{0,6},{2,0},{4,2},{6,4},{1,7},{3,1},{5,3},{7,5},{8,14},{10,8},{12,... | collective-permute-start | bytes 24584 | tf_op jit(solution)/shard_map/ppermute | solution.py:29
  60.9 5.1 %collective-permute-start.9 = (f32[2,8,128]{2,1,0:T(8,128)}, f32[2,8,128]{2,1,0:T(8,128)S(1)}, u32[]{:S(2)}, u32[]{:S(2)}) collective-permute-start(f32[2,8,128]{2,1,0:T(8,128)} %get-tuple-element.44), channel_id=1, source_target_pairs={{0,2},{2,4},{4,6},{6,0},{1,3},{3,5},{5,7},{7,1},{8,10},{10,12},{12... | collective-permute-start | bytes 24584 | tf_op jit(solution)/shard_map/ppermute | solution.py:29
  66.6 6.0 %collective-permute-start.12 = (f32[3,2,8,128]{3,2,1,0:T(8,128)S(1)}, f32[3,2,8,128]{3,2,1,0:T(8,128)S(1)}, u32[]{:S(2)}, u32[]{:S(2)}) collective-permute-start(f32[3,2,8,128]{3,2,1,0:T(8,128)S(1)} %pad_maximum_fusion.1), channel_id=1, source_target_pairs={{0,120},{8,0},{16,8},{24,16},{32,24},{40,32},{48,40},{56,48},{64,5... | collective-permute-start | bytes 73736 | tf_op jit(solution)/shard_map/ppermute | solution.py:29
  71.1 6.9 %collective-permute-start.11 = (f32[3,2,8,128]{3,2,1,0:T(8,128)S(1)}, f32[3,2,8,128]{3,2,1,0:T(8,128)S(1)}, u32[]{:S(2)}, u32[]{:S(2)}) collective-permute-start(f32[3,2,8,128]{3,2,1,0:T(8,128)S(1)} %pad_maximum_fusion.1), channel_id=1, source_target_pairs={{0,8},{8,16},{16,24},{24,32},{32,40},{40,48},{48,56},{56,64},{64,7... | collective-permute-start | bytes 73736 | tf_op jit(solution)/shard_map/ppermute | solution.py:29
  78.7 24.6 %copy-start = (f32[3,2,24,128]{3,2,1,0:T(8,128)}, f32[3,2,24,128]{3,2,1,0:T(8,128)S(1)}, u32[]{:S(2)}) copy-start(f32[3,2,24,128]{3,2,1,0:T(8,128)S(1)} %pad_maximum_fusion.own) | copy-start | bytes 221188
  78.7 24.6 %collective-permute-start.15 = (f32[3,2,24,128]{3,2,1,0:T(8,128)S(1)}, f32[3,2,24,128]{3,2,1,0:T(8,128)S(1)}, u32[]{:S(2)}, u32[]{:S(2)}) collective-permute-start(f32[3,2,24,128]{3,2,1,0:T(8,128)S(1)} %pad_maximum_fusion.own), channel_id=1, source_target_pairs={{1,0},{3,2},{5,4},{7,6},{9,8},{11,10},{13,12},{15,14},{17,16},{19,... | collective-permute-start | bytes 221192 | tf_op jit(solution)/shard_map/ppermute | solution.py:626
  103.3 0.6 copy-start.2

commit v8 on v6

--- a/solution.py
+++ b/solution.py
@@ -15,7 +15,7 @@
 ROWS = 8 + 2 * W
 BASE = 4
 HELD = BASE + ROWS + 2
-CUT = 8
+CUT = 7
 HIGH = 11 - CUT
 LAG = 4
 VMEM = 63 * 1024 * 1024
@@ -641,7 +641,6 @@
     low_c, high_c = around(up_c, "gx", 1), around(down_c, "gx", -1)
     low_l, high_l = around(up_l, "gx", 1), around(down_l, "gx", -1)
 
-    low_u, high_u, weights = lax.optimization_barrier((low_u, high_u, weights))
     sides = [low_c, high_c, strips, edge]
     field, plane = run_steps(True, decay, gain, sides, [own_u, low_u, high_u])
     top = jnp.stack([plane, around(plane, "gy", 1), around(plane, "gy", -1)])

time: 104 us -> 96.4 us (0.927)
  Pallas kernels: 51.5 us -> 47.6 us
  waiting for transfers between devices: 10.3 us -> 6.69 us
    pallas_call x2, Pallas kernels: 38.2 us -> 34.2 us  [run_steps(): pl.pallas_call(functools.partial(steps_kernel, upper), out_shape=out_shap...]
    ppermute x13, waiting for transfers between devices: 10.3 us -> 6.68 us  [around(): lax.ppermute(value, axis, [(i, (i + steps) % count) for i in range(count)])]
    unnamed x20 -> x18, local copies, waits for them, and re-layouts: 2.3 us -> 2.19 us
  transfers between devices with their start and end apart: 16 -> 16, of which waited for: 3 -> 3; matrix products, arithmetic and copies ran while one was open for 2% -> 2% of each run, Pallas kernels for 44% -> 43%
where the time goes in v8:
time: 96.4 us; the launch traced here: 95.9 us
  Pallas kernels  47.6 us (49%)
  starting transfers between devices  36.3 us (38%)
  waiting for transfers between devices  6.69 us (7%)
  local copies, waits for them, and re-layouts  3.11 us (3%)
  other arithmetic  1.4 us (1%)
    pallas_call x2, Pallas kernels, run_steps(): pl.pallas_call(functools.partial(steps_kernel, upper), out_shape=out_shap...  34.2 us
    ppermute x13, starting transfers between devices, around(): lax.ppermute(value, axis, [(i, (i + steps) % count) for i in range(count)])  28.6 us
    ppermute x13, waiting for transfers between devices, around(): lax.ppermute(value, axis, [(i, (i + steps) % count) for i in range(count)])  6.68 us
    pallas_call x1, Pallas kernels, pack(): pl.pallas_call(pack_kernel, out_shape=shapes, in_specs=[HBM] * 3, out_spe...  4.32 us
    ppermute x2, starting transfers between devices, beyond(): return lax.ppermute(value, ('gy', 'gz'), pairs)  4.2 us
    pallas_call x1, Pallas kernels, own_strips(): pl.pallas_call(strip_kernel, out_shape=[jax.ShapeDtypeStruct((8, 80, 128)...  3.62 us
    ppermute x1, starting transfers between devices, on_device(): received = lax.ppermute(top, 'gz', [(1, 0)])  3.48 us
    pallas_call x1, Pallas kernels, corners(): pl.pallas_call(corner_kernel, out_shape=[jax.ShapeDtypeStruct((8, 88, 128...  2.92 us
  transfers between devices with their start and end apart: 16, of which 3 were waited for; matrix products, arithmetic and copies ran while one was open for 2% of the time, Pallas kernels for 43%

profile of v8, /device:TPU:2, one launch (start us, length us, event | category | flops | bytes accessed | tf_op | source)
XLA Modules:
  0.0 95.9 jit_solution(15607924541781735366)
XLA Ops:
  0.6 3.6 %own_strips.1 = (f32[8,80,128]{2,1,0:T(8,128)}, f32[56,8,128]{2,1,0:T(8,128)}, f32[8,8,128]{2,1,0:T(8,128)}) custom-call(f32[3,640,128]{2,1,0:T(8,128)} %bitcast.19, f32[3,640,128]{2,1,0:T(8,128)} %bitcast.21, s32[640,128]{1,0:T(8,128)} %bitcast.23), custom_call_target="tpu_custom_call" | custom-call | flops 3000000000 | bytes 9000000 | tf_op jit(solution)/shard_map/own_strips/pallas_call | solution.py:106
  4.3 1.6 %collective-permute-start.2 = (f32[8,8,128]{2,1,0:T(8,128)}, f32[8,8,128]{2,1,0:T(8,128)S(1)}, u32[]{:S(2)}, u32[]{:S(2)}) collective-permute-start(f32[8,8,128]{2,1,0:T(8,128)} %get-tuple-element.28), channel_id=1, source_target_pairs={{0,3},{1,2},{2,5},{3,4},{4,7},{5,6},{6,1},{7,0},{8,11},{9,10},{10,... | collective-permute-start | bytes 98312 | tf_op jit(solution)/shard_map/ppermute | solution.py:37
  5.9 2.6 %collective-permute-start.3 = (f32[8,8,128]{2,1,0:T(8,128)}, f32[8,8,128]{2,1,0:T(8,128)S(1)}, u32[]{:S(2)}, u32[]{:S(2)}) collective-permute-start(f32[8,8,128]{2,1,0:T(8,128)} %get-tuple-element.28), channel_id=1, source_target_pairs={{0,7},{1,6},{2,1},{3,0},{4,3},{5,2},{6,5},{7,4},{8,15},{9,14},{10,... | collective-permute-start | bytes 98312 | tf_op jit(solution)/shard_map/ppermute | solution.py:37
  8.5 0.4 collective-permute-start
  8.8 2.9 %collective-permute-start.1 = (f32[8,80,128]{2,1,0:T(8,128)}, f32[8,80,128]{2,1,0:T(8,128)}, u32[]{:S(2)}, u32[]{:S(2)}) collective-permute-start(f32[8,80,128]{2,1,0:T(8,128)} %get-tuple-element.25), channel_id=1, source_target_pairs={{0,6},{2,0},{4,2},{6,4},{1,7},{3,1},{5,3},{7,5},{8,14},{10,8},{12,... | collective-permute-start | bytes 983048 | tf_op jit(solution)/shard_map/ppermute | solution.py:29
  11.7 0.5 collective-permute-start.4
  12.1 4.3 %pack.1 = (f32[56,24,128]{2,1,0:T(8,128)}, f32[40,24,128]{2,1,0:T(8,128)}, f32[37,24,128]{2,1,0:T(8,128)}, f32[56,56,128]{2,1,0:T(8,128)}, f32[46,56,128]{2,1,0:T(8,128)}, /*index=5*/f32[43,56,128]{2,1,0:T(8,128)}) custom-call(f32[3,640,128]{2,1,0:T(8,128)} %bitcast.20, f32[3,640,128]{2,1,0:T(8,128)} %bitcast.22, s32[640,128]{1,0:T(8,128)} %bitcast.24), custom_call_target="tpu_custom_call" | custom-call | flops 20000000000 | bytes 60000000 | tf_op jit(solution)/shard_map/pack/pallas_call | solution.py:180
  16.5 0.0 collective-permute-done.2.edge_low
  16.5 0.0 copy-start.7
  16.5 0.0 collective-permute-done.3.edge_high
  16.5 0.0 copy-start.8
  16.5 0.6 copy-done.8
  17.1 0.0 collective-permute-start.7
  17.1 5.4 %collective-permute-start.8 = (f32[37,24,128]{2,1,0:T(8,128)}, f32[37,24,128]{2,1,0:T(8,128)S(1)}, u32[]{:S(2)}, u32[]{:S(2)}) collective-permute-start(f32[37,24,128]{2,1,0:T(8,128)} %get-tuple-element.39), channel_id=1, source_target_pairs={{0,120},{8,0},{16,8},{24,16},{32,24},{40,32},{48,40},{56,48},{64,5... | collective-permute-start | bytes 1363976 | tf_op jit(solution)/shard_map/ppermute | solution.py:29
  22.5 0.0 collective-permute-done.4.edge
  22.5 0.0 collective-permute-done.from_low
  22.5 0.0 collective-permute-done.1.from_high
  22.5 0.0 copy-done.7
  22.5 2.9 %corners.1 = (f32[8,88,128]{2,1,0:T(8,128)}, f32[64,8,128]{2,1,0:T(8,128)}, f32[61,8,128]{2,1,0:T(8,128)}, f32[46,56,128]{2,1,0:T(8,128)}, f32[43,56,128]{2,1,0:T(8,128)}) custom-call(f32[8,80,128]{2,1,0:T(8,128)} %collective-permute-done.from_low, f32[8,80,128]{2,1,0:T(8,128)} %collective-permute-done.1.from_high, ...), custom_call_target="tpu_custom_call", output_to_operand_aliasing={{3}: (5, {}), {4}: (6, {})} | custom-call | flops 1000000000 | bytes 3000000 | tf_op jit(solution)/shard_map/corners/pallas_call | solution.py:224
  25.4 0.1 collective-permute-start.5
  25.5 5.3 %collective-permute-start.6 = (f32[61,8,128]{2,1,0:T(8,128)}, f32[61,8,128]{2,1,0:T(8,128)S(1)}, u32[]{:S(2)}, u32[]{:S(2)}) collective-permute-start(f32[61,8,128]{2,1,0:T(8,128)} %get-tuple-element.35), channel_id=1, source_target_pairs={{0,120},{8,0},{16,8},{24,16},{32,24},{40,32},{48,40},{56,48},{64,5... | collective-permute-start | bytes 749576 | tf_op jit(solution)/shard_map/ppermute | solution.py:29
  30.9 0.0 collective-permute-start.13
  30.9 2.8 %collective-permute-done.8.refs_2_ = f32[37,24,128]{2,1,0:T(8,128)S(1)} collective-permute-done((f32[37,24,128]{2,1,0:T(8,128)}, f32[37,24,128]{2,1,0:T(8,128)S(1)}, u32[]{:S(2)}, u32[]{:S(2)}) %collective-permute-start.8) | collective-permute-done | bytes 454688 | tf_op jit(solution)/shard_map/ppermute | solution.py:29
  33.7 0.0 copy-start.4
  33.7 5.4 %collective-permute-start.14 = (f32[43,56,128]{2,1,0:T(8,128)}, f32[43,56,128]{2,1,0:T(8,128)}, u32[]{:S(2)}, u32[]{:S(2)}) collective-permute-start(f32[43,56,128]{2,1,0:T(8,128)} %get-tuple-element.43), channel_id=1, source_target_pairs={{0,120},{8,0},{16,8},{24,16},{32,24},{40,32},{48,40},{56,48},{64,5... | collective-permute-start | bytes 3698696 | tf_op jit(solution)/shard_map/ppermute | solution.py:29
  39.1 0.0 collective-permute-done.7.refs_1_
  39.1 0.0 copy-start.3
  39.1 0.0 collective-permute-done.6.high_c
  39.1 0.0 copy-start.6
  39.1 0.0 collective-permute-done.5.low_c
  39.1 0.0 copy-start.5
  39.1 0.0 copy-done.4
  39.1 0.7 copy-done.6
  39.9 0.1 copy-done.5
  39.9 0.2 copy-done.3
  40.1 0.0 copy-start.1
  40.1 12.5 %steps_upper.1 = (f32[3,640,128]{2,1,0:T(8,128)}, f32[2,8,128]{2,1,0:T(8,128)}) custom-call(f32[5]{0:T(128)} %decay.3, f32[5]{0:T(128)} %gain.3, f32[64,8,128]{2,1,0:T(8,128)} %copy-done.5, f32[61,8,128]{2,1,0:T(8,128)} %copy-done.6, f32[8,88,128]{2,1,0:T(8,128)} %get-tuple-element.36.strips, f32[56,8,128]{2,1,0:T(8,128)} %collective-permute-done.4.edge, ...), custom_call_target="tpu_custom_call" | custom-call | flops 99999997952 | bytes 300000000 | tf_op jit(solution)/shard_map/steps_upper/pallas_call | solution.py:533
  52.6 0.1 collective-permute-start.9
  52.7 3.3 %collective-permute-start.10 = (f32[2,8,128]{2,1,0:T(8,128)}, f32[2,8,128]{2,1,0:T(8,128)S(1)}, u32[]{:S(2)}, u32[]{:S(2)}) collective-permute-start(f32[2,8,128]{2,1,0:T(8,128)} %get-tuple-element.41), channel_id=1, source_target_pairs={{0,6},{2,0},{4,2},{6,4},{1,7},{3,1},{5,3},{7,5},{8,14},{10,8},{12,... | collective-permute-start | bytes 24584 | tf_op jit(solution)/shard_map/ppermute | solution.py:29
  55.9 1.8 %collective-permute-done.9 = f32[2,8,128]{2,1,0:T(8,128)S(1)} collective-permute-done((f32[2,8,128]{2,1,0:T(8,128)}, f32[2,8,128]{2,1,0:T(8,128)S(1)}, u32[]{:S(2)}, u32[]{:S(2)}) %collective-permute-start.9) | collective-permute-done | bytes 8224 | tf_op jit(solution)/shard_map/ppermute | solution.py:29
  57.7 0.0 collective-permute-done.10
  57.8 0.7 pad_maximum_fusion.1
  58.5 0.0 collective-permute-start.11
  58.5 5.4 %collective-permute-start.12 = (f32[3,2,8,128]{3,2,1,0:T(8,128)S(1)}, f32[3,2,8,128]{3,2,1,0:T(8,128)S(1)}, u32[]{:S(2)}, u32[]{:S(2)}) collective-permute-start(f32[3,2,8,128]{3,2,1,0:T(8,128)S(1)} %pad_maximum_fusion.1), channel_id=1, source_target_pairs={{0,120},{8,0},{16,8},{24,16},{32,24},{40,32},{48,40},{56,48},{64,5... | collective-permute-start | bytes 73736 | tf_op jit(solution)/shard_map/ppermute | solution.py:29
  63.8 0.0 copy-done.1
  63.8 0.2 reshape.26
  64.1 0.7 copy.13.weights
  64.8 2.0 %collective-permute-done.11 = f32[3,2,8,128]{3,2,1,0:T(8,128)S(1)} collective-permute-done((f32[3,2,8,128]{3,2,1,0:T(8,128)S(1)}, f32[3,2,8,128]{3,2,1,0:T(8,128)S(1)}, u32[]{:S(2)}, u32[]{:S(2)}) %collective-permute-start.11) | collective-permute-done | bytes 24608 | tf_op jit(solution)/shard_map/ppermute | solution.py:29
  66.8 0.0 collective-permute-done.12
  66.8 0.7 pad_maximum_fusion.own
  67.5 0.0 copy-start
  67.5 0.0 collective-permute-done.14.refs_5_
  67.5 0.0 collective-permute-done.13.refs_4_
  67.5 3.5 %collective-permute-start.15 = (f32[3,2,24,128]{3,2,1,0:T(8,128)S(1)}, f32[3,2,24,128]{3,2,1,0:T(8,128)S(1)}, u32[]{:S(2)}, u32[]{:S(2)}) collective-permute-start(f32[3,2,24,128]{3,2,1,0:T(8,128)S(1)} %pad_maximum_fusion.own), channel_id=1, source_target_pairs={{1,0},{3,2},{5,4},{7,6},{9,8},{11,10},{13,12},{15,14},{17,16},{19,... | collective-permute-start | bytes 221192 | tf_op jit(solution)/shard_map/ppermute | solution.py:649
  71.0 21.7 %steps_lower.1 = f32[3,640,128]{2,1,0:T(8,128)} custom-call(f32[5]{0:T(128)} %decay.3, f32[5]{0:T(128)} %gain.3, f32[64,8,128]{2,1,0:T(8,128)} %copy-done.5, f32[61,8,128]{2,1,0:T(8,128)} %copy-done.6, f32[8,88,128]{2,1,0:T(8,128)} %get-tuple-element.36.strips, f32[56,8,128]{2,1,0:T(8,128)} %collective-permute-done.4.edge, ...), custom_call_target="tpu_custom_call", output_to_operand_aliasing={{}: (12, {})} | custom-call | flops 99999997952 | bytes 300000000 | tf_op jit(solution)/shard_map/steps_lower/pallas_call | solution.py:533
  92.7 0.0 copy-done
  92.7 0.0 collective-permute-done.15.received
  92.7 0.0 copy-start.2
  92.8 0.6 copy-done.2
  93.4 2.5 %image.1 = f32[4,128]{1,0:T(4,128)} custom-call(f32[48,240]{1,0:T(8,128)} %copy.13.weights, f32[3,2,24,128]{3,2,1,0:T(8,128)} %copy-done, f32[3,2,24,128]{3,2,1,0:T(8,128)} %copy-done.2), custom_call_target="tpu_custom_call" | custom-call | tf_op jit(solution)/shard_map/image/pallas_call | solution.py:607
  (2 shorter events, 0.1 us)
Async XLA Ops:
  4.3 12.2 %collective-permute-start.2 = (f32[8,8,128]{2,1,0:T(8,128)}, f32[8,8,128]{2,1,0:T(8,128)S(1)}, u32[]{:S(2)}, u32[]{:S(2)}) collective-permute-start(f32[8,8,128]{2,1,0:T(8,128)} %get-tuple-element.28), channel_id=1, source_target_pairs={{0,3},{1,2},{2,5},{3,4},{4,7},{5,6},{6,1},{7,0},{8,11},{9,10},{10,... | collective-permute-start | bytes 98312 | tf_op jit(solution)/shard_map/ppermute | solution.py:37
  5.9 10.6 %collective-permute-start.3 = (f32[8,8,128]{2,1,0:T(8,128)}, f32[8,8,128]{2,1,0:T(8,128)S(1)}, u32[]{:S(2)}, u32[]{:S(2)}) collective-permute-start(f32[8,8,128]{2,1,0:T(8,128)} %get-tuple-element.28), channel_id=1, source_target_pairs={{0,7},{1,6},{2,1},{3,0},{4,3},{5,2},{6,5},{7,4},{8,15},{9,14},{10,... | collective-permute-start | bytes 98312 | tf_op jit(solution)/shard_map/ppermute | solution.py:37
  8.5 14.0 %collective-permute-start = (f32[8,80,128]{2,1,0:T(8,128)}, f32[8,80,128]{2,1,0:T(8,128)}, u32[]{:S(2)}, u32[]{:S(2)}) collective-permute-start(f32[8,80,128]{2,1,0:T(8,128)} %get-tuple-element.25), channel_id=1, source_target_pairs={{0,2},{2,4},{4,6},{6,0},{1,3},{3,5},{5,7},{7,1},{8,10},{10,12},{12... | collective-permute-start | bytes 983048 | tf_op jit(solution)/shard_map/ppermute | solution.py:29
  8.8 13.7 %collective-permute-start.1 = (f32[8,80,128]{2,1,0:T(8,128)}, f32[8,80,128]{2,1,0:T(8,128)}, u32[]{:S(2)}, u32[]{:S(2)}) collective-permute-start(f32[8,80,128]{2,1,0:T(8,128)} %get-tuple-element.25), channel_id=1, source_target_pairs={{0,6},{2,0},{4,2},{6,4},{1,7},{3,1},{5,3},{7,5},{8,14},{10,8},{12,... | collective-permute-start | bytes 983048 | tf_op jit(solution)/shard_map/ppermute | solution.py:29
  11.7 10.8 %collective-permute-start.4 = (f32[56,8,128]{2,1,0:T(8,128)}, f32[56,8,128]{2,1,0:T(8,128)}, u32[]{:S(2)}, u32[]{:S(2)}) collective-permute-start(f32[56,8,128]{2,1,0:T(8,128)} %get-tuple-element.31), channel_id=1, source_target_pairs={{0,1},{1,0},{2,3},{3,2},{4,5},{5,4},{6,7},{7,6},{8,9},{9,8},{10,11... | collective-permute-start | bytes 688136 | tf_op jit(solution)/shard_map/ppermute | solution.py:29
  16.5 6.0 %copy-start.7 = (f32[8,8,128]{2,1,0:T(8,128)}, f32[8,8,128]{2,1,0:T(8,128)S(1)}, u32[]{:S(2)}) copy-start(f32[8,8,128]{2,1,0:T(8,128)S(1)} %collective-permute-done.2.edge_low) | copy-start | bytes 98308
  16.5 0.6 copy-start.8
  17.1 22.0 %collective-permute-start.7 = (f32[40,24,128]{2,1,0:T(8,128)}, f32[40,24,128]{2,1,0:T(8,128)S(1)}, u32[]{:S(2)}, u32[]{:S(2)}) collective-permute-start(f32[40,24,128]{2,1,0:T(8,128)} %get-tuple-element.38), channel_id=1, source_target_pairs={{0,8},{8,16},{16,24},{24,32},{32,40},{40,48},{48,56},{56,64},{64,7... | collective-permute-start | bytes 1474568 | tf_op jit(solution)/shard_map/ppermute | solution.py:29
  17.1 16.6 %collective-permute-start.8 = (f32[37,24,128]{2,1,0:T(8,128)}, f32[37,24,128]{2,1,0:T(8,128)S(1)}, u32[]{:S(2)}, u32[]{:S(2)}) collective-permute-start(f32[37,24,128]{2,1,0:T(8,128)} %get-tuple-element.39), channel_id=1, source_target_pairs={{0,120},{8,0},{16,8},{24,16},{32,24},{40,32},{48,40},{56,48},{64,5... | collective-permute-start | bytes 1363976 | tf_op jit(solution)/shard_map/ppermute | solution.py:29
  25.4 13.7 %collective-permute-start.5 = (f32[64,8,128]{2,1,0:T(8,128)}, f32[64,8,128]{2,1,0:T(8,128)S(1)}, u32[]{:S(2)}, u32[]{:S(2)}) collective-permute-start(f32[64,8,128]{2,1,0:T(8,128)} %get-tuple-element.34), channel_id=1, source_target_pairs={{0,8},{8,16},{16,24},{24,32},{32,40},{40,48},{48,56},{56,64},{64,7... | collective-permute-start | bytes 786440 | tf_op jit(solution)/shard_map/ppermute | solution.py:29
  25.5 13.6 %collective-permute-start.6 = (f32[61,8,128]{2,1,0:T(8,128)}, f32[61,8,128]{2,1,0:T(8,128)S(1)}, u32[]{:S(2)}, u32[]{:S(2)}) collective-permute-start(f32[61,8,128]{2,1,0:T(8,128)} %get-tuple-element.35), channel_id=1, source_target_pairs={{0,120},{8,0},{16,8},{24,16},{32,24},{40,32},{48,40},{56,48},{64,5... | collective-permute-start | bytes 749576 | tf_op jit(solution)/shard_map/ppermute | solution.py:29
  30.9 36.6 %collective-permute-start.13 = (f32[46,56,128]{2,1,0:T(8,128)}, f32[46,56,128]{2,1,0:T(8,128)}, u32[]{:S(2)}, u32[]{:S(2)}) collective-permute-start(f32[46,56,128]{2,1,0:T(8,128)} %get-tuple-element.42), channel_id=1, source_target_pairs={{0,8},{8,16},{16,24},{24,32},{32,40},{40,48},{48,56},{56,64},{64,7... | collective-permute-start | bytes 3956744 | tf_op jit(solution)/shard_map/ppermute | solution.py:29
  33.7 5.5 %copy-start.4 = (f32[37,24,128]{2,1,0:T(8,128)}, f32[37,24,128]{2,1,0:T(8,128)S(1)}, u32[]{:S(2)}) copy-start(f32[37,24,128]{2,1,0:T(8,128)S(1)} %collective-permute-done.8.refs_2_) | copy-start | bytes 1363972
  33.7 33.8 %collective-permute-start.14 = (f32[43,56,128]{2,1,0:T(8,128)}, f32[43,56,128]{2,1,0:T(8,128)}, u32[]{:S(2)}, u32[]{:S(2)}) collective-permute-start(f32[43,56,128]{2,1,0:T(8,128)} %get-tuple-element.43), channel_id=1, source_target_pairs={{0,120},{8,0},{16,8},{24,16},{32,24},{40,32},{48,40},{56,48},{64,5... | collective-permute-start | bytes 3698696 | tf_op jit(solution)/shard_map/ppermute | solution.py:29
  39.1 1.0 %copy-start.3 = (f32[40,24,128]{2,1,0:T(8,128)}, f32[40,24,128]{2,1,0:T(8,128)S(1)}, u32[]{:S(2)}) copy-start(f32[40,24,128]{2,1,0:T(8,128)S(1)} %collective-permute-done.7.refs_1_) | copy-start | bytes 1474564
  39.1 0.8 copy-start.6
  39.1 0.8 copy-start.5
  40.1 23.7 %copy-start.1 = (f32[2,24,15,15]{1,0,3,2:T(2,128)S(1)}, f32[2,24,15,15]{1,0,3,2:T(2,128)}, u32[]{:S(2)}) copy-start(f32[2,24,15,15]{1,0,3,2:T(2,128)} %param.11) | copy-start | bytes 129604
  52.6 5.1 %collective-permute-start.9 = (f32[2,8,128]{2,1,0:T(8,128)}, f32[2,8,128]{2,1,0:T(8,128)S(1)}, u32[]{:S(2)}, u32[]{:S(2)}) collective-permute-start(f32[2,8,128]{2,1,0:T(8,128)} %get-tuple-element.41), channel_id=1, source_target_pairs={{0,2},{2,4},{4,6},{6,0},{1,3},{3,5},{5,7},{7,1},{8,10},{10,12},{12... | collective-permute-start | bytes 24584 | tf_op jit(solution)/shard_map/ppermute | solution.py:29
  52.7 5.1 %collective-permute-start.10 = (f32[2,8,128]{2,1,0:T(8,128)}, f32[2,8,128]{2,1,0:T(8,128)S(1)}, u32[]{:S(2)}, u32[]{:S(2)}) collective-permute-start(f32[2,8,128]{2,1,0:T(8,128)} %get-tuple-element.41), channel_id=1, source_target_pairs={{0,6},{2,0},{4,2},{6,4},{1,7},{3,1},{5,3},{7,5},{8,14},{10,8},{12,... | collective-permute-start | bytes 24584 | tf_op jit(solution)/shard_map/ppermute | solution.py:29
  58.5 8.3 %collective-permute-start.11 = (f32[3,2,8,128]{3,2,1,0:T(8,128)S(1)}, f32[3,2,8,128]{3,2,1,0:T(8,128)S(1)}, u32[]{:S(2)}, u32[]{:S(2)}) collective-permute-start(f32[3,2,8,128]{3,2,1,0:T(8,128)S(1)} %pad_maximum_fusion.1), channel_id=1, source_target_pairs={{0,8},{8,16},{16,24},{24,32},{32,40},{40,48},{48,56},{56,64},{64,7... | collective-permute-start | bytes 73736 | tf_op jit(solution)/shard_map/ppermute | solution.py:29
  58.5 8.3 %collective-permute-start.12 = (f32[3,2,8,128]{3,2,1,0:T(8,128)S(1)}, f32[3,2,8,128]{3,2,1,0:T(8,128)S(1)}, u32[]{:S(2)}, u32[]{:S(2)}) collective-permute-start(f32[3,2,8,128]{3,2,1,0:T(8,128)S(1)} %pad_maximum_fusion.1), channel_id=1, source_target_pairs={{0,120},{8,0},{16,8},{24,16},{32,24},{40,32},{48,40},{56,48},{64,5... | collective-permute-start | bytes 73736 | tf_op jit(solution)/shard_map/ppermute | solution.py:29
  67.5 25.2 %copy-start = (f32[3,2,24,128]{3,2,1,0:T(8,128)}, f32[3,2,24,128]{3,2,1,0:T(8,128)S(1)}, u32[]{:S(2)}) copy-start(f32[3,2,24,128]{3,2,1,0:T(8,128)S(1)} %pad_maximum_fusion.own) | copy-start | bytes 221188
  67.5 25.2 %collective-permute-start.15 = (f32[3,2,24,128]{3,2,1,0:T(8,128)S(1)}, f32[3,2,24,128]{3,2,1,0:T(8,128)S(1)}, u32[]{:S(2)}, u32[]{:S(2)}) collective-permute-start(f32[3,2,24,128]{3,2,1,0:T(8,128)S(1)} %pad_maximum_fusion.own), channel_id=1, source_target_pairs={{1,0},{3,2},{5,4},{7,6},{9,8},{11,10},{13,12},{15,14},{17,16},{19,... | collective-permute-start | bytes 221192 | tf_op jit(solution)/shard_map/ppermute | solution.py:649
  92.7 0.6 copy-start.2

commit v9 on v7

--- a/solution.py
+++ b/solution.py
@@ -15,7 +15,7 @@
 ROWS = 8 + 2 * W
 BASE = 4
 HELD = BASE + ROWS + 2
-CUT = 6
+CUT = 7
 HIGH = 11 - CUT
 LAG = 4
 VMEM = 63 * 1024 * 1024
@@ -608,8 +608,8 @@
     from_low, from_high = around(strips, "gy", 1), around(strips, "gy", -1)
     edge_low, edge_high = beyond(edge_strips, 1), beyond(edge_strips, -1)
     own_u, up_u, down_u = pack(CUT, 10, el, mg, mat)
-    up_u, down_u, edge, edge_low, edge_high = lax.optimization_barrier(
-        (up_u, down_u, edge, edge_low, edge_high)
+    up_u, down_u, edge_low, edge_high = lax.optimization_barrier(
+        (up_u, down_u, edge_low, edge_high)
     )
     low_u, high_u = around(up_u, "gx", 1), around(down_u, "gx", -1)
     strips, up_c, down_c = corners(from_low, from_high, edge_low, edge_high, edge)
@@ -617,7 +617,6 @@
     own_l, up_l, down_l = pack(0, CUT, el, mg, mat, strips)
     low_l, high_l = around(up_l, "gx", 1), around(down_l, "gx", -1)
 
-    low_u, high_u, weights = lax.optimization_barrier((low_u, high_u, weights))
     sides = [low_c, high_c, strips, edge]
     field, plane = run_steps(True, decay, gain, sides, [own_u, low_u, high_u])
     top = jnp.stack([plane, around(plane, "gy", 1), around(plane, "gy", -1)])

time: 107 us -> 97.7 us (0.913)
  waiting for transfers between devices: 19.6 us -> 5.73 us
  starting transfers between devices: 29.7 us -> 36.2 us
  Pallas kernels: 52.7 us -> 50.1 us
    ppermute x13, waiting for transfers between devices: 19.5 us -> 5.73 us  [around(): lax.ppermute(value, axis, [(i, (i + steps) % count) for i in range(count)])]
    ppermute x13, starting transfers between devices: 23.9 us -> 28.5 us  [around(): lax.ppermute(value, axis, [(i, (i + steps) % count) for i in range(count)])]
    pallas_call x2, Pallas kernels: 36.9 us -> 34.2 us  [run_steps(): pl.pallas_call(functools.partial(steps_kernel, upper), out_shape=out_shap...]
    ppermute x2, starting transfers between devices: 3.06 us -> 4.2 us  [beyond(): return lax.ppermute(value, ('gy', 'gz'), pairs)]
  transfers between devices with their start and end apart: 16 -> 16, of which waited for: 7 -> 2; matrix products, arithmetic and copies ran while one was open for 2% -> 2% of each run, Pallas kernels for 44% -> 45%
where the time goes in v9:
time: 97.7 us; the launch traced here: 97.2 us
  Pallas kernels  50.1 us (51%)
  starting transfers between devices  36.2 us (37%)
  waiting for transfers between devices  5.73 us (6%)
  local copies, waits for them, and re-layouts  2.91 us (3%)
  other arithmetic  1.4 us (1%)
    pallas_call x2, Pallas kernels, run_steps(): pl.pallas_call(functools.partial(steps_kernel, upper), out_shape=out_shap...  34.2 us
    ppermute x13, starting transfers between devices, around(): lax.ppermute(value, axis, [(i, (i + steps) % count) for i in range(count)])  28.5 us
    pallas_call x2, Pallas kernels, pack(): pl.pallas_call(functools.partial(pack_kernel, first, last), out_shape=[ja...  7.68 us
    ppermute x13, waiting for transfers between devices, around(): lax.ppermute(value, axis, [(i, (i + steps) % count) for i in range(count)])  5.73 us
    ppermute x2, starting transfers between devices, beyond(): return lax.ppermute(value, ('gy', 'gz'), pairs)  4.2 us
    pallas_call x1, Pallas kernels, own_strips(): pl.pallas_call(strip_kernel, out_shape=[jax.ShapeDtypeStruct((8, 80, 128)...  3.6 us
    ppermute x1, starting transfers between devices, on_device(): received = lax.ppermute(top, 'gz', [(1, 0)])  3.48 us
    pallas_call x1, Pallas kernels, image_of(): pl.pallas_call(image_kernel, out_shape=jax.ShapeDtypeStruct((4, 128), jnp...  2.52 us
  transfers between devices with their start and end apart: 16, of which 2 were waited for; matrix products, arithmetic and copies ran while one was open for 2% of the time, Pallas kernels for 45%

profile of v9, /device:TPU:2, one launch (start us, length us, event | category | flops | bytes accessed | tf_op | source)
XLA Modules:
  0.0 97.2 jit_solution(13410931323208246484)
XLA Ops:
  0.6 3.6 %own_strips.1 = (f32[8,80,128]{2,1,0:T(8,128)}, f32[56,8,128]{2,1,0:T(8,128)}, f32[8,8,128]{2,1,0:T(8,128)}) custom-call(f32[3,640,128]{2,1,0:T(8,128)} %bitcast.19, f32[3,640,128]{2,1,0:T(8,128)} %bitcast.22, s32[640,128]{1,0:T(8,128)} %bitcast.25), custom_call_target="tpu_custom_call" | custom-call | flops 3000000000 | bytes 9000000 | tf_op jit(solution)/shard_map/own_strips/pallas_call | solution.py:106
  4.2 1.6 %collective-permute-start.2 = (f32[8,8,128]{2,1,0:T(8,128)}, f32[8,8,128]{2,1,0:T(8,128)S(1)}, u32[]{:S(2)}, u32[]{:S(2)}) collective-permute-start(f32[8,8,128]{2,1,0:T(8,128)} %get-tuple-element.26), channel_id=1, source_target_pairs={{0,3},{1,2},{2,5},{3,4},{4,7},{5,6},{6,1},{7,0},{8,11},{9,10},{10,... | collective-permute-start | bytes 98312 | tf_op jit(solution)/shard_map/ppermute | solution.py:37
  5.8 2.6 %collective-permute-start.3 = (f32[8,8,128]{2,1,0:T(8,128)}, f32[8,8,128]{2,1,0:T(8,128)S(1)}, u32[]{:S(2)}, u32[]{:S(2)}) collective-permute-start(f32[8,8,128]{2,1,0:T(8,128)} %get-tuple-element.26), channel_id=1, source_target_pairs={{0,7},{1,6},{2,1},{3,0},{4,3},{5,2},{6,5},{7,4},{8,15},{9,14},{10,... | collective-permute-start | bytes 98312 | tf_op jit(solution)/shard_map/ppermute | solution.py:37
  8.4 0.4 collective-permute-start
  8.8 2.9 %collective-permute-start.1 = (f32[8,80,128]{2,1,0:T(8,128)}, f32[8,80,128]{2,1,0:T(8,128)}, u32[]{:S(2)}, u32[]{:S(2)}) collective-permute-start(f32[8,80,128]{2,1,0:T(8,128)} %get-tuple-element.23), channel_id=1, source_target_pairs={{0,6},{2,0},{4,2},{6,4},{1,7},{3,1},{5,3},{7,5},{8,14},{10,8},{12,... | collective-permute-start | bytes 983048 | tf_op jit(solution)/shard_map/ppermute | solution.py:29
  11.7 0.5 collective-permute-start.4
  12.1 2.6 %pack_upper.1 = (f32[56,24,128]{2,1,0:T(8,128)}, f32[40,24,128]{2,1,0:T(8,128)}, f32[37,24,128]{2,1,0:T(8,128)}) custom-call(f32[3,640,128]{2,1,0:T(8,128)} %bitcast.20, f32[3,640,128]{2,1,0:T(8,128)} %bitcast.23, s32[640,128]{1,0:T(8,128)} %bitcast.26), custom_call_target="tpu_custom_call" | custom-call | flops 20000000000 | bytes 60000000 | tf_op jit(solution)/shard_map/pack_upper/pallas_call | solution.py:167
  14.7 0.0 collective-permute-done.2.edge_low
  14.7 0.0 copy-start.5
  14.8 0.0 collective-permute-done.3.edge_high
  14.8 0.0 copy-start.6
  14.8 0.6 copy-done.6
  15.4 0.0 collective-permute-start.7
  15.4 5.4 %collective-permute-start.8 = (f32[37,24,128]{2,1,0:T(8,128)}, f32[37,24,128]{2,1,0:T(8,128)S(1)}, u32[]{:S(2)}, u32[]{:S(2)}) collective-permute-start(f32[37,24,128]{2,1,0:T(8,128)} %get-tuple-element.35), channel_id=1, source_target_pairs={{0,120},{8,0},{16,8},{24,16},{32,24},{40,32},{48,40},{56,48},{64,5... | collective-permute-start | bytes 1363976 | tf_op jit(solution)/shard_map/ppermute | solution.py:29
  20.7 0.0 collective-permute-done.4.edge
  20.7 0.0 collective-permute-done.from_low
  20.7 0.0 collective-permute-done.1.from_high
  20.7 0.0 copy-done.5
  20.8 2.1 %corners.1 = (f32[8,88,128]{2,1,0:T(8,128)}, f32[64,8,128]{2,1,0:T(8,128)}, f32[61,8,128]{2,1,0:T(8,128)}) custom-call(f32[8,80,128]{2,1,0:T(8,128)} %collective-permute-done.from_low, f32[8,80,128]{2,1,0:T(8,128)} %collective-permute-done.1.from_high, f32[8,8,128]{2,1,0:T(8,128)} %copy-done.5, f32[8,8,128]{2,1,0:T(8,128)} %copy-done.6, ...), custom_call_target="tpu_custom_call" | custom-call | flops 1000000000 | bytes 3000000 | tf_op jit(solution)/shard_map/corners/pallas_call | solution.py:205
  22.9 0.0 collective-permute-start.5
  22.9 5.4 %collective-permute-start.6 = (f32[61,8,128]{2,1,0:T(8,128)}, f32[61,8,128]{2,1,0:T(8,128)}, u32[]{:S(2)}, u32[]{:S(2)}) collective-permute-start(f32[61,8,128]{2,1,0:T(8,128)} %get-tuple-element.31), channel_id=1, source_target_pairs={{0,120},{8,0},{16,8},{24,16},{32,24},{40,32},{48,40},{56,48},{64,5... | collective-permute-start | bytes 749576 | tf_op jit(solution)/shard_map/ppermute | solution.py:29
  28.2 5.1 %pack_lower.1 = (f32[56,56,128]{2,1,0:T(8,128)}, f32[46,56,128]{2,1,0:T(8,128)}, f32[43,56,128]{2,1,0:T(8,128)}) custom-call(f32[3,640,128]{2,1,0:T(8,128)} %bitcast.21, f32[3,640,128]{2,1,0:T(8,128)} %bitcast.24, s32[640,128]{1,0:T(8,128)} %bitcast.27, f32[8,88,128]{2,1,0:T(8,128)} %get-tuple-element.32.refs_0_.strips), custom_call_target="tpu_custom_call" | custom-call | flops 3000000000 | bytes 9000000 | tf_op jit(solution)/shard_map/pack_lower/pallas_call | solution.py:167
  33.3 0.1 collective-permute-start.13
  33.4 0.0 collective-permute-done.8.refs_2_
  33.4 0.0 copy-start.4
  33.4 5.3 %collective-permute-start.14 = (f32[43,56,128]{2,1,0:T(8,128)}, f32[43,56,128]{2,1,0:T(8,128)}, u32[]{:S(2)}, u32[]{:S(2)}) collective-permute-start(f32[43,56,128]{2,1,0:T(8,128)} %get-tuple-element.39), channel_id=1, source_target_pairs={{0,120},{8,0},{16,8},{24,16},{32,24},{40,32},{48,40},{56,48},{64,5... | collective-permute-start | bytes 3698696 | tf_op jit(solution)/shard_map/ppermute | solution.py:29
  38.8 0.0 collective-permute-done.7.refs_1_
  38.8 0.0 copy-start.3
  38.8 0.0 collective-permute-done.6.high_c
  38.8 0.0 collective-permute-done.5.low_c
  38.8 0.0 copy-done.4
  38.8 0.8 copy-done.3
  39.6 0.0 copy-start.1
  39.6 12.5 %steps_upper.1 = (f32[3,640,128]{2,1,0:T(8,128)}, f32[2,8,128]{2,1,0:T(8,128)}) custom-call(f32[5]{0:T(128)} %decay.3, f32[5]{0:T(128)} %gain.3, f32[64,8,128]{2,1,0:T(8,128)} %collective-permute-done.5.low_c, f32[61,8,128]{2,1,0:T(8,128)} %collective-permute-done.6.high_c, f32[8,88,128]{2,1,0:T(8,128)} %get-tuple-element.32.refs_0_.strips, ...), custom_call_target="tpu_custom_call" | custom-call | flops 99999997952 | bytes 300000000 | tf_op jit(solution)/shard_map/steps_upper/pallas_call | solution.py:510
  52.1 0.1 collective-permute-start.9
  52.1 3.2 %collective-permute-start.10 = (f32[2,8,128]{2,1,0:T(8,128)}, f32[2,8,128]{2,1,0:T(8,128)S(1)}, u32[]{:S(2)}, u32[]{:S(2)}) collective-permute-start(f32[2,8,128]{2,1,0:T(8,128)} %get-tuple-element.37), channel_id=1, source_target_pairs={{0,6},{2,0},{4,2},{6,4},{1,7},{3,1},{5,3},{7,5},{8,14},{10,8},{12,... | collective-permute-start | bytes 24584 | tf_op jit(solution)/shard_map/ppermute | solution.py:29
  55.4 1.8 %collective-permute-done.9 = f32[2,8,128]{2,1,0:T(8,128)S(1)} collective-permute-done((f32[2,8,128]{2,1,0:T(8,128)}, f32[2,8,128]{2,1,0:T(8,128)S(1)}, u32[]{:S(2)}, u32[]{:S(2)}) %collective-permute-start.9) | collective-permute-done | bytes 8224 | tf_op jit(solution)/shard_map/ppermute | solution.py:29
  57.2 0.0 collective-permute-done.10
  57.2 0.7 pad_maximum_fusion.1
  57.9 0.0 collective-permute-start.11
  57.9 5.4 %collective-permute-start.12 = (f32[3,2,8,128]{3,2,1,0:T(8,128)S(1)}, f32[3,2,8,128]{3,2,1,0:T(8,128)S(1)}, u32[]{:S(2)}, u32[]{:S(2)}) collective-permute-start(f32[3,2,8,128]{3,2,1,0:T(8,128)S(1)} %pad_maximum_fusion.1), channel_id=1, source_target_pairs={{0,120},{8,0},{16,8},{24,16},{32,24},{40,32},{48,40},{56,48},{64,5... | collective-permute-start | bytes 73736 | tf_op jit(solution)/shard_map/ppermute | solution.py:29
  63.3 0.0 copy-done.1
  63.3 0.2 reshape.26
  63.5 0.7 copy.11.weights
  64.2 3.9 %collective-permute-done.11 = f32[3,2,8,128]{3,2,1,0:T(8,128)S(1)} collective-permute-done((f32[3,2,8,128]{3,2,1,0:T(8,128)S(1)}, f32[3,2,8,128]{3,2,1,0:T(8,128)S(1)}, u32[]{:S(2)}, u32[]{:S(2)}) %collective-permute-start.11) | collective-permute-done | bytes 24608 | tf_op jit(solution)/shard_map/ppermute | solution.py:29
  68.1 0.0 collective-permute-done.12
  68.1 0.7 pad_maximum_fusion.own
  68.8 0.0 copy-start
  68.8 0.0 collective-permute-done.14.refs_5_
  68.8 0.0 collective-permute-done.13.refs_4_
  68.8 3.5 %collective-permute-start.15 = (f32[3,2,24,128]{3,2,1,0:T(8,128)S(1)}, f32[3,2,24,128]{3,2,1,0:T(8,128)S(1)}, u32[]{:S(2)}, u32[]{:S(2)}) collective-permute-start(f32[3,2,24,128]{3,2,1,0:T(8,128)S(1)} %pad_maximum_fusion.own), channel_id=1, source_target_pairs={{1,0},{3,2},{5,4},{7,6},{9,8},{11,10},{13,12},{15,14},{17,16},{19,... | collective-permute-start | bytes 221192 | tf_op jit(solution)/shard_map/ppermute | solution.py:625
  72.3 21.7 %steps_lower.1 = f32[3,640,128]{2,1,0:T(8,128)} custom-call(f32[5]{0:T(128)} %decay.3, f32[5]{0:T(128)} %gain.3, f32[64,8,128]{2,1,0:T(8,128)} %collective-permute-done.5.low_c, f32[61,8,128]{2,1,0:T(8,128)} %collective-permute-done.6.high_c, f32[8,88,128]{2,1,0:T(8,128)} %get-tuple-element.32.refs_0_.strips, ...), custom_call_target="tpu_custom_call", output_to_operand_aliasing={{}: (12, {})} | custom-call | flops 99999997952 | bytes 300000000 | tf_op jit(solution)/shard_map/steps_lower/pallas_call | solution.py:510
  94.0 0.0 copy-done
  94.0 0.0 collective-permute-done.15.received
  94.0 0.0 copy-start.2
  94.1 0.6 copy-done.2
  94.7 2.5 %image.1 = f32[4,128]{1,0:T(4,128)} custom-call(f32[48,240]{1,0:T(8,128)} %copy.11.weights, f32[3,2,24,128]{3,2,1,0:T(8,128)} %copy-done, f32[3,2,24,128]{3,2,1,0:T(8,128)} %copy-done.2), custom_call_target="tpu_custom_call" | custom-call | tf_op jit(solution)/shard_map/image/pallas_call | solution.py:584
  (2 shorter events, 0.1 us)
Async XLA Ops:
  4.2 10.5 %collective-permute-start.2 = (f32[8,8,128]{2,1,0:T(8,128)}, f32[8,8,128]{2,1,0:T(8,128)S(1)}, u32[]{:S(2)}, u32[]{:S(2)}) collective-permute-start(f32[8,8,128]{2,1,0:T(8,128)} %get-tuple-element.26), channel_id=1, source_target_pairs={{0,3},{1,2},{2,5},{3,4},{4,7},{5,6},{6,1},{7,0},{8,11},{9,10},{10,... | collective-permute-start | bytes 98312 | tf_op jit(solution)/shard_map/ppermute | solution.py:37
  5.8 8.9 %collective-permute-start.3 = (f32[8,8,128]{2,1,0:T(8,128)}, f32[8,8,128]{2,1,0:T(8,128)S(1)}, u32[]{:S(2)}, u32[]{:S(2)}) collective-permute-start(f32[8,8,128]{2,1,0:T(8,128)} %get-tuple-element.26), channel_id=1, source_target_pairs={{0,7},{1,6},{2,1},{3,0},{4,3},{5,2},{6,5},{7,4},{8,15},{9,14},{10,... | collective-permute-start | bytes 98312 | tf_op jit(solution)/shard_map/ppermute | solution.py:37
  8.4 12.3 %collective-permute-start = (f32[8,80,128]{2,1,0:T(8,128)}, f32[8,80,128]{2,1,0:T(8,128)}, u32[]{:S(2)}, u32[]{:S(2)}) collective-permute-start(f32[8,80,128]{2,1,0:T(8,128)} %get-tuple-element.23), channel_id=1, source_target_pairs={{0,2},{2,4},{4,6},{6,0},{1,3},{3,5},{5,7},{7,1},{8,10},{10,12},{12... | collective-permute-start | bytes 983048 | tf_op jit(solution)/shard_map/ppermute | solution.py:29
  8.8 11.9 %collective-permute-start.1 = (f32[8,80,128]{2,1,0:T(8,128)}, f32[8,80,128]{2,1,0:T(8,128)}, u32[]{:S(2)}, u32[]{:S(2)}) collective-permute-start(f32[8,80,128]{2,1,0:T(8,128)} %get-tuple-element.23), channel_id=1, source_target_pairs={{0,6},{2,0},{4,2},{6,4},{1,7},{3,1},{5,3},{7,5},{8,14},{10,8},{12,... | collective-permute-start | bytes 983048 | tf_op jit(solution)/shard_map/ppermute | solution.py:29
  11.7 9.1 %collective-permute-start.4 = (f32[56,8,128]{2,1,0:T(8,128)}, f32[56,8,128]{2,1,0:T(8,128)}, u32[]{:S(2)}, u32[]{:S(2)}) collective-permute-start(f32[56,8,128]{2,1,0:T(8,128)} %get-tuple-element.29), channel_id=1, source_target_pairs={{0,1},{1,0},{2,3},{3,2},{4,5},{5,4},{6,7},{7,6},{8,9},{9,8},{10,11... | collective-permute-start | bytes 688136 | tf_op jit(solution)/shard_map/ppermute | solution.py:29
  14.7 6.0 %copy-start.5 = (f32[8,8,128]{2,1,0:T(8,128)}, f32[8,8,128]{2,1,0:T(8,128)S(1)}, u32[]{:S(2)}) copy-start(f32[8,8,128]{2,1,0:T(8,128)S(1)} %collective-permute-done.2.edge_low) | copy-start | bytes 98308
  14.8 0.6 copy-start.6
  15.4 23.4 %collective-permute-start.7 = (f32[40,24,128]{2,1,0:T(8,128)}, f32[40,24,128]{2,1,0:T(8,128)S(1)}, u32[]{:S(2)}, u32[]{:S(2)}) collective-permute-start(f32[40,24,128]{2,1,0:T(8,128)} %get-tuple-element.34), channel_id=1, source_target_pairs={{0,8},{8,16},{16,24},{24,32},{32,40},{40,48},{48,56},{56,64},{64,7... | collective-permute-start | bytes 1474568 | tf_op jit(solution)/shard_map/ppermute | solution.py:29
  15.4 18.0 %collective-permute-start.8 = (f32[37,24,128]{2,1,0:T(8,128)}, f32[37,24,128]{2,1,0:T(8,128)S(1)}, u32[]{:S(2)}, u32[]{:S(2)}) collective-permute-start(f32[37,24,128]{2,1,0:T(8,128)} %get-tuple-element.35), channel_id=1, source_target_pairs={{0,120},{8,0},{16,8},{24,16},{32,24},{40,32},{48,40},{56,48},{64,5... | collective-permute-start | bytes 1363976 | tf_op jit(solution)/shard_map/ppermute | solution.py:29
  22.9 15.9 %collective-permute-start.5 = (f32[64,8,128]{2,1,0:T(8,128)}, f32[64,8,128]{2,1,0:T(8,128)}, u32[]{:S(2)}, u32[]{:S(2)}) collective-permute-start(f32[64,8,128]{2,1,0:T(8,128)} %get-tuple-element.30), channel_id=1, source_target_pairs={{0,8},{8,16},{16,24},{24,32},{32,40},{40,48},{48,56},{56,64},{64,7... | collective-permute-start | bytes 786440 | tf_op jit(solution)/shard_map/ppermute | solution.py:29
  22.9 15.9 %collective-permute-start.6 = (f32[61,8,128]{2,1,0:T(8,128)}, f32[61,8,128]{2,1,0:T(8,128)}, u32[]{:S(2)}, u32[]{:S(2)}) collective-permute-start(f32[61,8,128]{2,1,0:T(8,128)} %get-tuple-element.31), channel_id=1, source_target_pairs={{0,120},{8,0},{16,8},{24,16},{32,24},{40,32},{48,40},{56,48},{64,5... | collective-permute-start | bytes 749576 | tf_op jit(solution)/shard_map/ppermute | solution.py:29
  33.3 35.5 %collective-permute-start.13 = (f32[46,56,128]{2,1,0:T(8,128)}, f32[46,56,128]{2,1,0:T(8,128)}, u32[]{:S(2)}, u32[]{:S(2)}) collective-permute-start(f32[46,56,128]{2,1,0:T(8,128)} %get-tuple-element.38), channel_id=1, source_target_pairs={{0,8},{8,16},{16,24},{24,32},{32,40},{40,48},{48,56},{56,64},{64,7... | collective-permute-start | bytes 3956744 | tf_op jit(solution)/shard_map/ppermute | solution.py:29
  33.4 5.4 %copy-start.4 = (f32[37,24,128]{2,1,0:T(8,128)}, f32[37,24,128]{2,1,0:T(8,128)S(1)}, u32[]{:S(2)}) copy-start(f32[37,24,128]{2,1,0:T(8,128)S(1)} %collective-permute-done.8.refs_2_) | copy-start | bytes 1363972
  33.4 35.4 %collective-permute-start.14 = (f32[43,56,128]{2,1,0:T(8,128)}, f32[43,56,128]{2,1,0:T(8,128)}, u32[]{:S(2)}, u32[]{:S(2)}) collective-permute-start(f32[43,56,128]{2,1,0:T(8,128)} %get-tuple-element.39), channel_id=1, source_target_pairs={{0,120},{8,0},{16,8},{24,16},{32,24},{40,32},{48,40},{56,48},{64,5... | collective-permute-start | bytes 3698696 | tf_op jit(solution)/shard_map/ppermute | solution.py:29
  38.8 0.8 copy-start.3
  39.6 23.7 %copy-start.1 = (f32[2,24,15,15]{1,0,3,2:T(2,128)S(1)}, f32[2,24,15,15]{1,0,3,2:T(2,128)}, u32[]{:S(2)}) copy-start(f32[2,24,15,15]{1,0,3,2:T(2,128)} %param.11) | copy-start | bytes 129604
  52.1 5.1 %collective-permute-start.9 = (f32[2,8,128]{2,1,0:T(8,128)}, f32[2,8,128]{2,1,0:T(8,128)S(1)}, u32[]{:S(2)}, u32[]{:S(2)}) collective-permute-start(f32[2,8,128]{2,1,0:T(8,128)} %get-tuple-element.37), channel_id=1, source_target_pairs={{0,2},{2,4},{4,6},{6,0},{1,3},{3,5},{5,7},{7,1},{8,10},{10,12},{12... | collective-permute-start | bytes 24584 | tf_op jit(solution)/shard_map/ppermute | solution.py:29
  52.1 5.1 %collective-permute-start.10 = (f32[2,8,128]{2,1,0:T(8,128)}, f32[2,8,128]{2,1,0:T(8,128)S(1)}, u32[]{:S(2)}, u32[]{:S(2)}) collective-permute-start(f32[2,8,128]{2,1,0:T(8,128)} %get-tuple-element.37), channel_id=1, source_target_pairs={{0,6},{2,0},{4,2},{6,4},{1,7},{3,1},{5,3},{7,5},{8,14},{10,8},{12,... | collective-permute-start | bytes 24584 | tf_op jit(solution)/shard_map/ppermute | solution.py:29
  57.9 10.2 %collective-permute-start.11 = (f32[3,2,8,128]{3,2,1,0:T(8,128)S(1)}, f32[3,2,8,128]{3,2,1,0:T(8,128)S(1)}, u32[]{:S(2)}, u32[]{:S(2)}) collective-permute-start(f32[3,2,8,128]{3,2,1,0:T(8,128)S(1)} %pad_maximum_fusion.1), channel_id=1, source_target_pairs={{0,8},{8,16},{16,24},{24,32},{32,40},{40,48},{48,56},{56,64},{64,7... | collective-permute-start | bytes 73736 | tf_op jit(solution)/shard_map/ppermute | solution.py:29
  57.9 10.2 %collective-permute-start.12 = (f32[3,2,8,128]{3,2,1,0:T(8,128)S(1)}, f32[3,2,8,128]{3,2,1,0:T(8,128)S(1)}, u32[]{:S(2)}, u32[]{:S(2)}) collective-permute-start(f32[3,2,8,128]{3,2,1,0:T(8,128)S(1)} %pad_maximum_fusion.1), channel_id=1, source_target_pairs={{0,120},{8,0},{16,8},{24,16},{32,24},{40,32},{48,40},{56,48},{64,5... | collective-permute-start | bytes 73736 | tf_op jit(solution)/shard_map/ppermute | solution.py:29
  68.8 25.2 %copy-start = (f32[3,2,24,128]{3,2,1,0:T(8,128)}, f32[3,2,24,128]{3,2,1,0:T(8,128)S(1)}, u32[]{:S(2)}) copy-start(f32[3,2,24,128]{3,2,1,0:T(8,128)S(1)} %pad_maximum_fusion.own) | copy-start | bytes 221188
  68.8 25.2 %collective-permute-start.15 = (f32[3,2,24,128]{3,2,1,0:T(8,128)S(1)}, f32[3,2,24,128]{3,2,1,0:T(8,128)S(1)}, u32[]{:S(2)}, u32[]{:S(2)}) collective-permute-start(f32[3,2,24,128]{3,2,1,0:T(8,128)S(1)} %pad_maximum_fusion.own), channel_id=1, source_target_pairs={{1,0},{3,2},{5,4},{7,6},{9,8},{11,10},{13,12},{15,14},{17,16},{19,... | collective-permute-start | bytes 221192 | tf_op jit(solution)/shard_map/ppermute | solution.py:625
  94.0 0.6 copy-start.2
